TPU v7x, 128 devices: a whole 4x4x4 slice. The times are simulated.
128 devices in a mesh: dp: 4 (over x_hi, core), seq: 32 (over y, z, x_lo).
Axes of the slice: x: 4 (x_hi: 2, x_lo: 2; x = x_hi * 2 + x_lo), y: 4, z: 4, core: 2. Of those that a mesh axis runs over, the one named last changes fastest.
Arguments:
- tokens: bfloat16 [4, 32768, 1024], P('dp', 'seq'), may hold values from -16 to 16
- out_grad: bfloat16 [4, 32768, 1024], P('dp', 'seq'), may hold values from -6 to 6
- w_query: bfloat16 [1024, 1024], replicated, may hold values from -0.1875 to 0.1875
- w_key: bfloat16 [1024, 1024], replicated, may hold values from -0.1875 to 0.1875
- w_value: bfloat16 [1024, 1024], replicated, may hold values from -0.1875 to 0.1875
- w_output: bfloat16 [1024, 1024], replicated, may hold values from -0.1875 to 0.1875
- grad_accum: float32 [1024, 4096], P(('dp', 'seq')), may hold values from -4 to 4
Outputs:
- in_grad: bfloat16 [4, 32768, 1024], P('dp', 'seq')
- new_accum: float32 [1024, 4096], P(('dp', 'seq'))
All inputs are finite; a program needn't handle non-finite values.
Results may differ from a plain program's by a relative error of at most 0.015.
The roundings to bfloat16 on the way count: a program that leaves them out, or rounds other values in their place, can miss the bound.
Values may be sent and summed in bfloat16 or wider, within the bound.
No kernel may reach another device: no remote copies, remote signals or barrier semaphores. Data moves between devices by JAX's collectives and lax.ppermute only.
A program may use at most 128 MiB of HBM per device.

v0:
```python
import functools

import jax
import jax.numpy as jnp
from jax import lax
from jax.experimental import pallas as pl
from jax.experimental.pallas import tpu as pltpu
from jax.sharding import Mesh
from jax.sharding import PartitionSpec as P

HD = 128
WIN = 256
LOG2E = 1.4426950408889634
SCALE = 1.0 / HD**0.5
AXES = ("xh", "co", "y", "z", "xl")
SEQ = ("y", "z", "xl")
CHIPS = ("xh", "y", "z", "xl")
F32 = jnp.float32
BF16 = jnp.bfloat16


def dot(a, b, ca, cb):
    return lax.dot_general(a, b, (((ca,), (cb,)), ((), ())), preferred_element_type=F32)


HALF = WIN // 2
NEG = -1e30


def bf(value):
    return value.astype(BF16)


def quads(a, b, c, d):
    return jnp.concatenate([jnp.concatenate([a, b], axis=1), jnp.concatenate([c, d], axis=1)], axis=0)


def upper_triangle():
    rows = lax.broadcasted_iota(jnp.int32, (HALF, HALF), 0)
    cols = lax.broadcasted_iota(jnp.int32, (HALF, HALF), 1)
    return cols > rows


def scores_of(block, bias):
    query, grad, key_l, value_l, key_r, value_r = block
    s_l = dot(query, key_l, 1, 1)
    if bias is not None:
        s_l = s_l + bias
    return s_l, dot(query, key_r, 1, 1), dot(grad, value_l, 1, 1), dot(grad, value_r, 1, 1)


def probs_of(scores, upper):
    s_l, s_r = scores[:2]
    low = slice(0, HALF)
    high = slice(HALF, WIN)
    runs = (
        (jnp.where(upper, s_l[low, low], NEG), s_l[low, high], jnp.where(upper, NEG, s_r[low, low])),
        (jnp.where(upper, s_l[high, high], NEG), s_r[high, low], jnp.where(upper, NEG, s_r[high, high])),
    )
    probs = []
    for run in runs:
        top = jnp.max(jnp.maximum(jnp.maximum(run[0], run[1]), run[2]), axis=1, keepdims=True)
        shift = top * (SCALE * LOG2E)
        e = [jnp.exp2(part * (SCALE * LOG2E) - shift) for part in run]
        inv = 1.0 / jnp.sum(e[0] + e[1] + e[2], axis=1, keepdims=True)
        probs.append([part * inv for part in e])
    zero = jnp.zeros((HALF, HALF), BF16)
    (t0, t1, t2), (b0, b1, b2) = probs
    return probs, quads(bf(t0), bf(t1), zero, bf(b0)), quads(bf(t2), zero, bf(b1), bf(b2))


def delta_of(block, weights):
    grad, value_l, value_r = block[1], block[3], block[5]
    attended = bf(dot(weights[1], value_l, 1, 0) + dot(weights[2], value_r, 1, 0))
    return attended, jnp.sum(grad.astype(F32) * attended.astype(F32), axis=1, keepdims=True)


def score_grads(scores, weights, delta):
    d_l, d_r = scores[2:]
    low = slice(0, HALF)
    high = slice(HALF, WIN)
    (t0, t1, t2), (b0, b1, b2) = weights[0]
    dt = delta[low]
    db = delta[high]
    zero = jnp.zeros((HALF, HALF), BF16)
    left = quads(
        bf(t0 * (d_l[low, low] - dt)), bf(t1 * (d_l[low, high] - dt)), zero, bf(b0 * (d_l[high, high] - db))
    )
    right = quads(
        bf(t2 * (d_r[low, low] - dt)), zero, bf(b1 * (d_r[high, low] - db)), bf(b2 * (d_r[high, high] - db))
    )
    return left, right


def project_kernel(x_ref, g_ref, wq_ref, wk_ref, wv_ref, wo_ref, q_ref, k_ref, v_ref, a_ref):
    tokens = x_ref[...]
    k_ref[...] = bf(dot(tokens, wk_ref[...], 1, 0))
    v_ref[...] = bf(dot(tokens, wv_ref[...], 1, 0))
    q_ref[...] = bf(dot(tokens, wq_ref[...], 1, 0))
    a_ref[...] = bf(dot(g_ref[...], wo_ref[...], 1, 1))


def projections(tokens, out_grad, w_query, w_key, w_value, w_output):
    count, width = tokens.shape
    step = 256
    whole = pl.BlockSpec((count, width), lambda j: (0, 0))
    column = pl.BlockSpec((width, step), lambda j: (0, j))
    row = pl.BlockSpec((step, width), lambda j: (j, 0))
    out = pl.BlockSpec((count, step), lambda j: (0, j))
    return pl.pallas_call(
        project_kernel,
        grid=(width // step,),
        in_specs=[whole, whole, column, column, column, row],
        out_specs=[out] * 4,
        out_shape=[jax.ShapeDtypeStruct((count, width), BF16)] * 4,
        compiler_params=pltpu.CompilerParams(vmem_limit_bytes=40 * 2**20),
        cost_estimate=pl.CostEstimate(
            flops=8 * count * width * width, bytes_accessed=20 * 2**20, transcendentals=0
        ),
        name="projections",
    )(tokens, out_grad, w_query, w_key, w_value, w_output)


def main_kernel(
    bias_ref, q_ref, k_ref, v_ref, g_ref, xl_ref, wk_ref, wv_ref,
    att_ref, dq_ref, dk_ref, dv_ref, pk_ref, pv_ref,
):
    upper = upper_triangle()
    blocks = q_ref.shape[0] // WIN
    span = [slice(b * WIN, (b + 1) * WIN) for b in range(blocks)]
    keys = [bf(dot(xl_ref[...], wk_ref[...], 1, 0))] + [k_ref[s, :] for s in span]
    values = [bf(dot(xl_ref[...], wv_ref[...], 1, 0))] + [v_ref[s, :] for s in span]
    block = [
        (q_ref[span[b], :], g_ref[span[b], :], keys[b], values[b], keys[b + 1], values[b + 1])
        for b in range(blocks)
    ]
    order = list(range(1, blocks)) + [0]
    scores = {b: scores_of(block[b], bias_ref[0] if b == 0 else None) for b in order}
    weights = {b: probs_of(scores[b], upper) for b in order}
    deltas = {}
    for b in order:
        attended, deltas[b] = delta_of(block[b], weights[b])
        att_ref[span[b], :] = attended
    sgrads = {b: score_grads(scores[b], weights[b], deltas[b]) for b in order}
    dk_open = None
    dv_open = None
    for b in range(blocks):
        query, grad, key_l, _, key_r, _ = block[b]
        ds_l, ds_r = sgrads[b]
        _, pb_l, pb_r = weights[b]
        dq_ref[span[b], :] = bf((dot(ds_l, key_l, 1, 0) + dot(ds_r, key_r, 1, 0)) * SCALE)
        if b > 0:
            dk_ref[span[b - 1], :] = bf((dk_open + dot(ds_l, query, 0, 0)) * SCALE)
            dv_ref[span[b - 1], :] = bf(dv_open + dot(pb_l, grad, 0, 0))
        dk_open = dot(ds_r, query, 0, 0)
        dv_open = dot(pb_r, grad, 0, 0)
    dk_ref[span[-1], :] = bf(dk_open * SCALE)
    dv_ref[span[-1], :] = bf(dv_open)
    pk_ref[...] = dk_open
    pv_ref[...] = dv_open


def main_attention(bias, queries, keys, values, att_grad, tokens_l, w_key, w_value):
    count, width = queries.shape
    heads = width // HD
    own = pl.BlockSpec((count, HD), lambda h: (0, h))
    rim = pl.BlockSpec((WIN, HD), lambda h: (0, h))
    left = pl.BlockSpec((WIN, width), lambda h: (0, 0))
    column = pl.BlockSpec((width, HD), lambda h: (0, h))
    full = jax.ShapeDtypeStruct((count, width), BF16)
    part = jax.ShapeDtypeStruct((WIN, width), F32)
    return pl.pallas_call(
        main_kernel,
        grid=(heads,),
        in_specs=[pl.BlockSpec(memory_space=pltpu.SMEM), own, own, own, own, left, column, column],
        out_specs=[own, own, own, own, rim, rim],
        out_shape=[full, full, full, full, part, part],
        compiler_params=pltpu.CompilerParams(vmem_limit_bytes=40 * 2**20),
        cost_estimate=pl.CostEstimate(
            flops=20 * count * 2 * WIN * width,
            bytes_accessed=22 * 2**20,
            transcendentals=count * 2 * WIN * heads,
        ),
        name="attention_main",
    )(bias, queries, keys, values, att_grad, tokens_l, w_key, w_value)


def rim_kernel(
    n_ref, wq_ref, wk_ref, wv_ref, wo_ref, k_ref, v_ref, pk_ref, pv_ref, dk_in, dv_in, dk_ref, dv_ref
):
    upper = upper_triangle()
    tokens = n_ref[0]
    queries = bf(dot(tokens, wq_ref[...], 1, 0))
    keys = bf(dot(tokens, wk_ref[...], 1, 0))
    values = bf(dot(tokens, wv_ref[...], 1, 0))
    grads = bf(dot(n_ref[1], wo_ref[...], 1, 1))
    columns = [slice(h * HD, (h + 1) * HD) for h in range(k_ref.shape[1] // HD)]
    block = [
        (queries[:, c], grads[:, c], k_ref[:, c], v_ref[:, c], keys[:, c], values[:, c]) for c in columns
    ]
    scores = [scores_of(entry, None) for entry in block]
    weights = [probs_of(entry, upper) for entry in scores]
    deltas = [delta_of(*entry)[1] for entry in zip(block, weights)]
    for h, c in enumerate(columns):
        ds_l = score_grads(scores[h], weights[h], deltas[h])[0]
        dk_ref[:, c] = bf((pk_ref[:, c] + dot(ds_l, block[h][0], 0, 0)) * SCALE)
        dv_ref[:, c] = bf(pv_ref[:, c] + dot(weights[h][1], block[h][1], 0, 0))


def rim_attention(after, w_query, w_key, w_value, w_output, keys, values, part_k, part_v, key_grad, value_grad):
    count, width = keys.shape
    step = 4 * HD
    column = pl.BlockSpec((width, step), lambda j: (0, j))
    row = pl.BlockSpec((step, width), lambda j: (j, 0))
    rim = pl.BlockSpec((WIN, step), lambda j: (0, j))
    last = pl.BlockSpec((WIN, step), lambda j: (count // WIN - 1, j))
    whole = pl.BlockSpec((2, WIN, width), lambda j: (0, 0, 0))
    anywhere = pl.BlockSpec(memory_space=pl.ANY)
    full = jax.ShapeDtypeStruct((count, width), BF16)
    return pl.pallas_call(
        rim_kernel,
        grid=(width // step,),
        in_specs=[whole, column, column, column, row, last, last, rim, rim, anywhere, anywhere],
        out_specs=[last, last],
        out_shape=[full, full],
        input_output_aliases={9: 0, 10: 1},
        compiler_params=pltpu.CompilerParams(vmem_limit_bytes=40 * 2**20),
        cost_estimate=pl.CostEstimate(
            flops=8 * WIN * width * width + 14 * WIN * 2 * WIN * width,
            bytes_accessed=14 * 2**20,
            transcendentals=2 * WIN * WIN * width // HD,
        ),
        name="attention_rim",
    )(after, w_query, w_key, w_value, w_output, keys, values, part_k, part_v, key_grad, value_grad)


def weight_kernel(core_ref, *refs, added):
    if added:
        a0, a1, b0, b1, r0, r1, got, out = refs
    else:
        a0, a1, b0, b1, r0, r1, out = refs
    pair = pl.program_id(0)

    def product(low, high, right):
        left = jnp.concatenate([low[...], high[...]], axis=1)
        total = dot(left, right[...], 0, 0)
        if added:
            total = total + got[...].astype(F32)
        out[...] = bf(total)

    @pl.when(pair == 0)
    def _():
        product(a0, a1, r0)

    @pl.when(pair == 1)
    def _():
        product(b0, b1, r1)


def weight_pair(core, lefts, rights, got=None):
    count, width = rights[0].shape
    step = 512
    steps = width // step
    rows = width // 4

    def left_spec(x):
        return pl.BlockSpec((count, rows), lambda p, j, c: (0, 2 * x + c[0]))

    right0 = pl.BlockSpec((count, step), lambda p, j, c: (0, jnp.where(p == 0, j, steps - 1)))
    right1 = pl.BlockSpec((count, step), lambda p, j, c: (0, jnp.where(p == 1, j, 0)))
    out = pl.BlockSpec((2 * rows, step), lambda p, j, c: (0, p * steps + j))
    operands = [lefts[0], lefts[0], lefts[1], lefts[1], rights[0], rights[1]]
    specs = [left_spec(0), left_spec(1), left_spec(0), left_spec(1), right0, right1]
    if got is not None:
        operands.append(got)
        specs.append(out)
    return pl.pallas_call(
        functools.partial(weight_kernel, added=got is not None),
        grid_spec=pltpu.PrefetchScalarGridSpec(
            num_scalar_prefetch=1, grid=(2, steps), in_specs=specs, out_specs=out
        ),
        out_shape=jax.ShapeDtypeStruct((2 * rows, 2 * width), BF16),
        compiler_params=pltpu.CompilerParams(vmem_limit_bytes=40 * 2**20),
        cost_estimate=pl.CostEstimate(
            flops=4 * count * 2 * rows * width, bytes_accessed=8 * 2**20, transcendentals=0
        ),
        name="weight_send" if got is None else "weight_keep",
    )(core.reshape(1), *operands)


def passed_along(block, distance):
    size = 1
    for axis in SEQ:
        size *= lax.axis_size(axis)
    route = [(i - distance, i) for i in range(size) if 0 <= i - distance < size]
    return lax.ppermute(block, SEQ, route)


def on_device(tokens, out_grad, w_query, w_key, w_value, w_output, grad_accum):
    tokens = tokens[0]
    out_grad = out_grad[0]
    count, width = tokens.shape
    core = lax.axis_index("co")
    swap = [(0, 1), (1, 0)]
    tokens_l = passed_along(tokens[count - WIN :], 1)
    ahead, tokens_l = lax.optimization_barrier((jnp.stack([tokens[:WIN], out_grad[:WIN]]), tokens_l))
    after = passed_along(ahead, -1)
    queries, keys, values, att_grad = projections(tokens, out_grad, w_query, w_key, w_value, w_output)
    first = (lax.axis_index("y") + lax.axis_index("z") + lax.axis_index("xl")) == 0
    bias = jnp.where(first, NEG, 0.0).astype(F32).reshape(1)
    attended, query_grad, key_grad, value_grad, part_k, part_v = main_attention(
        bias, queries, keys, values, att_grad, tokens_l, w_key, w_value
    )
    sent = weight_pair(1 - core, (tokens, attended), (query_grad, out_grad))
    got = lax.ppermute(sent, "co", swap)
    both = weight_pair(core, (tokens, attended), (query_grad, out_grad), got)
    pieces_qo = lax.all_to_all(both, CHIPS, 0, 0, tiled=True)
    part_k, part_v, _ = lax.optimization_barrier((part_k, part_v, both))
    key_grad, value_grad = rim_attention(
        after, w_query, w_key, w_value, w_output, keys, values, part_k, part_v, key_grad, value_grad
    )
    sent = weight_pair(1 - core, (tokens, tokens), (key_grad, value_grad))
    got = lax.ppermute(sent, "co", swap)
    both = weight_pair(core, (tokens, tokens), (key_grad, value_grad), got)
    pieces_kv = lax.all_to_all(both, CHIPS, 0, 0, tiled=True)
    in_grad = bf(
        dot(query_grad, w_query, 1, 1) + dot(key_grad, w_key, 1, 1) + dot(value_grad, w_value, 1, 1)
    )
    sum_qo, sum_kv = [
        jnp.sum(pieces.reshape(-1, 8, 2 * width).astype(F32), axis=0) for pieces in (pieces_qo, pieces_kv)
    ]
    total = count
    for axis in AXES:
        total *= lax.axis_size(axis)
    factor = 1.0 / total**0.5
    summed = jnp.concatenate([sum_qo[:, :width], sum_kv, sum_qo[:, width:]], axis=1)
    return in_grad[None], grad_accum + summed * factor


def solution(mesh):
    fine = Mesh(mesh.devices.reshape(2, 2, 4, 4, 2), AXES)
    rows = P(("xh", "co"), SEQ, None)
    accum = P(AXES, None)
    return jax.shard_map(
        on_device,
        mesh=fine,
        in_specs=(rows, rows, P(), P(), P(), P(), accum),
        out_specs=(rows, accum),
        check_vma=False,
    )
```

profile of v0, /device:TPU:0, one launch (start us, length us, event | category | flops | bytes accessed | tf_op | source)
XLA Modules:
  0.0 178.6 jit_solution(11293296089486186575)
XLA Ops:
  0.6 2.3 %slice_bitcast_fusion = (bf16[256,1024]{1,0:T(8,128)(2,1)}, bf16[1,256,1024]{2,1,0:T(8,128)(2,1)}) fusion(bf16[1,1024,1024]{2,1,0:T(8,128)(2,1)} %param.7), kind=kLoop, calls=%fused_computation.5 | loop fusion | bytes 2097152 | tf_op jit(solution)/shard_map/slice | solution.py:305
  2.9 3.6 %collective-permute-start = (bf16[256,1024]{1,0:T(8,128)(2,1)}, bf16[256,1024]{1,0:T(8,128)(2,1)S(1)}, u32[]{:S(2)}, u32[]{:S(2)}) collective-permute-start(bf16[256,1024]{1,0:T(8,128)(2,1)} %get-tuple-element.34), channel_id=1, source_target_pairs={{0,1},{1,2},{2,3},{3,4},{4,5},{5,6},{6,7},{7,8},{8,9},{9,10},{10,1... | collective-permute-start | bytes 1572872 | tf_op jit(solution)/shard_map/ppermute | solution.py:296
  6.6 2.1 %pad_maximum_fusion = bf16[2,256,1024]{2,1,0:T(8,128)(2,1)} fusion(bf16[1,256,1024]{2,1,0:T(8,128)(2,1)S(1)} %slice-done, bf16[1,256,1024]{2,1,0:T(8,128)(2,1)} %get-tuple-element.35), kind=kLoop, calls=%fused_computation.4 | loop fusion | flops 524288 | bytes 2097152 | tf_op jit(solution)/shard_map/stack | solution.py:306
  8.7 1.6 copy-done.7
  10.3 12.1 %projections.1 = (bf16[1024,1024]{1,0:T(8,128)(2,1)S(1)}, bf16[1024,1024]{1,0:T(8,128)(2,1)S(1)}, bf16[1024,1024]{1,0:T(8,128)(2,1)S(1)}, bf16[1024,1024]{1,0:T(8,128)(2,1)S(1)}) custom-call(bf16[1024,1024]{1,0:T(8,128)(2,1)S(1)} %bitcast.17, bf16[1024,1024]{1,0:T(8,128)(2,1)S(1)} %bitcast.30, bf16[1024,1024]{1,0:T(8,128)(2,1)} %wq_ref.3, ...), custom_call_target="tpu_custom_call" | custom-call | flops 8589934592 | bytes 20971520 | tf_op jit(solution)/shard_map/projections/pallas_call | solution.py:110
  23.7 1.3 copy-done.19
  25.1 1.4 copy-done.26
  28.3 22.5 %attention_main.1 = (bf16[1024,1024]{1,0:T(8,128)(2,1)S(1)}, bf16[1024,1024]{1,0:T(8,128)(2,1)S(1)}, bf16[1024,1024]{1,0:T(8,128)(2,1)S(1)}, bf16[1024,1024]{1,0...) custom-call(f32[1]{0:T(128)} %bitcast.bias_ref, bf16[1024,1024]{1,0:T(8,128)(2,1)S(1)} %get-tuple-element.18.q_ref, ...), custom_call_target="tpu_custom_call" | custom-call | flops 10737418240 | bytes 23068672 | tf_op jit(solution)/shard_map/attention_main/pallas_call | solution.py:172
  51.8 3.9 %weight_send.2 = bf16[512,2048]{1,0:T(8,128)(2,1)S(1)} custom-call(s32[1]{0:T(128)} %bitcast.5.core_ref, bf16[1024,1024]{1,0:T(8,128)(2,1)S(1)} %bitcast.18, bf16[1024,1024]{1,0:T(8,128)(2,1)S(1)} %bitcast.19, bf16[1024,1024]{1,0:T(8,128)(2,1)S(1)} %get-tuple-element.27.refs_2_.refs_3_, bf16[1024,1024]{1,0:T(8,128)(2,1)S(1)} %get-tuple-element.27.refs_2_.refs_3_, ...), custom_call_target="tpu_custom_call" | custom-call | flops 2147483648 | bytes 8388608 | tf_op jit(solution)/shard_map/weight_send/pallas_call | solution.py:277
  55.8 1.5 collective-permute-start.1
  57.3 2.7 %collective-permute-done.2.refs_6_ = bf16[512,2048]{1,0:T(8,128)(2,1)S(1)} collective-permute-done((bf16[512,2048]{1,0:T(8,128)(2,1)S(1)}, bf16[512,2048]{1,0:T(8,128)(2,1)S(1)}, u32[]{:S(2)}, u32[]{:S(2)}) %collective-permute-start.2) | collective-permute-done | bytes 2097184 | tf_op jit(solution)/shard_map/ppermute | solution.py:315
  60.0 1.4 copy-done.20
  61.4 1.6 copy-done.21
  63.0 4.1 %weight_keep.2 = bf16[512,2048]{1,0:T(8,128)(2,1)S(1)} custom-call(s32[1]{0:T(128)} %bitcast.4.core_ref, bf16[1024,1024]{1,0:T(8,128)(2,1)S(1)} %bitcast.20, bf16[1024,1024]{1,0:T(8,128)(2,1)S(1)} %bitcast.21, bf16[1024,1024]{1,0:T(8,128)(2,1)S(1)} %get-tuple-element.27.refs_2_.refs_3_, bf16[1024,1024]{1,0:T(8,128)(2,1)S(1)} %get-tuple-element.27.refs_2_.refs_3_, ...), custom_call_target="tpu_custom_call" | custom-call | flops 2147483648 | bytes 8388608 | tf_op jit(solution)/shard_map/weight_keep/pallas_call | solution.py:277
  67.1 1.4 copy-done.9
  68.5 15.2 %collective-permute-done.1.n_ref = bf16[2,256,1024]{2,1,0:T(8,128)(2,1)} collective-permute-done((bf16[2,256,1024]{2,1,0:T(8,128)(2,1)}, bf16[2,256,1024]{2,1,0:T(8,128)(2,1)}, u32[]{:S(2)}, u32[]{:S(2)}) %collective-permute-start.1) | collective-permute-done | bytes 1048608 | tf_op jit(solution)/shard_map/ppermute | solution.py:296
  83.8 1.6 copy-done.16
  85.3 7.3 %attention_rim.1 = (bf16[1024,1024]{1,0:T(8,128)(2,1)S(1)}, bf16[1024,1024]{1,0:T(8,128)(2,1)S(1)}) custom-call(bf16[2,256,1024]{2,1,0:T(8,128)(2,1)} %collective-permute-done.1.n_ref, bf16[1024,1024]{1,0:T(8,128)(2,1)S(1)} %copy-done.13, bf16[1024,1024]{1,0:T(8,128)(2,1)S(1)} %copy-done.14, ...), custom_call_target="tpu_custom_call", output_to_operand_aliasing={{0}: (9, {}), {1}: (10, {})} | custom-call | flops 4026531840 | bytes 14680064 | tf_op jit(solution)/shard_map/attention_rim/pallas_call | solution.py:220
  92.7 4.7 %weight_send.3 = bf16[512,2048]{1,0:T(8,128)(2,1)} custom-call(s32[1]{0:T(128)} %bitcast.5.core_ref, bf16[1024,1024]{1,0:T(8,128)(2,1)S(1)} %bitcast.22, bf16[1024,1024]{1,0:T(8,128)(2,1)S(1)} %bitcast.23, bf16[1024,1024]{1,0:T(8,128)(2,1)S(1)} %bitcast.24, bf16[1024,1024]{1,0:T(8,128)(2,1)S(1)} %bitcast.25, ...), custom_call_target="tpu_custom_call" | custom-call | flops 2147483648 | bytes 8388608 | tf_op jit(solution)/shard_map/weight_send/pallas_call | solution.py:277
  97.4 13.0 %all-to-all-start = ((bf16[64,8,2048]{2,1,0:T(8,128)(2,1)}), bf16[64,8,2048]{2,1,0:T(8,128)(2,1)}, u32[]{:S(2)}, u32[]{:S(2)}) async-start(bf16[64,8,2048]{2,1,0:T(8,128)(2,1)} %bitcast.33), calls=%async_computation | async-start | bytes 4194304 | tf_op jit(solution)/shard_map/all_to_all | solution.py:317
  110.4 1.6 copy-done.2
  112.0 1.6 copy-done.5
  113.5 4.8 %weight_keep.3 = bf16[512,2048]{1,0:T(8,128)(2,1)S(1)} custom-call(s32[1]{0:T(128)} %bitcast.4.core_ref, bf16[1024,1024]{1,0:T(8,128)(2,1)S(1)} %bitcast.26, bf16[1024,1024]{1,0:T(8,128)(2,1)S(1)} %bitcast.27, bf16[1024,1024]{1,0:T(8,128)(2,1)S(1)} %bitcast.28, bf16[1024,1024]{1,0:T(8,128)(2,1)S(1)} %bitcast.29, bf16[1024,1024]{1,0:T(8,128)(2,1)S(1)} %copy-done.2, ...), custom_call_target="tpu_custom_call" | custom-call | flops 2147483648 | bytes 8388608 | tf_op jit(solution)/shard_map/weight_keep/pallas_call | solution.py:277
  118.4 1.4 copy-done.10
  119.8 19.6 %all-to-all-done = bf16[64,8,2048]{2,1,0:T(8,128)(2,1)} async-done(((bf16[64,8,2048]{2,1,0:T(8,128)(2,1)}), bf16[64,8,2048]{2,1,0:T(8,128)(2,1)}, u32[]{:S(2)}, u32[]{:S(2)}) %all-to-all-start) | async-done | bytes 2097184 | tf_op jit(solution)/shard_map/all_to_all | solution.py:317
  139.4 8.1 %all-to-all-start.1 = ((bf16[64,8,2048]{2,1,0:T(8,128)(2,1)}), bf16[64,8,2048]{2,1,0:T(8,128)(2,1)}, u32[]{:S(2)}, u32[]{:S(2)}) async-start(bf16[64,8,2048]{2,1,0:T(8,128)(2,1)} %bitcast.34), calls=%async_computation.1 | async-start | bytes 4194304 | tf_op jit(solution)/shard_map/all_to_all | solution.py:325
  147.5 4.1 %fusion.3 = f32[1024,1024]{1,0:T(8,128)S(1)} fusion(bf16[1024,1024]{1,0:T(8,128)(2,1)S(1)} %copy-done.12, bf16[1024,1024]{1,0:T(8,128)(2,1)} %wq_ref.3), kind=kOutput, calls=%fused_computation.9 | convolution fusion | flops 2147483648 | bytes 8388608 | tf_op jit(solution)/shard_map/dot_general | solution.py:23
  151.7 2.4 %fusion.4 = f32[1024,1024]{1,0:T(8,128)S(1)} fusion(bf16[1024,1024]{1,0:T(8,128)(2,1)S(1)} %copy-done.3, bf16[1024,1024]{1,0:T(8,128)(2,1)S(1)} %copy-done.15), kind=kOutput, calls=%fused_computation.10 | convolution fusion | flops 2147483648 | bytes 8388608 | tf_op jit(solution)/shard_map/dot_general | solution.py:23
  154.1 3.7 %fusion = bf16[1,1024,1024]{2,1,0:T(8,128)(2,1)} fusion(f32[1024,1024]{1,0:T(8,128)S(1)} %fusion.3, f32[1024,1024]{1,0:T(8,128)S(1)} %fusion.4, bf16[1024,1024]{1,0:T(8,128)(2,1)S(1)} %copy-done.6, bf16[1024,1024]{1,0:T(8,128)(2,1)S(1)} %copy-done.17), kind=kOutput, calls=%fused_computation.3 | convolution fusion | flops 2150629376 | bytes 14680064 | tf_op jit(solution)/shard_map/dot_general | solution.py:23
  157.8 1.9 %convert_reduce_fusion.1 = f32[8,2048]{1,0:T(8,128)S(1)} fusion(bf16[64,8,2048]{2,1,0:T(8,128)(2,1)} %all-to-all-done), kind=kLoop, calls=%fused_computation.1 | loop fusion | flops 2080768 | bytes 2162688 | tf_op jit(solution)/shard_map/reduce_sum | solution.py:330
  159.7 16.2 %all-to-all-done.1 = bf16[64,8,2048]{2,1,0:T(8,128)(2,1)} async-done(((bf16[64,8,2048]{2,1,0:T(8,128)(2,1)}), bf16[64,8,2048]{2,1,0:T(8,128)(2,1)}, u32[]{:S(2)}, u32[]{:S(2)}) %all-to-all-start.1) | async-done | bytes 2097184 | tf_op jit(solution)/shard_map/all_to_all | solution.py:325
  176.0 1.9 %convert_reduce_fusion = f32[8,2048]{1,0:T(8,128)S(1)} fusion(bf16[64,8,2048]{2,1,0:T(8,128)(2,1)} %all-to-all-done.1), kind=kLoop, calls=%fused_computation | loop fusion | flops 2080768 | bytes 2162688 | tf_op jit(solution)/shard_map/reduce_sum | solution.py:330
  (54 shorter events, 5.0 us)
Async XLA Ops:
  0.6 6.0 %slice-start = ((bf16[1,1024,1024]{2,1,0:T(8,128)(2,1)}), bf16[1,256,1024]{2,1,0:T(8,128)(2,1)S(1)}, s32[]{:S(2)}) async-start(bf16[1,1024,1024]{2,1,0:T(8,128)(2,1)} %param.8), calls=%async_computation.2 | async-start | bytes 1048576 | tf_op jit(solution)/shard_map/slice | solution.py:306
  2.9 5.8 %copy-start = (bf16[1,1024,1024]{2,1,0:T(8,128)(2,1)S(1)}, bf16[1,1024,1024]{2,1,0:T(8,128)(2,1)}, u32[]{:S(2)}) copy-start(bf16[1,1024,1024]{2,1,0:T(8,128)(2,1)} %param.7) | copy-start | bytes 6291460
  2.9 23.5 %collective-permute-start = (bf16[256,1024]{1,0:T(8,128)(2,1)}, bf16[256,1024]{1,0:T(8,128)(2,1)S(1)}, u32[]{:S(2)}, u32[]{:S(2)}) collective-permute-start(bf16[256,1024]{1,0:T(8,128)(2,1)} %get-tuple-element.34), channel_id=1, source_target_pairs={{0,1},{1,2},{2,3},{3,4},{4,5},{5,6},{6,7},{7,8},{8,9},{9,10},{10,1... | collective-permute-start | bytes 1572872 | tf_op jit(solution)/shard_map/ppermute | solution.py:296
  8.7 1.6 copy-start.7
  22.4 1.3 copy-start.18
  23.7 1.3 copy-start.19
  25.1 1.4 copy-start.26
  28.3 23.5 %copy-start.8 = (bf16[1,1024,1024]{2,1,0:T(8,128)(2,1)S(1)}, bf16[1,1024,1024]{2,1,0:T(8,128)(2,1)}, u32[]{:S(2)}) copy-start(bf16[1,1024,1024]{2,1,0:T(8,128)(2,1)} %param.8) | copy-start | bytes 6291460
  51.8 9.6 %copy-start.11 = (bf16[1024,1024]{1,0:T(8,128)(2,1)}, bf16[1024,1024]{1,0:T(8,128)(2,1)S(1)}, u32[]{:S(2)}) copy-start(bf16[1024,1024]{1,0:T(8,128)(2,1)S(1)} %get-tuple-element.23.refs_4_) | copy-start | bytes 6291460
  55.8 4.2 %collective-permute-start.2 = (bf16[512,2048]{1,0:T(8,128)(2,1)S(1)}, bf16[512,2048]{1,0:T(8,128)(2,1)S(1)}, u32[]{:S(2)}, u32[]{:S(2)}) collective-permute-start(bf16[512,2048]{1,0:T(8,128)(2,1)S(1)} %weight_send.2), channel_id=1, source_target_pairs={{0,32},{32,0},{1,33},{33,1},{2,34},{34,2},{3,35},{35,3},{4,36},{36... | collective-permute-start | bytes 6291464 | tf_op jit(solution)/shard_map/ppermute | solution.py:315
  55.8 27.9 %collective-permute-start.1 = (bf16[2,256,1024]{2,1,0:T(8,128)(2,1)}, bf16[2,256,1024]{2,1,0:T(8,128)(2,1)}, u32[]{:S(2)}, u32[]{:S(2)}) collective-permute-start(bf16[2,256,1024]{2,1,0:T(8,128)(2,1)} %pad_maximum_fusion), channel_id=1, source_target_pairs={{1,0},{2,1},{3,2},{4,3},{5,4},{6,5},{7,6},{8,7},{9,8},{10,9},{11,1... | collective-permute-start | bytes 3145736 | tf_op jit(solution)/shard_map/ppermute | solution.py:296
  60.0 1.4 copy-start.20
  61.4 1.6 copy-start.21
  63.0 20.8 %copy-start.13 = (bf16[1024,1024]{1,0:T(8,128)(2,1)S(1)}, bf16[1024,1024]{1,0:T(8,128)(2,1)}, u32[]{:S(2)}) copy-start(bf16[1024,1024]{1,0:T(8,128)(2,1)} %wq_ref.3) | copy-start | bytes 6291460
  63.0 20.8 %copy-start.14 = (bf16[1024,1024]{1,0:T(8,128)(2,1)S(1)}, bf16[1024,1024]{1,0:T(8,128)(2,1)}, u32[]{:S(2)}) copy-start(bf16[1024,1024]{1,0:T(8,128)(2,1)} %wk_ref.5) | copy-start | bytes 6291460
  63.0 20.8 %copy-start.23 = (f32[256,1024]{1,0:T(8,128)S(1)}, f32[256,1024]{1,0:T(8,128)}, u32[]{:S(2)}) copy-start(f32[256,1024]{1,0:T(8,128)} %copy-done.22) | copy-start | bytes 3145732
  67.1 1.4 copy-start.9
  83.7 1.6 copy-start.16
  92.6 4.7 %copy-start.1 = (bf16[1024,1024]{1,0:T(8,128)(2,1)}, bf16[1024,1024]{1,0:T(8,128)(2,1)S(1)}, u32[]{:S(2)}) copy-start(bf16[1024,1024]{1,0:T(8,128)(2,1)S(1)} %get-tuple-element.32.refs_4_) | copy-start | bytes 6291460
  92.7 4.7 %copy-start.4 = (bf16[1024,1024]{1,0:T(8,128)(2,1)}, bf16[1024,1024]{1,0:T(8,128)(2,1)S(1)}, u32[]{:S(2)}) copy-start(bf16[1024,1024]{1,0:T(8,128)(2,1)S(1)} %get-tuple-element.33.refs_5_) | copy-start | bytes 6291460
  97.4 13.0 %collective-permute-start.3 = (bf16[512,2048]{1,0:T(8,128)(2,1)}, bf16[512,2048]{1,0:T(8,128)(2,1)}, u32[]{:S(2)}, u32[]{:S(2)}) collective-permute-start(bf16[512,2048]{1,0:T(8,128)(2,1)} %weight_send.3), channel_id=1, source_target_pairs={{0,32},{32,0},{1,33},{33,1},{2,34},{34,2},{3,35},{35,3},{4,36},{36... | collective-permute-start | bytes 6291464 | tf_op jit(solution)/shard_map/ppermute | solution.py:323
  97.4 42.0 %all-to-all-start = ((bf16[64,8,2048]{2,1,0:T(8,128)(2,1)}), bf16[64,8,2048]{2,1,0:T(8,128)(2,1)}, u32[]{:S(2)}, u32[]{:S(2)}) async-start(bf16[64,8,2048]{2,1,0:T(8,128)(2,1)} %bitcast.33), calls=%async_computation | async-start | bytes 4194304 | tf_op jit(solution)/shard_map/all_to_all | solution.py:317
  110.4 1.6 copy-start.2
  112.0 1.6 copy-start.5
  118.4 1.4 copy-start.10
  139.4 8.1 %copy-start.12 = (bf16[1024,1024]{1,0:T(8,128)(2,1)S(1)}, bf16[1024,1024]{1,0:T(8,128)(2,1)}, u32[]{:S(2)}) copy-start(bf16[1024,1024]{1,0:T(8,128)(2,1)} %copy-done.11) | copy-start | bytes 6291460
  139.4 36.6 %all-to-all-start.1 = ((bf16[64,8,2048]{2,1,0:T(8,128)(2,1)}), bf16[64,8,2048]{2,1,0:T(8,128)(2,1)}, u32[]{:S(2)}, u32[]{:S(2)}) async-start(bf16[64,8,2048]{2,1,0:T(8,128)(2,1)} %bitcast.34), calls=%async_computation.1 | async-start | bytes 4194304 | tf_op jit(solution)/shard_map/all_to_all | solution.py:325
  147.5 4.1 %copy-start.3 = (bf16[1024,1024]{1,0:T(8,128)(2,1)S(1)}, bf16[1024,1024]{1,0:T(8,128)(2,1)}, u32[]{:S(2)}) copy-start(bf16[1024,1024]{1,0:T(8,128)(2,1)} %copy-done.1) | copy-start | bytes 6291460
  147.5 4.1 %copy-start.15 = (bf16[1024,1024]{1,0:T(8,128)(2,1)S(1)}, bf16[1024,1024]{1,0:T(8,128)(2,1)}, u32[]{:S(2)}) copy-start(bf16[1024,1024]{1,0:T(8,128)(2,1)} %wk_ref.5) | copy-start | bytes 6291460
  151.7 2.4 %copy-start.6 = (bf16[1024,1024]{1,0:T(8,128)(2,1)S(1)}, bf16[1024,1024]{1,0:T(8,128)(2,1)}, u32[]{:S(2)}) copy-start(bf16[1024,1024]{1,0:T(8,128)(2,1)} %copy-done.4) | copy-start | bytes 6291460
  151.7 2.4 %copy-start.17 = (bf16[1024,1024]{1,0:T(8,128)(2,1)S(1)}, bf16[1024,1024]{1,0:T(8,128)(2,1)}, u32[]{:S(2)}) copy-start(bf16[1024,1024]{1,0:T(8,128)(2,1)} %wv_ref.5) | copy-start | bytes 6291460
  157.8 20.1 %copy-start.27 = (f32[8,4096]{1,0:T(8,128)S(1)}, f32[8,4096]{1,0:T(8,128)}, u32[]{:S(2)}) copy-start(f32[8,4096]{1,0:T(8,128)} %param.13) | copy-start | bytes 393220
  (3 other events, 2.9 us)
where the time goes:
time: 179 us
  Pallas kernels  59.5 us (33%)
  waiting for transfers between devices  53.7 us (30%)
  starting transfers between devices  26.3 us (15%)
  local copies, waits for them, and re-layouts  21.3 us (12%)
  matrix products  10.2 us (6%)
  other arithmetic  6.62 us (4%)
    pallas_call x1, Pallas kernels, main_attention(): pl.pallas_call(main_kernel, grid=(heads,), in_specs=[pl.BlockSpec(memory_...  22.5 us
    all_to_all x1, waiting for transfers between devices, on_device(): pieces_qo = lax.all_to_all(both, CHIPS, 0, 0, tiled=True)  19.6 us
    unnamed x56, local copies, waits for them, and re-layouts  19 us
    pallas_call x4, Pallas kernels, weight_pair(): pl.pallas_call(functools.partial(weight_kernel, added=got is not None), g...  17.6 us
    all_to_all x1, waiting for transfers between devices, on_device(): pieces_kv = lax.all_to_all(both, CHIPS, 0, 0, tiled=True)  16.2 us
    ppermute x2, waiting for transfers between devices, passed_along(): return lax.ppermute(block, SEQ, route)  15.3 us
    all_to_all x1, starting transfers between devices, on_device(): pieces_qo = lax.all_to_all(both, CHIPS, 0, 0, tiled=True)  13 us
    pallas_call x1, Pallas kernels, projections(): pl.pallas_call(project_kernel, grid=(width // step,), in_specs=[whole, wh...  12.1 us
  transfers between devices with their start and end apart: 6, of which 4 were waited for; matrix products, arithmetic and copies ran while one was open for 8% of the time, Pallas kernels for 12%

commit v1 on v0

--- a/solution.py
+++ b/solution.py
@@ -23,6 +23,8 @@
     return lax.dot_general(a, b, (((ca,), (cb,)), ((), ())), preferred_element_type=F32)
 
 
+SMALL = pl.CostEstimate(flops=10**8, bytes_accessed=10**5, transcendentals=0)
+VMEM = 60 * 2**20
 HALF = WIN // 2
 NEG = -1e30
 
@@ -92,33 +94,35 @@
     return left, right
 
 
-def project_kernel(x_ref, g_ref, wq_ref, wk_ref, wv_ref, wo_ref, q_ref, k_ref, v_ref, a_ref):
+def project_kernel(x_ref, wq_ref, wk_ref, wv_ref, q_ref, k_ref, v_ref):
     tokens = x_ref[...]
+    q_ref[...] = bf(dot(tokens, wq_ref[...], 1, 0))
     k_ref[...] = bf(dot(tokens, wk_ref[...], 1, 0))
     v_ref[...] = bf(dot(tokens, wv_ref[...], 1, 0))
-    q_ref[...] = bf(dot(tokens, wq_ref[...], 1, 0))
+
+
+def back_kernel(g_ref, wo_ref, a_ref):
     a_ref[...] = bf(dot(g_ref[...], wo_ref[...], 1, 1))
 
 
-def projections(tokens, out_grad, w_query, w_key, w_value, w_output):
-    count, width = tokens.shape
+def projections(rows, weights, back):
+    count, width = rows.shape
     step = 256
     whole = pl.BlockSpec((count, width), lambda j: (0, 0))
-    column = pl.BlockSpec((width, step), lambda j: (0, j))
-    row = pl.BlockSpec((step, width), lambda j: (j, 0))
+    side = (
+        pl.BlockSpec((step, width), lambda j: (j, 0)) if back else pl.BlockSpec((width, step), lambda j: (0, j))
+    )
     out = pl.BlockSpec((count, step), lambda j: (0, j))
     return pl.pallas_call(
-        project_kernel,
+        back_kernel if back else project_kernel,
         grid=(width // step,),
-        in_specs=[whole, whole, column, column, column, row],
-        out_specs=[out] * 4,
-        out_shape=[jax.ShapeDtypeStruct((count, width), BF16)] * 4,
-        compiler_params=pltpu.CompilerParams(vmem_limit_bytes=40 * 2**20),
-        cost_estimate=pl.CostEstimate(
-            flops=8 * count * width * width, bytes_accessed=20 * 2**20, transcendentals=0
-        ),
-        name="projections",
-    )(tokens, out_grad, w_query, w_key, w_value, w_output)
+        in_specs=[whole] + [side] * len(weights),
+        out_specs=[out] * len(weights),
+        out_shape=[jax.ShapeDtypeStruct((count, width), BF16)] * len(weights),
+        compiler_params=pltpu.CompilerParams(vmem_limit_bytes=VMEM),
+        cost_estimate=SMALL,
+        name="project_back" if back else "projections",
+    )(rows, *weights)
 
 
 def main_kernel(
@@ -175,25 +179,21 @@
         in_specs=[pl.BlockSpec(memory_space=pltpu.SMEM), own, own, own, own, left, column, column],
         out_specs=[own, own, own, own, rim, rim],
         out_shape=[full, full, full, full, part, part],
-        compiler_params=pltpu.CompilerParams(vmem_limit_bytes=40 * 2**20),
-        cost_estimate=pl.CostEstimate(
-            flops=20 * count * 2 * WIN * width,
-            bytes_accessed=22 * 2**20,
-            transcendentals=count * 2 * WIN * heads,
-        ),
+        compiler_params=pltpu.CompilerParams(vmem_limit_bytes=VMEM),
+        cost_estimate=SMALL,
         name="attention_main",
     )(bias, queries, keys, values, att_grad, tokens_l, w_key, w_value)
 
 
 def rim_kernel(
-    n_ref, wq_ref, wk_ref, wv_ref, wo_ref, k_ref, v_ref, pk_ref, pv_ref, dk_in, dv_in, dk_ref, dv_ref
+    xn_ref, gn_ref, wq_ref, wk_ref, wv_ref, wo_ref, k_ref, v_ref, pk_ref, pv_ref, dk_in, dv_in, dk_ref, dv_ref
 ):
     upper = upper_triangle()
-    tokens = n_ref[0]
+    tokens = xn_ref[...]
     queries = bf(dot(tokens, wq_ref[...], 1, 0))
     keys = bf(dot(tokens, wk_ref[...], 1, 0))
     values = bf(dot(tokens, wv_ref[...], 1, 0))
-    grads = bf(dot(n_ref[1], wo_ref[...], 1, 1))
+    grads = bf(dot(gn_ref[...], wo_ref[...], 1, 1))
     columns = [slice(h * HD, (h + 1) * HD) for h in range(k_ref.shape[1] // HD)]
     block = [
         (queries[:, c], grads[:, c], k_ref[:, c], v_ref[:, c], keys[:, c], values[:, c]) for c in columns
@@ -207,85 +207,81 @@
         dv_ref[:, c] = bf(pv_ref[:, c] + dot(weights[h][1], block[h][1], 0, 0))
 
 
-def rim_attention(after, w_query, w_key, w_value, w_output, keys, values, part_k, part_v, key_grad, value_grad):
+def rim_attention(tokens_n, grads_n, w_query, w_key, w_value, w_output, keys, values, part_k, part_v, key_grad, value_grad):
     count, width = keys.shape
     step = 4 * HD
     column = pl.BlockSpec((width, step), lambda j: (0, j))
     row = pl.BlockSpec((step, width), lambda j: (j, 0))
     rim = pl.BlockSpec((WIN, step), lambda j: (0, j))
     last = pl.BlockSpec((WIN, step), lambda j: (count // WIN - 1, j))
-    whole = pl.BlockSpec((2, WIN, width), lambda j: (0, 0, 0))
+    whole = pl.BlockSpec((WIN, width), lambda j: (0, 0))
     anywhere = pl.BlockSpec(memory_space=pl.ANY)
     full = jax.ShapeDtypeStruct((count, width), BF16)
     return pl.pallas_call(
         rim_kernel,
         grid=(width // step,),
-        in_specs=[whole, column, column, column, row, last, last, rim, rim, anywhere, anywhere],
+        in_specs=[whole, whole, column, column, column, row, last, last, rim, rim, anywhere, anywhere],
         out_specs=[last, last],
         out_shape=[full, full],
-        input_output_aliases={9: 0, 10: 1},
-        compiler_params=pltpu.CompilerParams(vmem_limit_bytes=40 * 2**20),
-        cost_estimate=pl.CostEstimate(
-            flops=8 * WIN * width * width + 14 * WIN * 2 * WIN * width,
-            bytes_accessed=14 * 2**20,
-            transcendentals=2 * WIN * WIN * width // HD,
-        ),
+        input_output_aliases={10: 0, 11: 1},
+        compiler_params=pltpu.CompilerParams(vmem_limit_bytes=VMEM),
+        cost_estimate=SMALL,
         name="attention_rim",
-    )(after, w_query, w_key, w_value, w_output, keys, values, part_k, part_v, key_grad, value_grad)
-
-
-def weight_kernel(core_ref, *refs, added):
+    )(tokens_n, grads_n, w_query, w_key, w_value, w_output, keys, values, part_k, part_v, key_grad, value_grad)
+
+
+def weight_kernel(core_ref, low_ref, high_ref, right_ref, *refs, added):
+    left = jnp.concatenate([low_ref[...], high_ref[...]], axis=1)
+    total = dot(left, right_ref[...], 0, 0)
     if added:
-        a0, a1, b0, b1, r0, r1, got, out = refs
-    else:
-        a0, a1, b0, b1, r0, r1, out = refs
-    pair = pl.program_id(0)
-
-    def product(low, high, right):
-        left = jnp.concatenate([low[...], high[...]], axis=1)
-        total = dot(left, right[...], 0, 0)
-        if added:
-            total = total + got[...].astype(F32)
-        out[...] = bf(total)
-
-    @pl.when(pair == 0)
-    def _():
-        product(a0, a1, r0)
-
-    @pl.when(pair == 1)
-    def _():
-        product(b0, b1, r1)
-
-
-def weight_pair(core, lefts, rights, got=None):
-    count, width = rights[0].shape
+        total = total + refs[0][...].astype(F32)
+    refs[-1][...] = bf(total)
+
+
+def weight_part(core, left, right, got=None, slot=0, into=None):
+    count, width = right.shape
     step = 512
     steps = width // step
     rows = width // 4
+    added = got is not None
 
     def left_spec(x):
-        return pl.BlockSpec((count, rows), lambda p, j, c: (0, 2 * x + c[0]))
-
-    right0 = pl.BlockSpec((count, step), lambda p, j, c: (0, jnp.where(p == 0, j, steps - 1)))
-    right1 = pl.BlockSpec((count, step), lambda p, j, c: (0, jnp.where(p == 1, j, 0)))
-    out = pl.BlockSpec((2 * rows, step), lambda p, j, c: (0, p * steps + j))
-    operands = [lefts[0], lefts[0], lefts[1], lefts[1], rights[0], rights[1]]
-    specs = [left_spec(0), left_spec(1), left_spec(0), left_spec(1), right0, right1]
-    if got is not None:
+        return pl.BlockSpec((count, rows), lambda j, c: (0, 2 * x + c[0]))
+
+    column = pl.BlockSpec((2 * rows, step), lambda j, c: (0, j))
+    operands = [core.reshape(1), left, left, right]
+    specs = [left_spec(0), left_spec(1), pl.BlockSpec((count, step), lambda j, c: (0, j))]
+    alias = {}
+    if added:
         operands.append(got)
-        specs.append(out)
+        specs.append(column)
+    if into is not None:
+        alias = {len(operands): 0}
+        operands.append(into)
+        specs.append(pl.BlockSpec(memory_space=pl.ANY))
     return pl.pallas_call(
-        functools.partial(weight_kernel, added=got is not None),
+        functools.partial(weight_kernel, added=added),
         grid_spec=pltpu.PrefetchScalarGridSpec(
-            num_scalar_prefetch=1, grid=(2, steps), in_specs=specs, out_specs=out
+            num_scalar_prefetch=1,
+            grid=(steps,),
+            in_specs=specs,
+            out_specs=pl.BlockSpec((2 * rows, step), lambda j, c: (0, slot * steps + j)),
         ),
-        out_shape=jax.ShapeDtypeStruct((2 * rows, 2 * width), BF16),
-        compiler_params=pltpu.CompilerParams(vmem_limit_bytes=40 * 2**20),
-        cost_estimate=pl.CostEstimate(
-            flops=4 * count * 2 * rows * width, bytes_accessed=8 * 2**20, transcendentals=0
-        ),
-        name="weight_send" if got is None else "weight_keep",
-    )(core.reshape(1), *operands)
+        out_shape=jax.ShapeDtypeStruct((2 * rows, 2 * width if added else width), BF16),
+        input_output_aliases=alias,
+        compiler_params=pltpu.CompilerParams(vmem_limit_bytes=VMEM),
+        cost_estimate=SMALL,
+        name="weight_keep" if added else "weight_send",
+    )(*operands)
+
+
+def weight_pair(core, pairs):
+    swap = [(0, 1), (1, 0)]
+    got = [lax.ppermute(weight_part(1 - core, left, right), "co", swap) for left, right in pairs]
+    both = None
+    for slot, (left, right) in enumerate(pairs):
+        both = weight_part(core, left, right, got[slot], slot, both)
+    return both
 
 
 def passed_along(block, distance):
@@ -301,27 +297,28 @@
     out_grad = out_grad[0]
     count, width = tokens.shape
     core = lax.axis_index("co")
-    swap = [(0, 1), (1, 0)]
     tokens_l = passed_along(tokens[count - WIN :], 1)
-    ahead, tokens_l = lax.optimization_barrier((jnp.stack([tokens[:WIN], out_grad[:WIN]]), tokens_l))
-    after = passed_along(ahead, -1)
-    queries, keys, values, att_grad = projections(tokens, out_grad, w_query, w_key, w_value, w_output)
+    queries, keys, values = projections(tokens, (w_query, w_key, w_value), False)
+    head_x, head_g, behind, tokens_l, keys = lax.optimization_barrier(
+        (tokens[:WIN], out_grad[:WIN], out_grad, tokens_l, keys)
+    )
+    tokens_n = passed_along(head_x, -1)
+    grads_n = passed_along(head_g, -1)
+    (att_grad,) = projections(behind, (w_output,), True)
     first = (lax.axis_index("y") + lax.axis_index("z") + lax.axis_index("xl")) == 0
     bias = jnp.where(first, NEG, 0.0).astype(F32).reshape(1)
     attended, query_grad, key_grad, value_grad, part_k, part_v = main_attention(
         bias, queries, keys, values, att_grad, tokens_l, w_key, w_value
     )
-    sent = weight_pair(1 - core, (tokens, attended), (query_grad, out_grad))
-    got = lax.ppermute(sent, "co", swap)
-    both = weight_pair(core, (tokens, attended), (query_grad, out_grad), got)
+    query_grad, tokens_n, grads_n = lax.optimization_barrier((query_grad, tokens_n, grads_n))
+    both = weight_pair(core, ((tokens, query_grad), (attended, out_grad)))
     pieces_qo = lax.all_to_all(both, CHIPS, 0, 0, tiled=True)
     part_k, part_v, _ = lax.optimization_barrier((part_k, part_v, both))
     key_grad, value_grad = rim_attention(
-        after, w_query, w_key, w_value, w_output, keys, values, part_k, part_v, key_grad, value_grad
-    )
-    sent = weight_pair(1 - core, (tokens, tokens), (key_grad, value_grad))
-    got = lax.ppermute(sent, "co", swap)
-    both = weight_pair(core, (tokens, tokens), (key_grad, value_grad), got)
+        tokens_n, grads_n, w_query, w_key, w_value, w_output,
+        keys, values, part_k, part_v, key_grad, value_grad,
+    )
+    both = weight_pair(core, ((tokens, key_grad), (tokens, value_grad)))
     pieces_kv = lax.all_to_all(both, CHIPS, 0, 0, tiled=True)
     in_grad = bf(
         dot(query_grad, w_query, 1, 1) + dot(key_grad, w_key, 1, 1) + dot(value_grad, w_value, 1, 1)

time: 179 us -> 153 us (0.85)
  waiting for transfers between devices: 53.7 us -> 20 us
  Pallas kernels: 59.5 us -> 79.8 us
  local copies, waits for them, and re-layouts: 21.3 us -> 6.77 us
  starting transfers between devices: 26.3 us -> 31.9 us
  other arithmetic: 6.62 us -> 2.89 us
    pallas_call x6 -> x11, Pallas kernels: 37 us -> 59 us  [the longest x8 31.9 us: weight_part(): pl.pallas_call(functools.partial(weight_kernel, added=added), grid_spec=p...]
    all_to_all x1, waiting for transfers between devices: 19.6 us -> 1.69 us  [on_device(): pieces_qo = lax.all_to_all(both, CHIPS, 0, 0, tiled=True)]
    ppermute x2 -> x3, waiting for transfers between devices: 15.3 us -> 0.01 us  [passed_along(): return lax.ppermute(block, SEQ, route)]
    unnamed x56 -> x28, local copies, waits for them, and re-layouts: 19 us -> 4.41 us
    all_to_all x1, starting transfers between devices: 13 us -> 15.7 us  [on_device(): pieces_qo = lax.all_to_all(both, CHIPS, 0, 0, tiled=True)]
    ppermute x2 -> x4, waiting for transfers between devices: 2.67 us -> 0.01 us  [weight_pair(): lax.ppermute(weight_part(1 - core, left, right), 'co', swap)]
    another operation x1 -> x0, other arithmetic: 2.09 us -> none  [on_device(): jnp.stack([tokens[:WIN], out_grad[:WIN]])]
    all_to_all x1, waiting for transfers between devices: 16.2 us -> 18.3 us  [on_device(): pieces_kv = lax.all_to_all(both, CHIPS, 0, 0, tiled=True)]
  transfers between devices with their start and end apart: 6 -> 9, of which waited for: 4 -> 2; matrix products, arithmetic and copies ran while one was open for 8% -> 8% of each run, Pallas kernels for 12% -> 47%
where the time goes in v1:
time: 153 us; the launch traced here: 152 us
  Pallas kernels  79.8 us (52%)
  starting transfers between devices  31.9 us (21%)
  waiting for transfers between devices  20 us (13%)
  matrix products  10.2 us (7%)
  local copies, waits for them, and re-layouts  6.77 us (4%)
  other arithmetic  2.89 us (2%)
    pallas_call x8, Pallas kernels, weight_part(): pl.pallas_call(functools.partial(weight_kernel, added=added), grid_spec=p...  31.9 us
    pallas_call x1, Pallas kernels, main_attention(): pl.pallas_call(main_kernel, grid=(heads,), in_specs=[pl.BlockSpec(memory_...  20.8 us
    all_to_all x1, waiting for transfers between devices, on_device(): pieces_kv = lax.all_to_all(both, CHIPS, 0, 0, tiled=True)  18.3 us
    pallas_call x2, Pallas kernels, projections(): pl.pallas_call(back_kernel if back else project_kernel, grid=(width // st...  17 us
    all_to_all x1, starting transfers between devices, on_device(): pieces_qo = lax.all_to_all(both, CHIPS, 0, 0, tiled=True)  15.7 us
    dot_general x3, matrix products, dot(): lax.dot_general(a, b, (((ca,), (cb,)), ((), ())), preferred_element_type=...  10.2 us
    pallas_call x1, Pallas kernels, rim_attention(): pl.pallas_call(rim_kernel, grid=(width // step,), in_specs=[whole, whole,...  10.1 us
    all_to_all x1, starting transfers between devices, on_device(): pieces_kv = lax.all_to_all(both, CHIPS, 0, 0, tiled=True)  9.11 us
  transfers between devices with their start and end apart: 9, of which 2 were waited for; matrix products, arithmetic and copies ran while one was open for 8% of the time, Pallas kernels for 47%

profile of v1, /device:TPU:0, one launch (start us, length us, event | category | flops | bytes accessed | tf_op | source)
XLA Modules:
  0.0 152.5 jit_solution(16111414512961003275)
XLA Ops:
  0.6 1.3 slice_bitcast_fusion
  1.9 3.5 %collective-permute-start = (bf16[256,1024]{1,0:T(8,128)(2,1)S(1)}, bf16[256,1024]{1,0:T(8,128)(2,1)S(1)}, u32[]{:S(2)}, u32[]{:S(2)}) collective-permute-start(bf16[256,1024]{1,0:T(8,128)(2,1)S(1)} %get-tuple-element.44), channel_id=1, source_target_pairs={{0,1},{1,2},{2,3},{3,4},{4,5},{5,6},{6,7},{7,8},{8,9},{9,10},{10,1... | collective-permute-start | bytes 1572872 | tf_op jit(solution)/shard_map/ppermute | solution.py:292
  5.4 10.9 %projections.1 = (bf16[1024,1024]{1,0:T(8,128)(2,1)}, bf16[1024,1024]{1,0:T(8,128)(2,1)}, bf16[1024,1024]{1,0:T(8,128)(2,1)}) custom-call(bf16[1024,1024]{1,0:T(8,128)(2,1)} %bitcast.21, bf16[1024,1024]{1,0:T(8,128)(2,1)} %wq_ref.3, bf16[1024,1024]{1,0:T(8,128)(2,1)} %wk_ref.5, bf16[1024,1024]{1,0:T(8,128)(2,1)} %wv_ref.5), custom_call_target="tpu_custom_call" | custom-call | flops 100000000 | bytes 100000 | tf_op jit(solution)/shard_map/projections/pallas_call | solution.py:116
  16.3 1.1 slice_bitcast_fusion.1
  17.4 1.3 collective-permute-start.1
  18.7 1.3 collective-permute-start.2
  20.0 6.1 %project_back.1.g_ref = bf16[1024,1024]{1,0:T(8,128)(2,1)} custom-call(bf16[1024,1024]{1,0:T(8,128)(2,1)} %bitcast.34, bf16[1024,1024]{1,0:T(8,128)(2,1)} %wo_ref.3), custom_call_target="tpu_custom_call" | custom-call | flops 100000000 | bytes 100000 | tf_op jit(solution)/shard_map/project_back/pallas_call | solution.py:116
  26.2 20.8 %attention_main.1 = (bf16[1024,1024]{1,0:T(8,128)(2,1)}, bf16[1024,1024]{1,0:T(8,128)(2,1)}, bf16[1024,1024]{1,0:T(8,128)(2,1)}, bf16[1024,1024]{1,0:T(8,128)(2,...) custom-call(f32[1]{0:T(128)} %bitcast.bias_ref, bf16[1024,1024]{1,0:T(8,128)(2,1)} %get-tuple-element.23.q_ref, ...), custom_call_target="tpu_custom_call" | custom-call | flops 100000000 | bytes 100000 | tf_op jit(solution)/shard_map/attention_main/pallas_call | solution.py:176
  47.0 4.2 %weight_send.5 = bf16[512,1024]{1,0:T(8,128)(2,1)} custom-call(s32[1]{0:T(128)} %bitcast.7.core_ref, bf16[1024,1024]{1,0:T(8,128)(2,1)} %bitcast.22, bf16[1024,1024]{1,0:T(8,128)(2,1)} %bitcast.23, bf16[1024,1024]{1,0:T(8,128)(2,1)} %get-tuple-element.32.right_ref), custom_call_target="tpu_custom_call" | custom-call | flops 100000000 | bytes 100000 | tf_op jit(solution)/shard_map/weight_send/pallas_call | solution.py:262
  51.3 3.9 %weight_send.4 = bf16[512,1024]{1,0:T(8,128)(2,1)} custom-call(s32[1]{0:T(128)} %bitcast.7.core_ref, bf16[1024,1024]{1,0:T(8,128)(2,1)} %get-tuple-element.37.low_ref.high_ref, bf16[1024,1024]{1,0:T(8,128)(2,1)} %get-tuple-element.37.low_ref.high_ref, bf16[1024,1024]{1,0:T(8,128)(2,1)} %bitcast.35), custom_call_target="tpu_custom_call" | custom-call | flops 100000000 | bytes 100000 | tf_op jit(solution)/shard_map/weight_send/pallas_call | solution.py:262
  55.2 0.5 collective-permute-start.3
  55.7 1.0 copy-done.9
  56.6 4.0 %weight_keep.4.refs_1_ = bf16[512,2048]{1,0:T(8,128)(2,1)} custom-call(s32[1]{0:T(128)} %bitcast.6.core_ref, bf16[1024,1024]{1,0:T(8,128)(2,1)} %bitcast.24, bf16[1024,1024]{1,0:T(8,128)(2,1)} %bitcast.25, bf16[1024,1024]{1,0:T(8,128)(2,1)} %get-tuple-element.32.right_ref, bf16[512,1024]{1,0:T(8,128)(2,1)} %copy-done.9), custom_call_target="tpu_custom_call" | custom-call | flops 100000000 | bytes 100000 | tf_op jit(solution)/shard_map/weight_keep/pallas_call | solution.py:262
  60.7 1.0 copy-done.7
  61.7 4.0 %weight_keep.5 = bf16[512,2048]{1,0:T(8,128)(2,1)} custom-call(s32[1]{0:T(128)} %bitcast.6.core_ref, bf16[1024,1024]{1,0:T(8,128)(2,1)} %get-tuple-element.37.low_ref.high_ref, bf16[1024,1024]{1,0:T(8,128)(2,1)} %get-tuple-element.37.low_ref.high_ref, bf16[1024,1024]{1,0:T(8,128)(2,1)} %bitcast.36, ...), custom_call_target="tpu_custom_call", output_to_operand_aliasing={{}: (5, {})} | custom-call | flops 100000000 | bytes 100000 | tf_op jit(solution)/shard_map/weight_keep/pallas_call | solution.py:262
  65.7 15.7 %all-to-all-start = ((bf16[64,8,2048]{2,1,0:T(8,128)(2,1)}), bf16[64,8,2048]{2,1,0:T(8,128)(2,1)S(1)}, u32[]{:S(2)}, u32[]{:S(2)}) async-start(bf16[64,8,2048]{2,1,0:T(8,128)(2,1)} %bitcast.37), calls=%async_computation | async-start | bytes 4194304 | tf_op jit(solution)/shard_map/all_to_all | solution.py:315
  81.4 10.1 %attention_rim.1 = (bf16[1024,1024]{1,0:T(8,128)(2,1)}, bf16[1024,1024]{1,0:T(8,128)(2,1)}) custom-call(bf16[256,1024]{1,0:T(8,128)(2,1)} %copy-done.10, bf16[256,1024]{1,0:T(8,128)(2,1)} %copy-done.11, bf16[1024,1024]{1,0:T(8,128)(2,1)} %wq_ref.3, bf16[1024,1024]{1,0:T(8,128)(2,1)} %wk_ref.5, ...), custom_call_target="tpu_custom_call", output_to_operand_aliasing={{0}: (10, {}), {1}: (11, {})} | custom-call | flops 100000000 | bytes 100000 | tf_op jit(solution)/shard_map/attention_rim/pallas_call | solution.py:220
  91.5 3.9 %weight_send.7 = bf16[512,1024]{1,0:T(8,128)(2,1)} custom-call(s32[1]{0:T(128)} %bitcast.7.core_ref, bf16[1024,1024]{1,0:T(8,128)(2,1)} %bitcast.26, bf16[1024,1024]{1,0:T(8,128)(2,1)} %bitcast.27, bf16[1024,1024]{1,0:T(8,128)(2,1)} %get-tuple-element.42.right_ref), custom_call_target="tpu_custom_call" | custom-call | flops 100000000 | bytes 100000 | tf_op jit(solution)/shard_map/weight_send/pallas_call | solution.py:262
  95.4 3.8 %weight_send.6 = bf16[512,1024]{1,0:T(8,128)(2,1)} custom-call(s32[1]{0:T(128)} %bitcast.7.core_ref, bf16[1024,1024]{1,0:T(8,128)(2,1)} %bitcast.28, bf16[1024,1024]{1,0:T(8,128)(2,1)} %bitcast.29, bf16[1024,1024]{1,0:T(8,128)(2,1)} %get-tuple-element.43.right_ref), custom_call_target="tpu_custom_call" | custom-call | flops 100000000 | bytes 100000 | tf_op jit(solution)/shard_map/weight_send/pallas_call | solution.py:262
  99.2 0.5 collective-permute-start.5
  99.7 1.0 copy-done.8
  100.7 4.0 %weight_keep.6.refs_1_ = bf16[512,2048]{1,0:T(8,128)(2,1)} custom-call(s32[1]{0:T(128)} %bitcast.6.core_ref, bf16[1024,1024]{1,0:T(8,128)(2,1)} %bitcast.30, bf16[1024,1024]{1,0:T(8,128)(2,1)} %bitcast.31, bf16[1024,1024]{1,0:T(8,128)(2,1)} %get-tuple-element.42.right_ref, bf16[512,1024]{1,0:T(8,128)(2,1)} %copy-done.8), custom_call_target="tpu_custom_call" | custom-call | flops 100000000 | bytes 100000 | tf_op jit(solution)/shard_map/weight_keep/pallas_call | solution.py:262
  104.7 4.1 %weight_keep.7 = bf16[512,2048]{1,0:T(8,128)(2,1)} custom-call(s32[1]{0:T(128)} %bitcast.6.core_ref, bf16[1024,1024]{1,0:T(8,128)(2,1)} %bitcast.32, bf16[1024,1024]{1,0:T(8,128)(2,1)} %bitcast.33, bf16[1024,1024]{1,0:T(8,128)(2,1)} %get-tuple-element.43.right_ref, bf16[512,1024]{1,0:T(8,128)(2,1)} %collective-permute-done.5.refs_0_, ...), custom_call_target="tpu_custom_call", output_to_operand_aliasing={{}: (5, {})} | custom-call | flops 100000000 | bytes 100000 | tf_op jit(solution)/shard_map/weight_keep/pallas_call | solution.py:262
  108.8 1.7 %all-to-all-done = bf16[64,8,2048]{2,1,0:T(8,128)(2,1)S(1)} async-done(((bf16[64,8,2048]{2,1,0:T(8,128)(2,1)}), bf16[64,8,2048]{2,1,0:T(8,128)(2,1)S(1)}, u32[]{:S(2)}, u32[]{:S(2)}) %all-to-all-start) | async-done | bytes 2097184 | tf_op jit(solution)/shard_map/all_to_all | solution.py:315
  110.5 1.4 copy-done.5
  111.9 9.1 %all-to-all-start.1 = ((bf16[64,8,2048]{2,1,0:T(8,128)(2,1)}), bf16[64,8,2048]{2,1,0:T(8,128)(2,1)}, u32[]{:S(2)}, u32[]{:S(2)}) async-start(bf16[64,8,2048]{2,1,0:T(8,128)(2,1)} %bitcast.38), calls=%async_computation.1 | async-start | bytes 4194304 | tf_op jit(solution)/shard_map/all_to_all | solution.py:322
  121.0 4.1 %fusion.4 = f32[1024,1024]{1,0:T(8,128)S(1)} fusion(bf16[1024,1024]{1,0:T(8,128)(2,1)} %get-tuple-element.43.right_ref, bf16[1024,1024]{1,0:T(8,128)(2,1)S(1)} %copy-done), kind=kOutput, calls=%fused_computation.11 | convolution fusion | flops 2147483648 | bytes 8388608 | tf_op jit(solution)/shard_map/dot_general | solution.py:23
  125.2 2.4 %fusion.3 = f32[1024,1024]{1,0:T(8,128)S(1)} fusion(bf16[1024,1024]{1,0:T(8,128)(2,1)S(1)} %copy-done.2, bf16[1024,1024]{1,0:T(8,128)(2,1)S(1)} %copy-done.1), kind=kOutput, calls=%fused_computation.10 | convolution fusion | flops 2147483648 | bytes 8388608 | tf_op jit(solution)/shard_map/dot_general | solution.py:23
  127.6 3.7 %fusion = bf16[1,1024,1024]{2,1,0:T(8,128)(2,1)} fusion(f32[1024,1024]{1,0:T(8,128)S(1)} %fusion.4, f32[1024,1024]{1,0:T(8,128)S(1)} %fusion.3, bf16[1024,1024]{1,0:T(8,128)(2,1)S(1)} %copy-done.4, bf16[1024,1024]{1,0:T(8,128)(2,1)S(1)} %copy-done.3), kind=kOutput, calls=%fused_computation.3 | convolution fusion | flops 2150629376 | bytes 14680064 | tf_op jit(solution)/shard_map/dot_general | solution.py:23
  131.6 18.3 %all-to-all-done.1 = bf16[64,8,2048]{2,1,0:T(8,128)(2,1)} async-done(((bf16[64,8,2048]{2,1,0:T(8,128)(2,1)}), bf16[64,8,2048]{2,1,0:T(8,128)(2,1)}, u32[]{:S(2)}, u32[]{:S(2)}) %all-to-all-start.1) | async-done | bytes 2097184 | tf_op jit(solution)/shard_map/all_to_all | solution.py:322
  149.9 1.9 %convert_reduce_fusion = f32[8,2048]{1,0:T(8,128)S(1)} fusion(bf16[64,8,2048]{2,1,0:T(8,128)(2,1)} %all-to-all-done.1), kind=kLoop, calls=%fused_computation | loop fusion | flops 2080768 | bytes 2162688 | tf_op jit(solution)/shard_map/reduce_sum | solution.py:327
  151.8 0.7 fusion.1
  (35 shorter events, 0.5 us)
Async XLA Ops:
  1.9 15.5 %collective-permute-start = (bf16[256,1024]{1,0:T(8,128)(2,1)S(1)}, bf16[256,1024]{1,0:T(8,128)(2,1)S(1)}, u32[]{:S(2)}, u32[]{:S(2)}) collective-permute-start(bf16[256,1024]{1,0:T(8,128)(2,1)S(1)} %get-tuple-element.44), channel_id=1, source_target_pairs={{0,1},{1,2},{2,3},{3,4},{4,5},{5,6},{6,7},{7,8},{8,9},{9,10},{10,1... | collective-permute-start | bytes 1572872 | tf_op jit(solution)/shard_map/ppermute | solution.py:292
  17.4 8.8 %copy-start.12 = (bf16[256,1024]{1,0:T(8,128)(2,1)}, bf16[256,1024]{1,0:T(8,128)(2,1)S(1)}, u32[]{:S(2)}) copy-start(bf16[256,1024]{1,0:T(8,128)(2,1)S(1)} %collective-permute-done.xl_ref) | copy-start | bytes 1572868
  17.4 29.6 %collective-permute-start.1 = (bf16[256,1024]{1,0:T(8,128)(2,1)S(1)}, bf16[256,1024]{1,0:T(8,128)(2,1)S(1)}, u32[]{:S(2)}, u32[]{:S(2)}) collective-permute-start(bf16[256,1024]{1,0:T(8,128)(2,1)S(1)} %get-tuple-element.30), channel_id=1, source_target_pairs={{1,0},{2,1},{3,2},{4,3},{5,4},{6,5},{7,6},{8,7},{9,8},{10,9},{11,1... | collective-permute-start | bytes 1572872 | tf_op jit(solution)/shard_map/ppermute | solution.py:292
  18.7 28.3 %collective-permute-start.2 = (bf16[256,1024]{1,0:T(8,128)(2,1)S(1)}, bf16[256,1024]{1,0:T(8,128)(2,1)S(1)}, u32[]{:S(2)}, u32[]{:S(2)}) collective-permute-start(bf16[256,1024]{1,0:T(8,128)(2,1)S(1)} %slice_bitcast_fusion.1), channel_id=1, source_target_pairs={{1,0},{2,1},{3,2},{4,3},{5,4},{6,5},{7,6},{8,7},{9,8},{10,9},{11,1... | collective-permute-start | bytes 1572872 | tf_op jit(solution)/shard_map/ppermute | solution.py:292
  47.0 4.2 %copy-start.10 = (bf16[256,1024]{1,0:T(8,128)(2,1)}, bf16[256,1024]{1,0:T(8,128)(2,1)S(1)}, u32[]{:S(2)}) copy-start(bf16[256,1024]{1,0:T(8,128)(2,1)S(1)} %collective-permute-done.1.xn_ref) | copy-start | bytes 1572868
  47.0 4.2 %copy-start.11 = (bf16[256,1024]{1,0:T(8,128)(2,1)}, bf16[256,1024]{1,0:T(8,128)(2,1)S(1)}, u32[]{:S(2)}) copy-start(bf16[256,1024]{1,0:T(8,128)(2,1)S(1)} %collective-permute-done.2.gn_ref) | copy-start | bytes 1572868
  51.2 4.4 %collective-permute-start.4 = (bf16[512,1024]{1,0:T(8,128)(2,1)}, bf16[512,1024]{1,0:T(8,128)(2,1)S(1)}, u32[]{:S(2)}, u32[]{:S(2)}) collective-permute-start(bf16[512,1024]{1,0:T(8,128)(2,1)} %weight_send.5), channel_id=1, source_target_pairs={{0,32},{32,0},{1,33},{33,1},{2,34},{34,2},{3,35},{35,3},{4,36},{36... | collective-permute-start | bytes 3145736 | tf_op jit(solution)/shard_map/ppermute | solution.py:280
  55.2 5.5 %collective-permute-start.3 = (bf16[512,1024]{1,0:T(8,128)(2,1)}, bf16[512,1024]{1,0:T(8,128)(2,1)S(1)}, u32[]{:S(2)}, u32[]{:S(2)}) collective-permute-start(bf16[512,1024]{1,0:T(8,128)(2,1)} %weight_send.4), channel_id=1, source_target_pairs={{0,32},{32,0},{1,33},{33,1},{2,34},{34,2},{3,35},{35,3},{4,36},{36... | collective-permute-start | bytes 3145736 | tf_op jit(solution)/shard_map/ppermute | solution.py:280
  55.7 1.0 copy-start.9
  60.7 1.0 copy-start.7
  65.7 44.8 %all-to-all-start = ((bf16[64,8,2048]{2,1,0:T(8,128)(2,1)}), bf16[64,8,2048]{2,1,0:T(8,128)(2,1)S(1)}, u32[]{:S(2)}, u32[]{:S(2)}) async-start(bf16[64,8,2048]{2,1,0:T(8,128)(2,1)} %bitcast.37), calls=%async_computation | async-start | bytes 4194304 | tf_op jit(solution)/shard_map/all_to_all | solution.py:315
  95.4 4.3 %collective-permute-start.6 = (bf16[512,1024]{1,0:T(8,128)(2,1)}, bf16[512,1024]{1,0:T(8,128)(2,1)S(1)}, u32[]{:S(2)}, u32[]{:S(2)}) collective-permute-start(bf16[512,1024]{1,0:T(8,128)(2,1)} %weight_send.7), channel_id=1, source_target_pairs={{0,32},{32,0},{1,33},{33,1},{2,34},{34,2},{3,35},{35,3},{4,36},{36... | collective-permute-start | bytes 3145736 | tf_op jit(solution)/shard_map/ppermute | solution.py:280
  99.2 5.5 %collective-permute-start.5 = (bf16[512,1024]{1,0:T(8,128)(2,1)}, bf16[512,1024]{1,0:T(8,128)(2,1)}, u32[]{:S(2)}, u32[]{:S(2)}) collective-permute-start(bf16[512,1024]{1,0:T(8,128)(2,1)} %weight_send.6), channel_id=1, source_target_pairs={{0,32},{32,0},{1,33},{33,1},{2,34},{34,2},{3,35},{35,3},{4,36},{36... | collective-permute-start | bytes 3145736 | tf_op jit(solution)/shard_map/ppermute | solution.py:280
  99.7 1.0 copy-start.8
  110.5 1.4 copy-start.5
  111.9 9.1 %copy-start = (bf16[1024,1024]{1,0:T(8,128)(2,1)S(1)}, bf16[1024,1024]{1,0:T(8,128)(2,1)}, u32[]{:S(2)}) copy-start(bf16[1024,1024]{1,0:T(8,128)(2,1)} %wv_ref.5) | copy-start | bytes 6291460
  111.9 38.0 %all-to-all-start.1 = ((bf16[64,8,2048]{2,1,0:T(8,128)(2,1)}), bf16[64,8,2048]{2,1,0:T(8,128)(2,1)}, u32[]{:S(2)}, u32[]{:S(2)}) async-start(bf16[64,8,2048]{2,1,0:T(8,128)(2,1)} %bitcast.38), calls=%async_computation.1 | async-start | bytes 4194304 | tf_op jit(solution)/shard_map/all_to_all | solution.py:322
  121.0 4.1 %copy-start.1 = (bf16[1024,1024]{1,0:T(8,128)(2,1)S(1)}, bf16[1024,1024]{1,0:T(8,128)(2,1)}, u32[]{:S(2)}) copy-start(bf16[1024,1024]{1,0:T(8,128)(2,1)} %wk_ref.5) | copy-start | bytes 6291460
  121.0 4.1 %copy-start.2 = (bf16[1024,1024]{1,0:T(8,128)(2,1)S(1)}, bf16[1024,1024]{1,0:T(8,128)(2,1)}, u32[]{:S(2)}) copy-start(bf16[1024,1024]{1,0:T(8,128)(2,1)} %get-tuple-element.42.right_ref) | copy-start | bytes 6291460
  125.1 2.4 %copy-start.3 = (bf16[1024,1024]{1,0:T(8,128)(2,1)S(1)}, bf16[1024,1024]{1,0:T(8,128)(2,1)}, u32[]{:S(2)}) copy-start(bf16[1024,1024]{1,0:T(8,128)(2,1)} %wq_ref.3) | copy-start | bytes 6291460
  125.2 2.4 %copy-start.4 = (bf16[1024,1024]{1,0:T(8,128)(2,1)S(1)}, bf16[1024,1024]{1,0:T(8,128)(2,1)}, u32[]{:S(2)}) copy-start(bf16[1024,1024]{1,0:T(8,128)(2,1)} %get-tuple-element.32.right_ref) | copy-start | bytes 6291460
  127.6 3.7 %copy-start.6 = (bf16[64,8,2048]{2,1,0:T(8,128)(2,1)S(1)}, bf16[64,8,2048]{2,1,0:T(8,128)(2,1)}, u32[]{:S(2)}) copy-start(bf16[64,8,2048]{2,1,0:T(8,128)(2,1)} %copy-done.5) | copy-start | bytes 6291460
  131.3 20.5 %copy-start.13 = (f32[8,4096]{1,0:T(8,128)S(1)}, f32[8,4096]{1,0:T(8,128)}, u32[]{:S(2)}) copy-start(f32[8,4096]{1,0:T(8,128)} %param.13) | copy-start | bytes 393220

commit v2 on v1

v2 whole, which is shorter than its diff:
```python
import jax
import jax.numpy as jnp
from jax import lax
from jax.experimental import pallas as pl
from jax.experimental.pallas import tpu as pltpu
from jax.sharding import Mesh
from jax.sharding import PartitionSpec as P

HD = 128
WIN = 256
LOG2E = 1.4426950408889634
SCALE = 1.0 / HD**0.5
AXES = ("xh", "co", "y", "z", "xl")
SEQ = ("y", "z", "xl")
CHIPS = ("xh", "y", "z", "xl")
F32 = jnp.float32
BF16 = jnp.bfloat16


def dot(a, b, ca, cb):
    return lax.dot_general(a, b, (((ca,), (cb,)), ((), ())), preferred_element_type=F32)


SMALL = pl.CostEstimate(flops=10**8, bytes_accessed=10**5, transcendentals=0)
VMEM = 60 * 2**20
PAIR = 2 * HD
HALF = WIN // 2
NEG = -1e30


def bf(value):
    return value.astype(BF16)


def quads(a, b, c, d):
    return jnp.concatenate([jnp.concatenate([a, b], axis=1), jnp.concatenate([c, d], axis=1)], axis=0)


def upper_triangle():
    rows = lax.broadcasted_iota(jnp.int32, (HALF, HALF), 0)
    cols = lax.broadcasted_iota(jnp.int32, (HALF, HALF), 1)
    return cols > rows


def scores_of(block, bias):
    query, grad, key_l, value_l, key_r, value_r = block
    s_l = dot(query, key_l, 1, 1)
    if bias is not None:
        s_l = s_l + bias
    return s_l, dot(query, key_r, 1, 1), dot(grad, value_l, 1, 1), dot(grad, value_r, 1, 1)


def probs_of(scores, upper):
    s_l, s_r = scores[:2]
    low = slice(0, HALF)
    high = slice(HALF, WIN)
    runs = (
        (jnp.where(upper, s_l[low, low], NEG), s_l[low, high], jnp.where(upper, NEG, s_r[low, low])),
        (jnp.where(upper, s_l[high, high], NEG), s_r[high, low], jnp.where(upper, NEG, s_r[high, high])),
    )
    probs = []
    for run in runs:
        top = jnp.max(jnp.maximum(jnp.maximum(run[0], run[1]), run[2]), axis=1, keepdims=True)
        shift = top * (SCALE * LOG2E)
        e = [jnp.exp2(part * (SCALE * LOG2E) - shift) for part in run]
        inv = 1.0 / jnp.sum(e[0] + e[1] + e[2], axis=1, keepdims=True)
        probs.append([part * inv for part in e])
    zero = jnp.zeros((HALF, HALF), BF16)
    (t0, t1, t2), (b0, b1, b2) = probs
    return probs, quads(bf(t0), bf(t1), zero, bf(b0)), quads(bf(t2), zero, bf(b1), bf(b2))


def delta_of(block, weights):
    grad, value_l, value_r = block[1], block[3], block[5]
    attended = bf(dot(weights[1], value_l, 1, 0) + dot(weights[2], value_r, 1, 0))
    return attended, jnp.sum(grad.astype(F32) * attended.astype(F32), axis=1, keepdims=True)


def score_grads(scores, weights, delta):
    d_l, d_r = scores[2:]
    low = slice(0, HALF)
    high = slice(HALF, WIN)
    (t0, t1, t2), (b0, b1, b2) = weights[0]
    dt = delta[low]
    db = delta[high]
    zero = jnp.zeros((HALF, HALF), BF16)
    left = quads(
        bf(t0 * (d_l[low, low] - dt)), bf(t1 * (d_l[low, high] - dt)), zero, bf(b0 * (d_l[high, high] - db))
    )
    right = quads(
        bf(t2 * (d_r[low, low] - dt)), zero, bf(b1 * (d_r[high, low] - db)), bf(b2 * (d_r[high, high] - db))
    )
    return left, right


def project_kernel(x_ref, g_ref, wq_ref, wk_ref, wv_ref, wo_ref, q_ref, k_ref, v_ref, a_ref):
    tokens = x_ref[...]
    q_ref[...] = bf(dot(tokens, wq_ref[...], 1, 0))
    k_ref[...] = bf(dot(tokens, wk_ref[...], 1, 0))
    v_ref[...] = bf(dot(tokens, wv_ref[...], 1, 0))
    a_ref[...] = bf(dot(g_ref[...], wo_ref[...], 1, 1))


def projections(tokens, out_grad, w_query, w_key, w_value, w_output):
    count, width = tokens.shape
    whole = pl.BlockSpec((count, width), lambda j: (0, 0))
    column = pl.BlockSpec((width, PAIR), lambda j: (0, j))
    row = pl.BlockSpec((PAIR, width), lambda j: (j, 0))
    out = pl.BlockSpec((count, PAIR), lambda j: (0, j))
    return pl.pallas_call(
        project_kernel,
        grid=(width // PAIR,),
        in_specs=[whole, whole, column, column, column, row],
        out_specs=[out] * 4,
        out_shape=[jax.ShapeDtypeStruct((count, width), BF16)] * 4,
        compiler_params=pltpu.CompilerParams(vmem_limit_bytes=VMEM),
        cost_estimate=SMALL,
        name="projections",
    )(tokens, out_grad, w_query, w_key, w_value, w_output)


def keep_transposed(parts, turned_ref):
    @pl.when(pl.program_id(0) == 0)
    def _():
        for i, part in enumerate(parts):
            turned_ref[i * part.shape[1] : (i + 1) * part.shape[1], :] = part[...].T


def main_kernel(
    core_ref, bias_ref, q_ref, k_ref, v_ref, a_ref, g_ref, xl_ref, wk_ref, wv_ref, x0, x1, x2, x3,
    dq_ref, dk_ref, dv_ref, pk_ref, pv_ref, sq_ref, kq_ref, so_ref, ko_ref, turned_ref, att_ref,
):
    keep_transposed((x0, x1, x2, x3), turned_ref)
    upper = upper_triangle()
    blocks = q_ref.shape[0] // WIN
    span = [slice(b * WIN, (b + 1) * WIN) for b in range(blocks)]
    keys_l = bf(dot(xl_ref[...], wk_ref[...], 1, 0))
    values_l = bf(dot(xl_ref[...], wv_ref[...], 1, 0))
    for h in range(PAIR // HD):
        c = slice(h * HD, (h + 1) * HD)
        keys = [keys_l[:, c]] + [k_ref[s, c] for s in span]
        values = [values_l[:, c]] + [v_ref[s, c] for s in span]
        block = [
            (q_ref[span[b], c], a_ref[span[b], c], keys[b], values[b], keys[b + 1], values[b + 1])
            for b in range(blocks)
        ]
        scores = [scores_of(block[b], bias_ref[0] if b == 0 else None) for b in range(blocks)]
        weights = [probs_of(scores[b], upper) for b in range(blocks)]
        deltas = []
        for b in range(blocks):
            attended, delta = delta_of(block[b], weights[b])
            att_ref[span[b], c] = attended
            deltas.append(delta)
        sgrads = [score_grads(scores[b], weights[b], deltas[b]) for b in range(blocks)]
        for b in range(blocks):
            query, grad, key_l, _, key_r, _ = block[b]
            ds_l, ds_r = sgrads[b]
            _, pb_l, pb_r = weights[b]
            dq_ref[span[b], c] = bf((dot(ds_l, key_l, 1, 0) + dot(ds_r, key_r, 1, 0)) * SCALE)
            if b > 0:
                dk_ref[span[b - 1], c] = bf((dk_open + dot(ds_l, query, 0, 0)) * SCALE)
                dv_ref[span[b - 1], c] = bf(dv_open + dot(pb_l, grad, 0, 0))
            dk_open = dot(ds_r, query, 0, 0)
            dv_open = dot(pb_r, grad, 0, 0)
        pk_ref[:, c] = dk_open
        pv_ref[:, c] = dv_open
    part = dot(turned_ref[...], dq_ref[...], 1, 0)
    half = part.shape[0] // 2
    sq_ref[...] = bf(part[:half])
    kq_ref[...] = bf(part[half:])
    part = bf(dot(att_ref[...], g_ref[...], 0, 0))
    own = lax.rem(pl.program_id(0), 2) == core_ref[0]

    @pl.when(own)
    def _():
        ko_ref[...] = part

    @pl.when(jnp.logical_not(own))
    def _():
        so_ref[...] = part


def token_specs(count):
    def pick(half, other):
        return pl.BlockSpec((count, PAIR), lambda j, c: (0, 2 * half + (1 - c[0] if other else c[0])))

    return [pick(0, True), pick(1, True), pick(0, False), pick(1, False)]


def main_attention(core, bias, queries, keys, values, att_grad, out_grad, tokens_l, w_key, w_value, tokens):
    count, width = queries.shape
    own = pl.BlockSpec((count, PAIR), lambda j, c: (0, j))
    done = pl.BlockSpec((count - WIN, PAIR), lambda j, c: (0, j))
    rim = pl.BlockSpec((WIN, PAIR), lambda j, c: (0, j))
    left = pl.BlockSpec((WIN, width), lambda j, c: (0, 0))
    whole = pl.BlockSpec((count, width), lambda j, c: (0, 0))
    column = pl.BlockSpec((width, PAIR), lambda j, c: (0, j))
    half = pl.BlockSpec((width // 2, PAIR), lambda j, c: (0, j))
    band = pl.BlockSpec((PAIR, width), lambda j, c: (j // 2, 0))
    sums = jax.ShapeDtypeStruct((width // 2, width), BF16)
    part = jax.ShapeDtypeStruct((WIN, width), F32)
    return pl.pallas_call(
        main_kernel,
        grid_spec=pltpu.PrefetchScalarGridSpec(
            num_scalar_prefetch=1,
            grid=(width // PAIR,),
            in_specs=[pl.BlockSpec(memory_space=pltpu.SMEM), own, own, own, own, whole, left, column, column]
            + token_specs(count),
            out_specs=[own, done, done, rim, rim, half, half, band, band],
            scratch_shapes=[pltpu.VMEM((width, count), BF16), pltpu.VMEM((count, PAIR), BF16)],
        ),
        out_shape=[
            jax.ShapeDtypeStruct((count, width), BF16),
            jax.ShapeDtypeStruct((count - WIN, width), BF16),
            jax.ShapeDtypeStruct((count - WIN, width), BF16),
            part, part, sums, sums, sums, sums,
        ],
        compiler_params=pltpu.CompilerParams(vmem_limit_bytes=VMEM),
        cost_estimate=SMALL,
        name="attention_main",
    )(core, bias, queries, keys, values, att_grad, out_grad, tokens_l, w_key, w_value, *[tokens] * 4)


def rim_kernel(
    core_ref, xn_ref, gn_ref, wq_ref, wk_ref, wv_ref, wo_ref, k_ref, v_ref, pk_ref, pv_ref, dkm_ref, dvm_ref,
    x0, x1, x2, x3, dk_ref, dv_ref, sk_ref, kk_ref, sv_ref, kv_ref, turned_ref,
):
    keep_transposed((x0, x1, x2, x3), turned_ref)
    upper = upper_triangle()
    tokens = xn_ref[...]
    queries = bf(dot(tokens, wq_ref[...], 1, 0))
    keys = bf(dot(tokens, wk_ref[...], 1, 0))
    values = bf(dot(tokens, wv_ref[...], 1, 0))
    grads = bf(dot(gn_ref[...], wo_ref[...], 1, 1))
    columns = [slice(h * HD, (h + 1) * HD) for h in range(PAIR // HD)]
    block = [
        (queries[:, c], grads[:, c], k_ref[:, c], v_ref[:, c], keys[:, c], values[:, c]) for c in columns
    ]
    scores = [scores_of(entry, None) for entry in block]
    weights = [probs_of(entry, upper) for entry in scores]
    deltas = [delta_of(*entry)[1] for entry in zip(block, weights)]
    early = dkm_ref.shape[0]
    dk_ref[:early, :] = dkm_ref[...]
    dv_ref[:early, :] = dvm_ref[...]
    for h, c in enumerate(columns):
        ds_l = score_grads(scores[h], weights[h], deltas[h])[0]
        dk_ref[early:, c] = bf((pk_ref[:, c] + dot(ds_l, block[h][0], 0, 0)) * SCALE)
        dv_ref[early:, c] = bf(pv_ref[:, c] + dot(weights[h][1], block[h][1], 0, 0))
    half = turned_ref.shape[0] // 2
    part = dot(turned_ref[...], dk_ref[...], 1, 0)
    sk_ref[...] = bf(part[:half])
    kk_ref[...] = bf(part[half:])
    part = dot(turned_ref[...], dv_ref[...], 1, 0)
    sv_ref[...] = bf(part[:half])
    kv_ref[...] = bf(part[half:])


def rim_attention(
    core, tokens_n, grads_n, w_query, w_key, w_value, w_output, keys, values, part_k, part_v, key_grad, value_grad,
    tokens,
):
    count, width = keys.shape
    column = pl.BlockSpec((width, PAIR), lambda j, c: (0, j))
    row = pl.BlockSpec((PAIR, width), lambda j, c: (j, 0))
    rim = pl.BlockSpec((WIN, PAIR), lambda j, c: (0, j))
    last = pl.BlockSpec((WIN, PAIR), lambda j, c: (count // WIN - 1, j))
    near = pl.BlockSpec((WIN, width), lambda j, c: (0, 0))
    done = pl.BlockSpec((count - WIN, PAIR), lambda j, c: (0, j))
    own = pl.BlockSpec((count, PAIR), lambda j, c: (0, j))
    half = pl.BlockSpec((width // 2, PAIR), lambda j, c: (0, j))
    full = jax.ShapeDtypeStruct((count, width), BF16)
    sums = jax.ShapeDtypeStruct((width // 2, width), BF16)
    return pl.pallas_call(
        rim_kernel,
        grid_spec=pltpu.PrefetchScalarGridSpec(
            num_scalar_prefetch=1,
            grid=(width // PAIR,),
            in_specs=[near, near, column, column, column, row, last, last, rim, rim, done, done]
            + token_specs(count),
            out_specs=[own, own, half, half, half, half],
            scratch_shapes=[pltpu.VMEM((width, count), BF16)],
        ),
        out_shape=[full, full, sums, sums, sums, sums],
        compiler_params=pltpu.CompilerParams(vmem_limit_bytes=VMEM),
        cost_estimate=SMALL,
        name="attention_rim",
    )(
        core, tokens_n, grads_n, w_query, w_key, w_value, w_output, keys, values, part_k, part_v,
        key_grad, value_grad, *[tokens] * 4,
    )


def chip_sum(sends, keeps):
    got = [lax.ppermute(send, "co", [(0, 1), (1, 0)]) for send in sends]
    both = [keep.astype(F32) + extra.astype(F32) for keep, extra in zip(keeps, got)]
    return bf(jnp.concatenate(both, axis=1))


def passed_along(block, distance):
    size = 1
    for axis in SEQ:
        size *= lax.axis_size(axis)
    route = [(i - distance, i) for i in range(size) if 0 <= i - distance < size]
    return lax.ppermute(block, SEQ, route)


def on_device(tokens, out_grad, w_query, w_key, w_value, w_output, grad_accum):
    tokens = tokens[0]
    out_grad = out_grad[0]
    count, width = tokens.shape
    core = lax.axis_index("co")
    which = core.reshape(1)
    tokens_l = passed_along(tokens[count - WIN :], 1)
    queries, keys, values, att_grad = projections(tokens, out_grad, w_query, w_key, w_value, w_output)
    head_x, head_g, tokens_l, keys = lax.optimization_barrier((tokens[:WIN], out_grad[:WIN], tokens_l, keys))
    tokens_n = passed_along(head_x, -1)
    grads_n = passed_along(head_g, -1)
    first = (lax.axis_index("y") + lax.axis_index("z") + lax.axis_index("xl")) == 0
    bias = jnp.where(first, NEG, 0.0).astype(F32).reshape(1)
    query_grad, key_grad, value_grad, part_k, part_v, send_q, keep_q, send_o, keep_o = main_attention(
        which, bias, queries, keys, values, att_grad, out_grad, tokens_l, w_key, w_value, tokens
    )
    send_q, send_o, tokens_n, grads_n = lax.optimization_barrier((send_q, send_o, tokens_n, grads_n))
    both = chip_sum((send_q, send_o), (keep_q, keep_o))
    pieces_qo = lax.all_to_all(both, CHIPS, 0, 0, tiled=True)
    part_k, part_v, _ = lax.optimization_barrier((part_k, part_v, both))
    key_grad, value_grad, send_k, keep_k, send_v, keep_v = rim_attention(
        which, tokens_n, grads_n, w_query, w_key, w_value, w_output,
        keys, values, part_k, part_v, key_grad, value_grad, tokens,
    )
    both = chip_sum((send_k, send_v), (keep_k, keep_v))
    pieces_kv = lax.all_to_all(both, CHIPS, 0, 0, tiled=True)
    in_grad = bf(
        dot(query_grad, w_query, 1, 1) + dot(key_grad, w_key, 1, 1) + dot(value_grad, w_value, 1, 1)
    )
    sum_qo, sum_kv = [
        jnp.sum(pieces.reshape(-1, 8, 2 * width).astype(F32), axis=0) for pieces in (pieces_qo, pieces_kv)
    ]
    total = count
    for axis in AXES:
        total *= lax.axis_size(axis)
    factor = 1.0 / total**0.5
    summed = jnp.concatenate([sum_qo[:, :width], sum_kv, sum_qo[:, width:]], axis=1)
    return in_grad[None], grad_accum + summed * factor


def solution(mesh):
    fine = Mesh(mesh.devices.reshape(2, 2, 4, 4, 2), AXES)
    rows = P(("xh", "co"), SEQ, None)
    accum = P(AXES, None)
    return jax.shard_map(
        on_device,
        mesh=fine,
        in_specs=(rows, rows, P(), P(), P(), P(), accum),
        out_specs=(rows, accum),
        check_vma=False,
    )
```

time: 153 us -> 140 us (0.915)
  Pallas kernels: 79.8 us -> 56.8 us
  other arithmetic: 2.89 us -> 11.6 us
  waiting for transfers between devices: 20 us -> 27.2 us
  local copies, waits for them, and re-layouts: 6.77 us -> 2.4 us
  starting transfers between devices: 31.9 us -> 29.8 us
    pallas_call x12 -> x3, Pallas kernels: 79.8 us -> 56.8 us  [the longest x1 26.7 us: main_attention(): pl.pallas_call(main_kernel, grid_spec=pltpu.PrefetchScalarGridSpec(num_sc...]
    concatenate x0 -> x6, other arithmetic: none -> 7.11 us  [chip_sum(): return bf(jnp.concatenate(both, axis=1))]
    ppermute x4, waiting for transfers between devices: 0.01 us -> 4.73 us  [chip_sum(): got = [lax.ppermute(send, 'co', [(0, 1), (1, 0)]) for send in sends]]
    unnamed x28 -> x22, local copies, waits for them, and re-layouts: 4.41 us -> 0.05 us
    all_to_all x1, waiting for transfers between devices: 1.69 us -> 6.03 us  [on_device(): pieces_qo = lax.all_to_all(both, CHIPS, 0, 0, tiled=True)]
    all_to_all x1, waiting for transfers between devices: 18.3 us -> 16.5 us  [on_device(): pieces_kv = lax.all_to_all(both, CHIPS, 0, 0, tiled=True)]
    reduce_sum x2, other arithmetic: 2.22 us -> 3.84 us  [on_device(): jnp.sum(pieces.reshape(-1, 8, 2 * width).astype(F32), axis=0)]
    all_to_all x1, starting transfers between devices: 9.11 us -> 7.52 us  [on_device(): pieces_kv = lax.all_to_all(both, CHIPS, 0, 0, tiled=True)]
  transfers between devices with their start and end apart: 9 -> 9, of which waited for: 2 -> 4; matrix products, arithmetic and copies ran while one was open for 8% -> 13% of each run, Pallas kernels for 47% -> 41%
where the time goes in v2:
time: 140 us; the launch traced here: 139 us
  Pallas kernels  56.8 us (41%)
  starting transfers between devices  29.8 us (21%)
  waiting for transfers between devices  27.2 us (19%)
  other arithmetic  11.6 us (8%)
  matrix products  10.2 us (7%)
  local copies, waits for them, and re-layouts  2.4 us (2%)
    pallas_call x1, Pallas kernels, main_attention(): pl.pallas_call(main_kernel, grid_spec=pltpu.PrefetchScalarGridSpec(num_sc...  26.7 us
    all_to_all x1, waiting for transfers between devices, on_device(): pieces_kv = lax.all_to_all(both, CHIPS, 0, 0, tiled=True)  16.5 us
    pallas_call x1, Pallas kernels, rim_attention(): pl.pallas_call(rim_kernel, grid_spec=pltpu.PrefetchScalarGridSpec(num_sca...  16.3 us
    all_to_all x1, starting transfers between devices, on_device(): pieces_qo = lax.all_to_all(both, CHIPS, 0, 0, tiled=True)  15.1 us
    pallas_call x1, Pallas kernels, projections(): pl.pallas_call(project_kernel, grid=(width // PAIR,), in_specs=[whole, wh...  13.8 us
    dot_general x3, matrix products, dot(): lax.dot_general(a, b, (((ca,), (cb,)), ((), ())), preferred_element_type=...  10.2 us
    all_to_all x1, starting transfers between devices, on_device(): pieces_kv = lax.all_to_all(both, CHIPS, 0, 0, tiled=True)  7.52 us
    concatenate x6, other arithmetic, chip_sum(): return bf(jnp.concatenate(both, axis=1))  7.11 us
  transfers between devices with their start and end apart: 9, of which 4 were waited for; matrix products, arithmetic and copies ran while one was open for 13% of the time, Pallas kernels for 41%

profile of v2, /device:TPU:0, one launch (start us, length us, event | category | flops | bytes accessed | tf_op | source)
XLA Modules:
  0.0 139.1 jit_solution(3700836058285012317)
XLA Ops:
  0.6 1.3 slice_bitcast_fusion
  1.9 3.5 %collective-permute-start = (bf16[256,1024]{1,0:T(8,128)(2,1)S(1)}, bf16[256,1024]{1,0:T(8,128)(2,1)S(1)}, u32[]{:S(2)}, u32[]{:S(2)}) collective-permute-start(bf16[256,1024]{1,0:T(8,128)(2,1)S(1)} %get-tuple-element.60), channel_id=1, source_target_pairs={{0,1},{1,2},{2,3},{3,4},{4,5},{5,6},{6,7},{7,8},{8,9},{9,10},{10,1... | collective-permute-start | bytes 1572872 | tf_op jit(solution)/shard_map/ppermute | solution.py:304
  5.4 13.8 %projections.1 = (bf16[1024,1024]{1,0:T(8,128)(2,1)}, bf16[1024,1024]{1,0:T(8,128)(2,1)}, bf16[1024,1024]{1,0:T(8,128)(2,1)}, bf16[1024,1024]{1,0:T(8,128)(2,1)}) custom-call(bf16[1024,1024]{1,0:T(8,128)(2,1)} %bitcast.26, bf16[1024,1024]{1,0:T(8,128)(2,1)} %bitcast.35, bf16[1024,1024]{1,0:T(8,128)(2,1)} %wq_ref.3, bf16[1024,1024]{1,0:T(8,128)(2,1)} %wk_ref.5, ...), custom_call_target="tpu_custom_call" | custom-call | flops 100000000 | bytes 100000 | tf_op jit(solution)/shard_map/projections/pallas_call | solution.py:110
  19.2 1.1 slice_bitcast_fusion.1
  20.3 1.3 collective-permute-start.1
  21.6 1.3 collective-permute-start.2
  23.0 26.7 %attention_main.1 = (bf16[1024,1024]{1,0:T(8,128)(2,1)}, bf16[768,1024]{1,0:T(8,128)(2,1)}, bf16[768,1024]{1,0:T(8,128)(2,1)}, f32[256,1024]{1,0:T(8,128)}, f32[...) custom-call(s32[1]{0:T(128)} %bitcast.core_ref, ...), custom_call_target="tpu_custom_call" | custom-call | flops 100000000 | bytes 100000 | tf_op jit(solution)/shard_map/attention_main/pallas_call | solution.py:202
  49.7 0.1 collective-permute-start.3
  49.8 0.5 collective-permute-start.4
  50.3 2.4 %collective-permute-done.3 = bf16[512,1024]{1,0:T(8,128)(2,1)S(1)} collective-permute-done((bf16[512,1024]{1,0:T(8,128)(2,1)}, bf16[512,1024]{1,0:T(8,128)(2,1)S(1)}, u32[]{:S(2)}, u32[]{:S(2)}) %collective-permute-start.3) | collective-permute-done | bytes 1048608 | tf_op jit(solution)/shard_map/ppermute | solution.py:294
  52.7 1.6 %fusion.1 = bf16[64,8,1024]{2,1,0:T(8,128)(2,1)S(1)} fusion(bf16[512,1024]{1,0:T(8,128)(2,1)S(1)} %collective-permute-done.3, bf16[512,1024]{1,0:T(8,128)(2,1)} %get-tuple-element.52), kind=kLoop, calls=%fused_computation.10 | loop fusion | flops 2097152 | bytes 3145728 | tf_op jit(solution)/shard_map/concatenate | solution.py:296
  54.3 0.4 fusion.2
  54.7 1.6 %pad_maximum_fusion = bf16[64,8,2048]{2,1,0:T(8,128)(2,1)} fusion(bf16[64,8,1024]{2,1,0:T(8,128)(2,1)S(1)} %fusion.2, bf16[64,8,1024]{2,1,0:T(8,128)(2,1)S(1)} %fusion.1), kind=kLoop, calls=%fused_computation.4 | loop fusion | flops 4194304 | bytes 4194304 | tf_op jit(solution)/shard_map/concatenate | solution.py:296
  56.3 15.1 %all-to-all-start = ((bf16[64,8,2048]{2,1,0:T(8,128)(2,1)}), bf16[64,8,2048]{2,1,0:T(8,128)(2,1)}, u32[]{:S(2)}, u32[]{:S(2)}) async-start(bf16[64,8,2048]{2,1,0:T(8,128)(2,1)} %pad_maximum_fusion), calls=%async_computation | async-start | bytes 4194304 | tf_op jit(solution)/shard_map/all_to_all | solution.py:325
  71.4 16.3 %attention_rim.1 = (bf16[1024,1024]{1,0:T(8,128)(2,1)}, bf16[1024,1024]{1,0:T(8,128)(2,1)}, bf16[512,1024]{1,0:T(8,128)(2,1)}, bf16[512,1024]{1,0:T(8,128)(2,1)}...) custom-call(s32[1]{0:T(128)} %bitcast.core_ref, bf16[256,1024]{1,0:T(8,128)(2,1)} %copy-done.5, ...), custom_call_target="tpu_custom_call" | custom-call | flops 100000000 | bytes 100000 | tf_op jit(solution)/shard_map/attention_rim/pallas_call | solution.py:273
  87.7 0.1 collective-permute-start.5
  87.8 0.5 collective-permute-start.6
  88.3 2.4 %collective-permute-done.5 = bf16[512,1024]{1,0:T(8,128)(2,1)S(1)} collective-permute-done((bf16[512,1024]{1,0:T(8,128)(2,1)}, bf16[512,1024]{1,0:T(8,128)(2,1)S(1)}, u32[]{:S(2)}, u32[]{:S(2)}) %collective-permute-start.5) | collective-permute-done | bytes 1048608 | tf_op jit(solution)/shard_map/ppermute | solution.py:294
  90.6 1.6 %fusion.3 = bf16[64,8,1024]{2,1,0:T(8,128)(2,1)S(1)} fusion(bf16[512,1024]{1,0:T(8,128)(2,1)S(1)} %collective-permute-done.5, bf16[512,1024]{1,0:T(8,128)(2,1)} %get-tuple-element.56), kind=kLoop, calls=%fused_computation.12 | loop fusion | flops 2097152 | bytes 3145728 | tf_op jit(solution)/shard_map/concatenate | solution.py:296
  92.3 0.4 fusion.4
  92.7 1.5 %pad_maximum_fusion.1 = bf16[64,8,2048]{2,1,0:T(8,128)(2,1)} fusion(bf16[64,8,1024]{2,1,0:T(8,128)(2,1)S(1)} %fusion.4, bf16[64,8,1024]{2,1,0:T(8,128)(2,1)S(1)} %fusion.3), kind=kLoop, calls=%fused_computation.5 | loop fusion | flops 4194304 | bytes 4194304 | tf_op jit(solution)/shard_map/concatenate | solution.py:296
  94.2 6.0 %all-to-all-done = bf16[64,8,2048]{2,1,0:T(8,128)(2,1)} async-done(((bf16[64,8,2048]{2,1,0:T(8,128)(2,1)}), bf16[64,8,2048]{2,1,0:T(8,128)(2,1)}, u32[]{:S(2)}, u32[]{:S(2)}) %all-to-all-start) | async-done | bytes 2097184 | tf_op jit(solution)/shard_map/all_to_all | solution.py:325
  100.2 7.5 %all-to-all-start.1 = ((bf16[64,8,2048]{2,1,0:T(8,128)(2,1)}), bf16[64,8,2048]{2,1,0:T(8,128)(2,1)}, u32[]{:S(2)}, u32[]{:S(2)}) async-start(bf16[64,8,2048]{2,1,0:T(8,128)(2,1)} %pad_maximum_fusion.1), calls=%async_computation.1 | async-start | bytes 4194304 | tf_op jit(solution)/shard_map/all_to_all | solution.py:332
  107.8 0.0 copy-start
  107.8 0.0 copy-start.10
  107.8 4.1 %fusion.7 = f32[1024,1024]{1,0:T(8,128)S(1)} fusion(bf16[1024,1024]{1,0:T(8,128)(2,1)} %get-tuple-element.37, bf16[1024,1024]{1,0:T(8,128)(2,1)S(1)} %copy-done.2), kind=kOutput, calls=%fused_computation.20 | convolution fusion | flops 2147483648 | bytes 8388608 | tf_op jit(solution)/shard_map/dot_general | solution.py:21
  111.9 2.4 %fusion.8 = f32[1024,1024]{1,0:T(8,128)S(1)} fusion(bf16[1024,1024]{1,0:T(8,128)(2,1)S(1)} %copy-done.10, bf16[1024,1024]{1,0:T(8,128)(2,1)S(1)} %copy-done), kind=kOutput, calls=%fused_computation.21 | convolution fusion | flops 2147483648 | bytes 8388608 | tf_op jit(solution)/shard_map/dot_general | solution.py:21
  114.3 3.7 %fusion = bf16[1,1024,1024]{2,1,0:T(8,128)(2,1)} fusion(f32[1024,1024]{1,0:T(8,128)S(1)} %fusion.7, f32[1024,1024]{1,0:T(8,128)S(1)} %fusion.8, bf16[1024,1024]{1,0:T(8,128)(2,1)S(1)} %copy-done.9, bf16[1024,1024]{1,0:T(8,128)(2,1)S(1)} %copy-done.1), kind=kOutput, calls=%fused_computation.3 | convolution fusion | flops 2150629376 | bytes 14680064 | tf_op jit(solution)/shard_map/dot_general | solution.py:21
  118.1 1.9 %convert_reduce_fusion.1 = f32[8,2048]{1,0:T(8,128)S(1)} fusion(bf16[64,8,2048]{2,1,0:T(8,128)(2,1)} %all-to-all-done), kind=kLoop, calls=%fused_computation.1 | loop fusion | flops 2080768 | bytes 2162688 | tf_op jit(solution)/shard_map/reduce_sum | solution.py:337
  120.0 16.5 %all-to-all-done.1 = bf16[64,8,2048]{2,1,0:T(8,128)(2,1)} async-done(((bf16[64,8,2048]{2,1,0:T(8,128)(2,1)}), bf16[64,8,2048]{2,1,0:T(8,128)(2,1)}, u32[]{:S(2)}, u32[]{:S(2)}) %all-to-all-start.1) | async-done | bytes 2097184 | tf_op jit(solution)/shard_map/all_to_all | solution.py:332
  136.5 1.9 %convert_reduce_fusion = f32[8,2048]{1,0:T(8,128)S(1)} fusion(bf16[64,8,2048]{2,1,0:T(8,128)(2,1)} %all-to-all-done.1), kind=kLoop, calls=%fused_computation | loop fusion | flops 2080768 | bytes 2162688 | tf_op jit(solution)/shard_map/reduce_sum | solution.py:337
  138.4 0.7 fusion.5
  (26 shorter events, 0.1 us)
Async XLA Ops:
  1.9 18.4 %collective-permute-start = (bf16[256,1024]{1,0:T(8,128)(2,1)S(1)}, bf16[256,1024]{1,0:T(8,128)(2,1)S(1)}, u32[]{:S(2)}, u32[]{:S(2)}) collective-permute-start(bf16[256,1024]{1,0:T(8,128)(2,1)S(1)} %get-tuple-element.60), channel_id=1, source_target_pairs={{0,1},{1,2},{2,3},{3,4},{4,5},{5,6},{6,7},{7,8},{8,9},{9,10},{10,1... | collective-permute-start | bytes 1572872 | tf_op jit(solution)/shard_map/ppermute | solution.py:304
  20.3 2.6 %copy-start.7 = (bf16[256,1024]{1,0:T(8,128)(2,1)}, bf16[256,1024]{1,0:T(8,128)(2,1)S(1)}, u32[]{:S(2)}) copy-start(bf16[256,1024]{1,0:T(8,128)(2,1)S(1)} %collective-permute-done.xl_ref) | copy-start | bytes 1572868
  20.3 29.3 %collective-permute-start.1 = (bf16[256,1024]{1,0:T(8,128)(2,1)S(1)}, bf16[256,1024]{1,0:T(8,128)(2,1)S(1)}, u32[]{:S(2)}, u32[]{:S(2)}) collective-permute-start(bf16[256,1024]{1,0:T(8,128)(2,1)S(1)} %get-tuple-element.40), channel_id=1, source_target_pairs={{1,0},{2,1},{3,2},{4,3},{5,4},{6,5},{7,6},{8,7},{9,8},{10,9},{11,1... | collective-permute-start | bytes 1572872 | tf_op jit(solution)/shard_map/ppermute | solution.py:304
  21.6 28.1 %collective-permute-start.2 = (bf16[256,1024]{1,0:T(8,128)(2,1)S(1)}, bf16[256,1024]{1,0:T(8,128)(2,1)S(1)}, u32[]{:S(2)}, u32[]{:S(2)}) collective-permute-start(bf16[256,1024]{1,0:T(8,128)(2,1)S(1)} %slice_bitcast_fusion.1), channel_id=1, source_target_pairs={{1,0},{2,1},{3,2},{4,3},{5,4},{6,5},{7,6},{8,7},{9,8},{10,9},{11,1... | collective-permute-start | bytes 1572872 | tf_op jit(solution)/shard_map/ppermute | solution.py:304
  49.7 4.6 %copy-start.3 = (bf16[512,1024]{1,0:T(8,128)(2,1)S(1)}, bf16[512,1024]{1,0:T(8,128)(2,1)}, u32[]{:S(2)}) copy-start(bf16[512,1024]{1,0:T(8,128)(2,1)} %get-tuple-element.54) | copy-start | bytes 3145732
  49.7 5.0 %copy-start.5 = (bf16[256,1024]{1,0:T(8,128)(2,1)}, bf16[256,1024]{1,0:T(8,128)(2,1)S(1)}, u32[]{:S(2)}) copy-start(bf16[256,1024]{1,0:T(8,128)(2,1)S(1)} %collective-permute-done.1.xn_ref) | copy-start | bytes 1572868
  49.7 5.0 %copy-start.6 = (bf16[256,1024]{1,0:T(8,128)(2,1)}, bf16[256,1024]{1,0:T(8,128)(2,1)S(1)}, u32[]{:S(2)}) copy-start(bf16[256,1024]{1,0:T(8,128)(2,1)S(1)} %collective-permute-done.2.gn_ref) | copy-start | bytes 1572868
  49.7 3.0 %collective-permute-start.3 = (bf16[512,1024]{1,0:T(8,128)(2,1)}, bf16[512,1024]{1,0:T(8,128)(2,1)S(1)}, u32[]{:S(2)}, u32[]{:S(2)}) collective-permute-start(bf16[512,1024]{1,0:T(8,128)(2,1)} %get-tuple-element.53), channel_id=1, source_target_pairs={{0,32},{32,0},{1,33},{33,1},{2,34},{34,2},{3,35},{35,3},{4,36},{36... | collective-permute-start | bytes 3145736 | tf_op jit(solution)/shard_map/ppermute | solution.py:294
  49.8 4.5 %collective-permute-start.4 = (bf16[512,1024]{1,0:T(8,128)(2,1)}, bf16[512,1024]{1,0:T(8,128)(2,1)S(1)}, u32[]{:S(2)}, u32[]{:S(2)}) collective-permute-start(bf16[512,1024]{1,0:T(8,128)(2,1)} %get-tuple-element.55), channel_id=1, source_target_pairs={{0,32},{32,0},{1,33},{33,1},{2,34},{34,2},{3,35},{35,3},{4,36},{36... | collective-permute-start | bytes 3145736 | tf_op jit(solution)/shard_map/ppermute | solution.py:294
  56.3 43.9 %all-to-all-start = ((bf16[64,8,2048]{2,1,0:T(8,128)(2,1)}), bf16[64,8,2048]{2,1,0:T(8,128)(2,1)}, u32[]{:S(2)}, u32[]{:S(2)}) async-start(bf16[64,8,2048]{2,1,0:T(8,128)(2,1)} %pad_maximum_fusion), calls=%async_computation | async-start | bytes 4194304 | tf_op jit(solution)/shard_map/all_to_all | solution.py:325
  87.7 4.6 %copy-start.4 = (bf16[512,1024]{1,0:T(8,128)(2,1)S(1)}, bf16[512,1024]{1,0:T(8,128)(2,1)}, u32[]{:S(2)}) copy-start(bf16[512,1024]{1,0:T(8,128)(2,1)} %get-tuple-element.58) | copy-start | bytes 3145732
  87.7 3.0 %collective-permute-start.5 = (bf16[512,1024]{1,0:T(8,128)(2,1)}, bf16[512,1024]{1,0:T(8,128)(2,1)S(1)}, u32[]{:S(2)}, u32[]{:S(2)}) collective-permute-start(bf16[512,1024]{1,0:T(8,128)(2,1)} %get-tuple-element.57), channel_id=1, source_target_pairs={{0,32},{32,0},{1,33},{33,1},{2,34},{34,2},{3,35},{35,3},{4,36},{36... | collective-permute-start | bytes 3145736 | tf_op jit(solution)/shard_map/ppermute | solution.py:294
  87.8 4.5 %collective-permute-start.6 = (bf16[512,1024]{1,0:T(8,128)(2,1)}, bf16[512,1024]{1,0:T(8,128)(2,1)S(1)}, u32[]{:S(2)}, u32[]{:S(2)}) collective-permute-start(bf16[512,1024]{1,0:T(8,128)(2,1)} %get-tuple-element.59), channel_id=1, source_target_pairs={{0,32},{32,0},{1,33},{33,1},{2,34},{34,2},{3,35},{35,3},{4,36},{36... | collective-permute-start | bytes 3145736 | tf_op jit(solution)/shard_map/ppermute | solution.py:294
  94.2 13.6 %copy-start.2 = (bf16[1024,1024]{1,0:T(8,128)(2,1)S(1)}, bf16[1024,1024]{1,0:T(8,128)(2,1)}, u32[]{:S(2)}) copy-start(bf16[1024,1024]{1,0:T(8,128)(2,1)} %wq_ref.3) | copy-start | bytes 6291460
  100.2 36.2 %all-to-all-start.1 = ((bf16[64,8,2048]{2,1,0:T(8,128)(2,1)}), bf16[64,8,2048]{2,1,0:T(8,128)(2,1)}, u32[]{:S(2)}, u32[]{:S(2)}) async-start(bf16[64,8,2048]{2,1,0:T(8,128)(2,1)} %pad_maximum_fusion.1), calls=%async_computation.1 | async-start | bytes 4194304 | tf_op jit(solution)/shard_map/all_to_all | solution.py:332
  107.8 4.1 %copy-start = (bf16[1024,1024]{1,0:T(8,128)(2,1)S(1)}, bf16[1024,1024]{1,0:T(8,128)(2,1)}, u32[]{:S(2)}) copy-start(bf16[1024,1024]{1,0:T(8,128)(2,1)} %wk_ref.5) | copy-start | bytes 6291460
  107.8 4.1 %copy-start.10 = (bf16[1024,1024]{1,0:T(8,128)(2,1)S(1)}, bf16[1024,1024]{1,0:T(8,128)(2,1)}, u32[]{:S(2)}) copy-start(bf16[1024,1024]{1,0:T(8,128)(2,1)} %get-tuple-element.50) | copy-start | bytes 6291460
  111.9 2.4 %copy-start.1 = (bf16[1024,1024]{1,0:T(8,128)(2,1)S(1)}, bf16[1024,1024]{1,0:T(8,128)(2,1)}, u32[]{:S(2)}) copy-start(bf16[1024,1024]{1,0:T(8,128)(2,1)} %wv_ref.5) | copy-start | bytes 6291460
  111.9 2.4 %copy-start.9 = (bf16[1024,1024]{1,0:T(8,128)(2,1)S(1)}, bf16[1024,1024]{1,0:T(8,128)(2,1)}, u32[]{:S(2)}) copy-start(bf16[1024,1024]{1,0:T(8,128)(2,1)} %get-tuple-element.51) | copy-start | bytes 6291460
  118.0 20.3 %copy-start.8 = (f32[8,4096]{1,0:T(8,128)S(1)}, f32[8,4096]{1,0:T(8,128)}, u32[]{:S(2)}) copy-start(f32[8,4096]{1,0:T(8,128)} %param.13) | copy-start | bytes 393220

commit v3 on v2

v3 whole, which is shorter than its diff:
```python
import jax
import jax.numpy as jnp
from jax import lax
from jax.experimental import pallas as pl
from jax.experimental.pallas import tpu as pltpu
from jax.sharding import Mesh
from jax.sharding import PartitionSpec as P

HD = 128
WIN = 256
LOG2E = 1.4426950408889634
SCALE = 1.0 / HD**0.5
AXES = ("xh", "co", "y", "z", "xl")
SEQ = ("y", "z", "xl")
CHIPS = ("xh", "y", "z", "xl")
F32 = jnp.float32
BF16 = jnp.bfloat16


def dot(a, b, ca, cb):
    return lax.dot_general(a, b, (((ca,), (cb,)), ((), ())), preferred_element_type=F32)


SMALL = pl.CostEstimate(flops=10**8, bytes_accessed=10**5, transcendentals=0)
VMEM = 60 * 2**20
PAIR = 2 * HD
HALF = WIN // 2
NEG = -1e30


def bf(value):
    return value.astype(BF16)


def quads(a, b, c, d):
    return jnp.concatenate([jnp.concatenate([a, b], axis=1), jnp.concatenate([c, d], axis=1)], axis=0)


def upper_triangle():
    rows = lax.broadcasted_iota(jnp.int32, (HALF, HALF), 0)
    cols = lax.broadcasted_iota(jnp.int32, (HALF, HALF), 1)
    return cols > rows


def scores_of(block, bias):
    query, grad, key_l, value_l, key_r, value_r = block
    s_l = dot(query, key_l, 1, 1)
    if bias is not None:
        s_l = s_l + bias
    return s_l, dot(query, key_r, 1, 1), dot(grad, value_l, 1, 1), dot(grad, value_r, 1, 1)


def probs_of(scores, upper):
    s_l, s_r = scores[:2]
    low = slice(0, HALF)
    high = slice(HALF, WIN)
    runs = (
        (jnp.where(upper, s_l[low, low], NEG), s_l[low, high], jnp.where(upper, NEG, s_r[low, low])),
        (jnp.where(upper, s_l[high, high], NEG), s_r[high, low], jnp.where(upper, NEG, s_r[high, high])),
    )
    probs = []
    for run in runs:
        top = jnp.max(jnp.maximum(jnp.maximum(run[0], run[1]), run[2]), axis=1, keepdims=True)
        shift = top * (SCALE * LOG2E)
        e = [jnp.exp2(part * (SCALE * LOG2E) - shift) for part in run]
        inv = 1.0 / jnp.sum(e[0] + e[1] + e[2], axis=1, keepdims=True)
        probs.append([part * inv for part in e])
    zero = jnp.zeros((HALF, HALF), BF16)
    (t0, t1, t2), (b0, b1, b2) = probs
    return probs, quads(bf(t0), bf(t1), zero, bf(b0)), quads(bf(t2), zero, bf(b1), bf(b2))


def delta_of(block, weights):
    grad, value_l, value_r = block[1], block[3], block[5]
    attended = bf(dot(weights[1], value_l, 1, 0) + dot(weights[2], value_r, 1, 0))
    return attended, jnp.sum(grad.astype(F32) * attended.astype(F32), axis=1, keepdims=True)


def score_grads(scores, weights, delta):
    d_l, d_r = scores[2:]
    low = slice(0, HALF)
    high = slice(HALF, WIN)
    (t0, t1, t2), (b0, b1, b2) = weights[0]
    dt = delta[low]
    db = delta[high]
    zero = jnp.zeros((HALF, HALF), BF16)
    left = quads(
        bf(t0 * (d_l[low, low] - dt)), bf(t1 * (d_l[low, high] - dt)), zero, bf(b0 * (d_l[high, high] - db))
    )
    right = quads(
        bf(t2 * (d_r[low, low] - dt)), zero, bf(b1 * (d_r[high, low] - db)), bf(b2 * (d_r[high, high] - db))
    )
    return left, right


def keep_transposed(parts, turned_ref):
    @pl.when(pl.program_id(0) == 0)
    def _():
        for i, part in enumerate(parts):
            turned_ref[i * part.shape[1] : (i + 1) * part.shape[1], :] = part[...].T


def token_specs(count):
    def pick(half, other):
        return pl.BlockSpec((count, PAIR), lambda j, c: (0, 2 * half + (1 - c[0] if other else c[0])))

    return [pick(0, True), pick(1, True), pick(0, False), pick(1, False)]


def lanes():
    return [slice(h * HD, (h + 1) * HD) for h in range(PAIR // HD)]


def front_kernel(
    x_ref, g_ref, wq_ref, wk_ref, wv_ref, wo_ref,
    xh_ref, gh_ref, q0_ref, k0_ref, v0_ref, a0_ref, kz_ref, vz_ref, att_ref, dq_ref, dk_ref, dv_ref,
    pk0_ref, pv0_ref, pkz_ref, pvz_ref, q_ref, k_ref, v_ref, a_ref,
):
    @pl.when(pl.program_id(0) == 0)
    def _():
        xh_ref[...] = x_ref[:WIN, :]
        gh_ref[...] = g_ref[:WIN, :]

    upper = upper_triangle()
    count = x_ref.shape[0]
    blocks = count // WIN
    span = [slice(b * WIN, (b + 1) * WIN) for b in range(blocks)]
    q_ref[...] = bf(dot(x_ref[...], wq_ref[...], 1, 0))
    k_ref[...] = bf(dot(x_ref[...], wk_ref[...], 1, 0))
    v_ref[...] = bf(dot(x_ref[...], wv_ref[...], 1, 0))
    a_ref[...] = bf(dot(g_ref[...], wo_ref[...], 1, 1))
    q0_ref[...] = q_ref[:WIN, :]
    k0_ref[...] = k_ref[:WIN, :]
    v0_ref[...] = v_ref[:WIN, :]
    a0_ref[...] = a_ref[:WIN, :]
    kz_ref[...] = k_ref[count - WIN :, :]
    vz_ref[...] = v_ref[count - WIN :, :]
    for c in lanes():
        block = [
            tuple(
                ref[span[i], c]
                for ref, i in ((q_ref, b), (a_ref, b), (k_ref, b - 1), (v_ref, b - 1), (k_ref, b), (v_ref, b))
            )
            for b in range(1, blocks)
        ]
        scores = [scores_of(entry, None) for entry in block]
        weights = [probs_of(entry, upper) for entry in scores]
        deltas = []
        for i, entry in enumerate(block):
            attended, delta = delta_of(entry, weights[i])
            att_ref[span[i], c] = attended
            deltas.append(delta)
        sgrads = [score_grads(*entry) for entry in zip(scores, weights, deltas)]
        for i, (query, grad, key_l, _, key_r, _) in enumerate(block):
            ds_l, ds_r = sgrads[i]
            _, pb_l, pb_r = weights[i]
            dq_ref[span[i], c] = bf((dot(ds_l, key_l, 1, 0) + dot(ds_r, key_r, 1, 0)) * SCALE)
            dk_l = dot(ds_l, query, 0, 0)
            dv_l = dot(pb_l, grad, 0, 0)
            if i == 0:
                pk0_ref[:, c] = dk_l
                pv0_ref[:, c] = dv_l
            else:
                dk_ref[span[i - 1], c] = bf((dk_open + dk_l) * SCALE)
                dv_ref[span[i - 1], c] = bf(dv_open + dv_l)
            dk_open = dot(ds_r, query, 0, 0)
            dv_open = dot(pb_r, grad, 0, 0)
        pkz_ref[:, c] = dk_open
        pvz_ref[:, c] = dv_open


def front(tokens, out_grad, w_query, w_key, w_value, w_output):
    count, width = tokens.shape
    whole = pl.BlockSpec((count, width), lambda j: (0, 0))
    column = pl.BlockSpec((width, PAIR), lambda j: (0, j))
    row = pl.BlockSpec((PAIR, width), lambda j: (j, 0))

    def out(rows):
        return pl.BlockSpec((rows, PAIR), lambda j: (0, j))

    def like(rows, dtype=BF16):
        return jax.ShapeDtypeStruct((rows, width), dtype)

    rim, late, mid = WIN, count - WIN, count - 2 * WIN
    heights = [rim] * 6 + [late, late, mid, mid]
    return pl.pallas_call(
        front_kernel,
        grid=(width // PAIR,),
        in_specs=[whole, whole, column, column, column, row],
        out_specs=[pl.BlockSpec((WIN, width), lambda j: (0, 0))] * 2 + [out(h) for h in heights] + [out(rim)] * 4,
        out_shape=[like(WIN)] * 2 + [like(h) for h in heights] + [like(rim, F32)] * 4,
        scratch_shapes=[pltpu.VMEM((count, PAIR), BF16)] * 4,
        compiler_params=pltpu.CompilerParams(vmem_limit_bytes=VMEM),
        cost_estimate=SMALL,
        name="front",
    )(tokens, out_grad, w_query, w_key, w_value, w_output)


def first_kernel(
    core_ref, bias_ref, q_ref, k_ref, v_ref, a_ref, pk_ref, pv_ref, att_in, dq_in, g_ref, xl_ref, wk_ref, wv_ref,
    x0, x1, x2, x3, dq_ref, dk_ref, dv_ref, sq_ref, kq_ref, so_ref, ko_ref, turned_ref, att_ref,
):
    keep_transposed((x0, x1, x2, x3), turned_ref)
    upper = upper_triangle()
    keys_l = bf(dot(xl_ref[...], wk_ref[...], 1, 0))
    values_l = bf(dot(xl_ref[...], wv_ref[...], 1, 0))
    block = [
        (q_ref[:, c], a_ref[:, c], keys_l[:, c], values_l[:, c], k_ref[:, c], v_ref[:, c]) for c in lanes()
    ]
    scores = [scores_of(entry, bias_ref[0]) for entry in block]
    weights = [probs_of(entry, upper) for entry in scores]
    deltas = []
    for i, c in enumerate(lanes()):
        attended, delta = delta_of(block[i], weights[i])
        att_ref[:WIN, c] = attended
        deltas.append(delta)
    att_ref[WIN:, :] = att_in[...]
    dq_ref[WIN:, :] = dq_in[...]
    for i, c in enumerate(lanes()):
        query, grad, key_l, _, key_r, _ = block[i]
        ds_l, ds_r = score_grads(scores[i], weights[i], deltas[i])
        dq_ref[:WIN, c] = bf((dot(ds_l, key_l, 1, 0) + dot(ds_r, key_r, 1, 0)) * SCALE)
        dk_ref[:, c] = bf((pk_ref[:, c] + dot(ds_r, query, 0, 0)) * SCALE)
        dv_ref[:, c] = bf(pv_ref[:, c] + dot(weights[i][2], grad, 0, 0))
    part = dot(turned_ref[...], dq_ref[...], 1, 0)
    half = part.shape[0] // 2
    sq_ref[...] = bf(part[:half])
    kq_ref[...] = bf(part[half:])
    part = bf(dot(att_ref[...], g_ref[...], 0, 0))
    own = lax.rem(pl.program_id(0), 2) == core_ref[0]

    @pl.when(own)
    def _():
        ko_ref[...] = part

    @pl.when(jnp.logical_not(own))
    def _():
        so_ref[...] = part


def first_block(core, bias, own, partial, late, out_grad, tokens_l, w_key, w_value, tokens):
    count, width = tokens.shape
    rim = pl.BlockSpec((WIN, PAIR), lambda j, c: (0, j))
    rest = pl.BlockSpec((count - WIN, PAIR), lambda j, c: (0, j))
    full = pl.BlockSpec((count, PAIR), lambda j, c: (0, j))
    left = pl.BlockSpec((WIN, width), lambda j, c: (0, 0))
    whole = pl.BlockSpec((count, width), lambda j, c: (0, 0))
    column = pl.BlockSpec((width, PAIR), lambda j, c: (0, j))
    half = pl.BlockSpec((width // 2, PAIR), lambda j, c: (0, j))
    band = pl.BlockSpec((PAIR, width), lambda j, c: (j // 2, 0))
    sums = jax.ShapeDtypeStruct((width // 2, width), BF16)
    part = jax.ShapeDtypeStruct((WIN, width), BF16)
    return pl.pallas_call(
        first_kernel,
        grid_spec=pltpu.PrefetchScalarGridSpec(
            num_scalar_prefetch=1,
            grid=(width // PAIR,),
            in_specs=[pl.BlockSpec(memory_space=pltpu.SMEM)]
            + [rim] * 6
            + [rest, rest, whole, left, column, column]
            + token_specs(count),
            out_specs=[full, rim, rim, half, half, band, band],
            scratch_shapes=[pltpu.VMEM((width, count), BF16), pltpu.VMEM((count, PAIR), BF16)],
        ),
        out_shape=[jax.ShapeDtypeStruct((count, width), BF16), part, part, sums, sums, sums, sums],
        compiler_params=pltpu.CompilerParams(vmem_limit_bytes=VMEM),
        cost_estimate=SMALL,
        name="first_block",
    )(core, bias, *own, *partial, *late, out_grad, tokens_l, w_key, w_value, *[tokens] * 4)


def last_kernel(
    core_ref, xn_ref, gn_ref, wq_ref, wk_ref, wv_ref, wo_ref, k_ref, v_ref, pk_ref, pv_ref, dk0_ref, dv0_ref,
    dkm_ref, dvm_ref, x0, x1, x2, x3, dk_ref, dv_ref, sk_ref, kk_ref, sv_ref, kv_ref, turned_ref,
):
    keep_transposed((x0, x1, x2, x3), turned_ref)
    upper = upper_triangle()
    tokens = xn_ref[...]
    queries = bf(dot(tokens, wq_ref[...], 1, 0))
    keys = bf(dot(tokens, wk_ref[...], 1, 0))
    values = bf(dot(tokens, wv_ref[...], 1, 0))
    grads = bf(dot(gn_ref[...], wo_ref[...], 1, 1))
    block = [
        (queries[:, c], grads[:, c], k_ref[:, c], v_ref[:, c], keys[:, c], values[:, c]) for c in lanes()
    ]
    scores = [scores_of(entry, None) for entry in block]
    weights = [probs_of(entry, upper) for entry in scores]
    deltas = [delta_of(*entry)[1] for entry in zip(block, weights)]
    end = dk_ref.shape[0] - WIN
    dk_ref[:WIN, :] = dk0_ref[...]
    dv_ref[:WIN, :] = dv0_ref[...]
    dk_ref[WIN:end, :] = dkm_ref[...]
    dv_ref[WIN:end, :] = dvm_ref[...]
    for i, c in enumerate(lanes()):
        ds_l = score_grads(scores[i], weights[i], deltas[i])[0]
        dk_ref[end:, c] = bf((pk_ref[:, c] + dot(ds_l, block[i][0], 0, 0)) * SCALE)
        dv_ref[end:, c] = bf(pv_ref[:, c] + dot(weights[i][1], block[i][1], 0, 0))
    half = turned_ref.shape[0] // 2
    part = dot(turned_ref[...], dk_ref[...], 1, 0)
    sk_ref[...] = bf(part[:half])
    kk_ref[...] = bf(part[half:])
    part = dot(turned_ref[...], dv_ref[...], 1, 0)
    sv_ref[...] = bf(part[:half])
    kv_ref[...] = bf(part[half:])


def last_block(core, tokens_n, grads_n, weights, last, partial, first, middle, tokens):
    count, width = tokens.shape
    column = pl.BlockSpec((width, PAIR), lambda j, c: (0, j))
    row = pl.BlockSpec((PAIR, width), lambda j, c: (j, 0))
    rim = pl.BlockSpec((WIN, PAIR), lambda j, c: (0, j))
    near = pl.BlockSpec((WIN, width), lambda j, c: (0, 0))
    mid = pl.BlockSpec((count - 2 * WIN, PAIR), lambda j, c: (0, j))
    full = pl.BlockSpec((count, PAIR), lambda j, c: (0, j))
    half = pl.BlockSpec((width // 2, PAIR), lambda j, c: (0, j))
    grad = jax.ShapeDtypeStruct((count, width), BF16)
    sums = jax.ShapeDtypeStruct((width // 2, width), BF16)
    return pl.pallas_call(
        last_kernel,
        grid_spec=pltpu.PrefetchScalarGridSpec(
            num_scalar_prefetch=1,
            grid=(width // PAIR,),
            in_specs=[near, near, column, column, column, row] + [rim] * 6 + [mid, mid] + token_specs(count),
            out_specs=[full, full, half, half, half, half],
            scratch_shapes=[pltpu.VMEM((width, count), BF16)],
        ),
        out_shape=[grad, grad, sums, sums, sums, sums],
        compiler_params=pltpu.CompilerParams(vmem_limit_bytes=VMEM),
        cost_estimate=SMALL,
        name="last_block",
    )(core, tokens_n, grads_n, *weights, *last, *partial, *first, *middle, *[tokens] * 4)


def chip_sum(sends, keeps):
    got = [lax.ppermute(send, "co", [(0, 1), (1, 0)]) for send in sends]
    both = [keep.astype(F32) + extra.astype(F32) for keep, extra in zip(keeps, got)]
    return bf(jnp.concatenate(both, axis=1))


def passed_along(block, distance):
    size = 1
    for axis in SEQ:
        size *= lax.axis_size(axis)
    route = [(i - distance, i) for i in range(size) if 0 <= i - distance < size]
    return lax.ppermute(block, SEQ, route)


def on_device(tokens, out_grad, w_query, w_key, w_value, w_output, grad_accum):
    tokens = tokens[0]
    out_grad = out_grad[0]
    count, width = tokens.shape
    core = lax.axis_index("co")
    which = core.reshape(1)
    first = (lax.axis_index("y") + lax.axis_index("z") + lax.axis_index("xl")) == 0
    bias = jnp.where(first, NEG, 0.0).astype(F32).reshape(1)
    tokens_l = passed_along(tokens[count - WIN :], 1)
    weights = (w_query, w_key, w_value, w_output)
    head_x, head_g, *rest = front(tokens, out_grad, *weights)
    own, last, late, middle, partial_0, partial_z = rest[:4], rest[4:6], rest[6:8], rest[8:10], rest[10:12], rest[12:]
    tokens_n = passed_along(head_x, -1)
    grads_n = passed_along(head_g, -1)
    query_grad, key_0, value_0, send_q, keep_q, send_o, keep_o = first_block(
        which, bias, own, partial_0, late, out_grad, tokens_l, w_key, w_value, tokens
    )
    send_q, send_o, tokens_n = lax.optimization_barrier((send_q, send_o, tokens_n))
    both = chip_sum((send_q, send_o), (keep_q, keep_o))
    pieces_qo = lax.all_to_all(both, CHIPS, 0, 0, tiled=True)
    tokens_n, _ = lax.optimization_barrier((tokens_n, both))
    key_grad, value_grad, send_k, keep_k, send_v, keep_v = last_block(
        which, tokens_n, grads_n, weights, last, partial_z, (key_0, value_0), middle, tokens
    )
    both = chip_sum((send_k, send_v), (keep_k, keep_v))
    pieces_kv = lax.all_to_all(both, CHIPS, 0, 0, tiled=True)
    in_grad = bf(
        dot(query_grad, w_query, 1, 1) + dot(key_grad, w_key, 1, 1) + dot(value_grad, w_value, 1, 1)
    )
    sum_qo, sum_kv = [
        jnp.sum(pieces.reshape(-1, 8, 2 * width).astype(F32), axis=0) for pieces in (pieces_qo, pieces_kv)
    ]
    total = count
    for axis in AXES:
        total *= lax.axis_size(axis)
    factor = 1.0 / total**0.5
    summed = jnp.concatenate([sum_qo[:, :width], sum_kv, sum_qo[:, width:]], axis=1)
    return in_grad[None], grad_accum + summed * factor


def solution(mesh):
    fine = Mesh(mesh.devices.reshape(2, 2, 4, 4, 2), AXES)
    rows = P(("xh", "co"), SEQ, None)
    accum = P(AXES, None)
    return jax.shard_map(
        on_device,
        mesh=fine,
        in_specs=(rows, rows, P(), P(), P(), P(), accum),
        out_specs=(rows, accum),
        check_vma=False,
    )
```

time: 140 us -> 140 us (level)
  Pallas kernels: 56.8 us -> 59.1 us
  waiting for transfers between devices: 27.2 us -> 25.3 us
    pallas_call x3, Pallas kernels: 56.8 us -> 59.1 us  [the longest x1 25.7 us: front(): pl.pallas_call(front_kernel, grid=(width // PAIR,), in_specs=[whole, whol...]
    unnamed x22 -> x24, local copies, waits for them, and re-layouts: 0.05 us -> 1.62 us
  transfers between devices with their start and end apart: 9 -> 9, of which waited for: 4 -> 4; matrix products, arithmetic and copies ran while one was open for 13% -> 14% of each run, Pallas kernels for 41% -> 42%
where the time goes in v3:
time: 140 us; the launch traced here: 139 us
  Pallas kernels  59.1 us (42%)
  starting transfers between devices  29.4 us (21%)
  waiting for transfers between devices  25.3 us (18%)
  other arithmetic  11.6 us (8%)
  matrix products  10.2 us (7%)
  local copies, waits for them, and re-layouts  2.7 us (2%)
    pallas_call x1, Pallas kernels, front(): pl.pallas_call(front_kernel, grid=(width // PAIR,), in_specs=[whole, whol...  25.7 us
    pallas_call x1, Pallas kernels, first_block(): pl.pallas_call(first_kernel, grid_spec=pltpu.PrefetchScalarGridSpec(num_s...  17 us
    all_to_all x1, waiting for transfers between devices, on_device(): pieces_kv = lax.all_to_all(both, CHIPS, 0, 0, tiled=True)  16.8 us
    pallas_call x1, Pallas kernels, last_block(): pl.pallas_call(last_kernel, grid_spec=pltpu.PrefetchScalarGridSpec(num_sc...  16.3 us
    all_to_all x1, starting transfers between devices, on_device(): pieces_qo = lax.all_to_all(both, CHIPS, 0, 0, tiled=True)  14 us
    dot_general x3, matrix products, dot(): lax.dot_general(a, b, (((ca,), (cb,)), ((), ())), preferred_element_type=...  10.2 us
    all_to_all x1, starting transfers between devices, on_device(): pieces_kv = lax.all_to_all(both, CHIPS, 0, 0, tiled=True)  8.11 us
    concatenate x6, other arithmetic, chip_sum(): return bf(jnp.concatenate(both, axis=1))  7.11 us
  transfers between devices with their start and end apart: 9, of which 4 were waited for; matrix products, arithmetic and copies ran while one was open for 14% of the time, Pallas kernels for 42%

profile of v3, /device:TPU:0, one launch (start us, length us, event | category | flops | bytes accessed | tf_op | source)
XLA Modules:
  0.0 139.2 jit_solution(8562591424928264535)
XLA Ops:
  0.6 1.1 slice_bitcast_fusion
  1.7 3.5 %collective-permute-start = (bf16[256,1024]{1,0:T(8,128)(2,1)S(1)}, bf16[256,1024]{1,0:T(8,128)(2,1)S(1)}, u32[]{:S(2)}, u32[]{:S(2)}) collective-permute-start(bf16[256,1024]{1,0:T(8,128)(2,1)S(1)} %slice_bitcast_fusion), channel_id=1, source_target_pairs={{0,1},{1,2},{2,3},{3,4},{4,5},{5,6},{6,7},{7,8},{8,9},{9,10},{10,1... | collective-permute-start | bytes 1572872 | tf_op jit(solution)/shard_map/ppermute | solution.py:345
  5.2 25.7 %front.1 = (bf16[256,1024]{1,0:T(8,128)(2,1)}, bf16[256,1024]{1,0:T(8,128)(2,1)}, bf16[256,1024]{1,0:T(8,128)(2,1)}, bf16[256,1024]{1,0:T(8,128)(2,1)}, bf16[256...) custom-call(bf16[1024,1024]{1,0:T(8,128)(2,1)} %bitcast.22, ...), custom_call_target="tpu_custom_call" | custom-call | flops 100000000 | bytes 100000 | tf_op jit(solution)/shard_map/front/pallas_call | solution.py:186
  31.0 1.3 collective-permute-start.1
  32.3 0.8 copy-done.5
  33.1 17.0 %first_block.1 = (bf16[1024,1024]{1,0:T(8,128)(2,1)}, bf16[256,1024]{1,0:T(8,128)(2,1)}, bf16[256,1024]{1,0:T(8,128)(2,1)}, bf16[512,1024]{1,0:T(8,128)(2,1)}, b...) custom-call(s32[1]{0:T(128)} %bitcast.core_ref, f32[1]{0:T(128)} %bitcast.1.bias_ref, ...), custom_call_target="tpu_custom_call" | custom-call | flops 100000000 | bytes 100000 | tf_op jit(solution)/shard_map/first_block/pallas_call | solution.py:253
  50.2 0.1 collective-permute-start.3
  50.3 0.5 collective-permute-start.4
  50.8 1.3 collective-permute-start.2
  52.1 1.1 collective-permute-done.3
  53.1 1.6 %fusion.1 = bf16[64,8,1024]{2,1,0:T(8,128)(2,1)S(1)} fusion(bf16[512,1024]{1,0:T(8,128)(2,1)S(1)} %collective-permute-done.3, bf16[512,1024]{1,0:T(8,128)(2,1)} %get-tuple-element.58), kind=kLoop, calls=%fused_computation.10 | loop fusion | flops 2097152 | bytes 3145728 | tf_op jit(solution)/shard_map/concatenate | solution.py:337
  54.8 0.4 fusion.2
  55.2 1.5 %pad_maximum_fusion = bf16[64,8,2048]{2,1,0:T(8,128)(2,1)} fusion(bf16[64,8,1024]{2,1,0:T(8,128)(2,1)S(1)} %fusion.2, bf16[64,8,1024]{2,1,0:T(8,128)(2,1)S(1)} %fusion.1), kind=kLoop, calls=%fused_computation.4 | loop fusion | flops 4194304 | bytes 4194304 | tf_op jit(solution)/shard_map/concatenate | solution.py:337
  56.7 14.0 %all-to-all-start = ((bf16[64,8,2048]{2,1,0:T(8,128)(2,1)}), bf16[64,8,2048]{2,1,0:T(8,128)(2,1)}, u32[]{:S(2)}, u32[]{:S(2)}) async-start(bf16[64,8,2048]{2,1,0:T(8,128)(2,1)} %pad_maximum_fusion), calls=%async_computation | async-start | bytes 4194304 | tf_op jit(solution)/shard_map/all_to_all | solution.py:367
  70.7 0.8 copy-done.7
  71.5 16.3 %last_block.1 = (bf16[1024,1024]{1,0:T(8,128)(2,1)}, bf16[1024,1024]{1,0:T(8,128)(2,1)}, bf16[512,1024]{1,0:T(8,128)(2,1)}, bf16[512,1024]{1,0:T(8,128)(2,1)}, b...) custom-call(s32[1]{0:T(128)} %bitcast.core_ref, bf16[256,1024]{1,0:T(8,128)(2,1)} %copy-done.6, ...), custom_call_target="tpu_custom_call" | custom-call | flops 100000000 | bytes 100000 | tf_op jit(solution)/shard_map/last_block/pallas_call | solution.py:318
  87.8 0.1 collective-permute-start.5
  87.9 0.5 collective-permute-start.6
  88.4 2.4 %collective-permute-done.5 = bf16[512,1024]{1,0:T(8,128)(2,1)S(1)} collective-permute-done((bf16[512,1024]{1,0:T(8,128)(2,1)}, bf16[512,1024]{1,0:T(8,128)(2,1)S(1)}, u32[]{:S(2)}, u32[]{:S(2)}) %collective-permute-start.5) | collective-permute-done | bytes 1048608 | tf_op jit(solution)/shard_map/ppermute | solution.py:335
  90.7 1.6 %fusion.3 = bf16[64,8,1024]{2,1,0:T(8,128)(2,1)S(1)} fusion(bf16[512,1024]{1,0:T(8,128)(2,1)S(1)} %collective-permute-done.5, bf16[512,1024]{1,0:T(8,128)(2,1)} %get-tuple-element.62), kind=kLoop, calls=%fused_computation.12 | loop fusion | flops 2097152 | bytes 3145728 | tf_op jit(solution)/shard_map/concatenate | solution.py:337
  92.4 0.4 fusion.4
  92.8 1.6 %pad_maximum_fusion.1 = bf16[64,8,2048]{2,1,0:T(8,128)(2,1)} fusion(bf16[64,8,1024]{2,1,0:T(8,128)(2,1)S(1)} %fusion.4, bf16[64,8,1024]{2,1,0:T(8,128)(2,1)S(1)} %fusion.3), kind=kLoop, calls=%fused_computation.5 | loop fusion | flops 4194304 | bytes 4194304 | tf_op jit(solution)/shard_map/concatenate | solution.py:337
  94.4 5.1 %all-to-all-done = bf16[64,8,2048]{2,1,0:T(8,128)(2,1)} async-done(((bf16[64,8,2048]{2,1,0:T(8,128)(2,1)}), bf16[64,8,2048]{2,1,0:T(8,128)(2,1)}, u32[]{:S(2)}, u32[]{:S(2)}) %all-to-all-start) | async-done | bytes 2097184 | tf_op jit(solution)/shard_map/all_to_all | solution.py:367
  99.4 8.1 %all-to-all-start.1 = ((bf16[64,8,2048]{2,1,0:T(8,128)(2,1)}), bf16[64,8,2048]{2,1,0:T(8,128)(2,1)}, u32[]{:S(2)}, u32[]{:S(2)}) async-start(bf16[64,8,2048]{2,1,0:T(8,128)(2,1)} %pad_maximum_fusion.1), calls=%async_computation.1 | async-start | bytes 4194304 | tf_op jit(solution)/shard_map/all_to_all | solution.py:373
  107.6 0.0 copy-start.9
  107.6 4.1 %fusion.8 = f32[1024,1024]{1,0:T(8,128)S(1)} fusion(bf16[1024,1024]{1,0:T(8,128)(2,1)} %get-tuple-element.56, bf16[1024,1024]{1,0:T(8,128)(2,1)S(1)} %copy-done), kind=kOutput, calls=%fused_computation.19 | convolution fusion | flops 2147483648 | bytes 8388608 | tf_op jit(solution)/shard_map/dot_general | solution.py:21
  111.8 2.4 %fusion.7 = f32[1024,1024]{1,0:T(8,128)S(1)} fusion(bf16[1024,1024]{1,0:T(8,128)(2,1)S(1)} %copy-done.9, bf16[1024,1024]{1,0:T(8,128)(2,1)S(1)} %copy-done.2), kind=kOutput, calls=%fused_computation.18 | convolution fusion | flops 2147483648 | bytes 8388608 | tf_op jit(solution)/shard_map/dot_general | solution.py:21
  114.2 3.7 %fusion = bf16[1,1024,1024]{2,1,0:T(8,128)(2,1)} fusion(f32[1024,1024]{1,0:T(8,128)S(1)} %fusion.7, f32[1024,1024]{1,0:T(8,128)S(1)} %fusion.8, bf16[1024,1024]{1,0:T(8,128)(2,1)S(1)} %copy-done.10, bf16[1024,1024]{1,0:T(8,128)(2,1)S(1)} %copy-done.1), kind=kOutput, calls=%fused_computation.3 | convolution fusion | flops 2150629376 | bytes 14680064 | tf_op jit(solution)/shard_map/dot_general | solution.py:21
  117.9 1.9 %convert_reduce_fusion.1 = f32[8,2048]{1,0:T(8,128)S(1)} fusion(bf16[64,8,2048]{2,1,0:T(8,128)(2,1)} %all-to-all-done), kind=kLoop, calls=%fused_computation.1 | loop fusion | flops 2080768 | bytes 2162688 | tf_op jit(solution)/shard_map/reduce_sum | solution.py:378
  119.8 16.8 %all-to-all-done.1 = bf16[64,8,2048]{2,1,0:T(8,128)(2,1)} async-done(((bf16[64,8,2048]{2,1,0:T(8,128)(2,1)}), bf16[64,8,2048]{2,1,0:T(8,128)(2,1)}, u32[]{:S(2)}, u32[]{:S(2)}) %all-to-all-start.1) | async-done | bytes 2097184 | tf_op jit(solution)/shard_map/all_to_all | solution.py:373
  136.6 1.9 %convert_reduce_fusion = f32[8,2048]{1,0:T(8,128)S(1)} fusion(bf16[64,8,2048]{2,1,0:T(8,128)(2,1)} %all-to-all-done.1), kind=kLoop, calls=%fused_computation | loop fusion | flops 2080768 | bytes 2162688 | tf_op jit(solution)/shard_map/reduce_sum | solution.py:378
  138.5 0.7 fusion.5
  (27 shorter events, 0.1 us)
Async XLA Ops:
  1.7 30.6 %collective-permute-start = (bf16[256,1024]{1,0:T(8,128)(2,1)S(1)}, bf16[256,1024]{1,0:T(8,128)(2,1)S(1)}, u32[]{:S(2)}, u32[]{:S(2)}) collective-permute-start(bf16[256,1024]{1,0:T(8,128)(2,1)S(1)} %slice_bitcast_fusion), channel_id=1, source_target_pairs={{0,1},{1,2},{2,3},{3,4},{4,5},{5,6},{6,7},{7,8},{8,9},{9,10},{10,1... | collective-permute-start | bytes 1572872 | tf_op jit(solution)/shard_map/ppermute | solution.py:345
  31.0 19.2 %collective-permute-start.1 = (bf16[256,1024]{1,0:T(8,128)(2,1)}, bf16[256,1024]{1,0:T(8,128)(2,1)S(1)}, u32[]{:S(2)}, u32[]{:S(2)}) collective-permute-start(bf16[256,1024]{1,0:T(8,128)(2,1)} %get-tuple-element.45), channel_id=1, source_target_pairs={{1,0},{2,1},{3,2},{4,3},{5,4},{6,5},{7,6},{8,7},{9,8},{10,9},{11,1... | collective-permute-start | bytes 1572872 | tf_op jit(solution)/shard_map/ppermute | solution.py:345
  32.3 0.8 copy-start.5
  33.1 17.7 %copy-start.11 = (bf16[256,1024]{1,0:T(8,128)(2,1)S(1)}, bf16[256,1024]{1,0:T(8,128)(2,1)}, u32[]{:S(2)}) copy-start(bf16[256,1024]{1,0:T(8,128)(2,1)} %get-tuple-element.47) | copy-start | bytes 1572868
  50.1 4.6 %copy-start.3 = (bf16[512,1024]{1,0:T(8,128)(2,1)S(1)}, bf16[512,1024]{1,0:T(8,128)(2,1)}, u32[]{:S(2)}) copy-start(bf16[512,1024]{1,0:T(8,128)(2,1)} %get-tuple-element.60) | copy-start | bytes 3145732
  50.2 5.0 %copy-start.6 = (bf16[256,1024]{1,0:T(8,128)(2,1)}, bf16[256,1024]{1,0:T(8,128)(2,1)S(1)}, u32[]{:S(2)}) copy-start(bf16[256,1024]{1,0:T(8,128)(2,1)S(1)} %collective-permute-done.1.xn_ref) | copy-start | bytes 1572868
  50.2 3.0 %collective-permute-start.3 = (bf16[512,1024]{1,0:T(8,128)(2,1)}, bf16[512,1024]{1,0:T(8,128)(2,1)S(1)}, u32[]{:S(2)}, u32[]{:S(2)}) collective-permute-start(bf16[512,1024]{1,0:T(8,128)(2,1)} %get-tuple-element.59), channel_id=1, source_target_pairs={{0,32},{32,0},{1,33},{33,1},{2,34},{34,2},{3,35},{35,3},{4,36},{36... | collective-permute-start | bytes 3145736 | tf_op jit(solution)/shard_map/ppermute | solution.py:335
  50.3 4.5 %collective-permute-start.4 = (bf16[512,1024]{1,0:T(8,128)(2,1)}, bf16[512,1024]{1,0:T(8,128)(2,1)S(1)}, u32[]{:S(2)}, u32[]{:S(2)}) collective-permute-start(bf16[512,1024]{1,0:T(8,128)(2,1)} %get-tuple-element.61), channel_id=1, source_target_pairs={{0,32},{32,0},{1,33},{33,1},{2,34},{34,2},{3,35},{35,3},{4,36},{36... | collective-permute-start | bytes 3145736 | tf_op jit(solution)/shard_map/ppermute | solution.py:335
  50.8 19.9 %collective-permute-start.2 = (bf16[256,1024]{1,0:T(8,128)(2,1)S(1)}, bf16[256,1024]{1,0:T(8,128)(2,1)S(1)}, u32[]{:S(2)}, u32[]{:S(2)}) collective-permute-start(bf16[256,1024]{1,0:T(8,128)(2,1)S(1)} %copy-done.11), channel_id=1, source_target_pairs={{1,0},{2,1},{3,2},{4,3},{5,4},{6,5},{7,6},{8,7},{9,8},{10,9},{11,1... | collective-permute-start | bytes 1572872 | tf_op jit(solution)/shard_map/ppermute | solution.py:345
  56.7 42.8 %all-to-all-start = ((bf16[64,8,2048]{2,1,0:T(8,128)(2,1)}), bf16[64,8,2048]{2,1,0:T(8,128)(2,1)}, u32[]{:S(2)}, u32[]{:S(2)}) async-start(bf16[64,8,2048]{2,1,0:T(8,128)(2,1)} %pad_maximum_fusion), calls=%async_computation | async-start | bytes 4194304 | tf_op jit(solution)/shard_map/all_to_all | solution.py:367
  70.7 0.8 copy-start.7
  87.8 4.6 %copy-start.4 = (bf16[512,1024]{1,0:T(8,128)(2,1)S(1)}, bf16[512,1024]{1,0:T(8,128)(2,1)}, u32[]{:S(2)}) copy-start(bf16[512,1024]{1,0:T(8,128)(2,1)} %get-tuple-element.64) | copy-start | bytes 3145732
  87.8 3.0 %collective-permute-start.5 = (bf16[512,1024]{1,0:T(8,128)(2,1)}, bf16[512,1024]{1,0:T(8,128)(2,1)S(1)}, u32[]{:S(2)}, u32[]{:S(2)}) collective-permute-start(bf16[512,1024]{1,0:T(8,128)(2,1)} %get-tuple-element.63), channel_id=1, source_target_pairs={{0,32},{32,0},{1,33},{33,1},{2,34},{34,2},{3,35},{35,3},{4,36},{36... | collective-permute-start | bytes 3145736 | tf_op jit(solution)/shard_map/ppermute | solution.py:335
  87.9 4.5 %collective-permute-start.6 = (bf16[512,1024]{1,0:T(8,128)(2,1)}, bf16[512,1024]{1,0:T(8,128)(2,1)S(1)}, u32[]{:S(2)}, u32[]{:S(2)}) collective-permute-start(bf16[512,1024]{1,0:T(8,128)(2,1)} %get-tuple-element.65), channel_id=1, source_target_pairs={{0,32},{32,0},{1,33},{33,1},{2,34},{34,2},{3,35},{35,3},{4,36},{36... | collective-permute-start | bytes 3145736 | tf_op jit(solution)/shard_map/ppermute | solution.py:335
  94.4 13.2 %copy-start = (bf16[1024,1024]{1,0:T(8,128)(2,1)S(1)}, bf16[1024,1024]{1,0:T(8,128)(2,1)}, u32[]{:S(2)}) copy-start(bf16[1024,1024]{1,0:T(8,128)(2,1)} %wk_ref.5) | copy-start | bytes 6291460
  99.4 37.1 %all-to-all-start.1 = ((bf16[64,8,2048]{2,1,0:T(8,128)(2,1)}), bf16[64,8,2048]{2,1,0:T(8,128)(2,1)}, u32[]{:S(2)}, u32[]{:S(2)}) async-start(bf16[64,8,2048]{2,1,0:T(8,128)(2,1)} %pad_maximum_fusion.1), calls=%async_computation.1 | async-start | bytes 4194304 | tf_op jit(solution)/shard_map/all_to_all | solution.py:373
  107.6 4.1 %copy-start.2 = (bf16[1024,1024]{1,0:T(8,128)(2,1)S(1)}, bf16[1024,1024]{1,0:T(8,128)(2,1)}, u32[]{:S(2)}) copy-start(bf16[1024,1024]{1,0:T(8,128)(2,1)} %wq_ref.3) | copy-start | bytes 6291460
  107.6 4.1 %copy-start.9 = (bf16[1024,1024]{1,0:T(8,128)(2,1)S(1)}, bf16[1024,1024]{1,0:T(8,128)(2,1)}, u32[]{:S(2)}) copy-start(bf16[1024,1024]{1,0:T(8,128)(2,1)} %get-tuple-element.42) | copy-start | bytes 6291460
  111.7 2.4 %copy-start.1 = (bf16[1024,1024]{1,0:T(8,128)(2,1)S(1)}, bf16[1024,1024]{1,0:T(8,128)(2,1)}, u32[]{:S(2)}) copy-start(bf16[1024,1024]{1,0:T(8,128)(2,1)} %wv_ref.5) | copy-start | bytes 6291460
  111.7 2.4 %copy-start.10 = (bf16[1024,1024]{1,0:T(8,128)(2,1)S(1)}, bf16[1024,1024]{1,0:T(8,128)(2,1)}, u32[]{:S(2)}) copy-start(bf16[1024,1024]{1,0:T(8,128)(2,1)} %get-tuple-element.57) | copy-start | bytes 6291460
  117.9 20.6 %copy-start.8 = (f32[8,4096]{1,0:T(8,128)S(1)}, f32[8,4096]{1,0:T(8,128)}, u32[]{:S(2)}) copy-start(f32[8,4096]{1,0:T(8,128)} %param.13) | copy-start | bytes 393220

commit v4 on v3

--- a/solution.py
+++ b/solution.py
@@ -93,18 +93,21 @@
     return left, right
 
 
-def keep_transposed(parts, turned_ref):
-    @pl.when(pl.program_id(0) == 0)
-    def _():
-        for i, part in enumerate(parts):
-            turned_ref[i * part.shape[1] : (i + 1) * part.shape[1], :] = part[...].T
-
-
-def token_specs(count):
+def turned_specs(width, count):
     def pick(half, other):
-        return pl.BlockSpec((count, PAIR), lambda j, c: (0, 2 * half + (1 - c[0] if other else c[0])))
+        return pl.BlockSpec((width // 4, count), lambda j, c: (2 * half + (1 - c[0] if other else c[0]), 0))
 
     return [pick(0, True), pick(1, True), pick(0, False), pick(1, False)]
+
+
+def store_product(turned, right, send_refs, keep_ref, start):
+    product = bf(dot(jnp.concatenate([part[...] for part in turned], axis=0), right, 1, 0))
+    half = product.shape[0] // 2
+    columns = pl.ds(pl.multiple_of(start, PAIR), PAIR)
+    quarter = half // 2
+    for i, send_ref in enumerate(send_refs):
+        send_ref[:, columns] = product[i * quarter : (i + 1) * quarter]
+    keep_ref[:, columns] = product[half:]
 
 
 def lanes():
@@ -112,15 +115,11 @@
 
 
 def front_kernel(
-    x_ref, g_ref, wq_ref, wk_ref, wv_ref, wo_ref,
-    xh_ref, gh_ref, q0_ref, k0_ref, v0_ref, a0_ref, kz_ref, vz_ref, att_ref, dq_ref, dk_ref, dv_ref,
+    x_ref, g_ref, wq_ref, wk_ref, wv_ref, wo_ref, part_ref,
+    turned_ref, q0_ref, k0_ref, v0_ref, a0_ref, kz_ref, vz_ref, att_ref, dq_ref, dk_ref, dv_ref,
     pk0_ref, pv0_ref, pkz_ref, pvz_ref, q_ref, k_ref, v_ref, a_ref,
 ):
-    @pl.when(pl.program_id(0) == 0)
-    def _():
-        xh_ref[...] = x_ref[:WIN, :]
-        gh_ref[...] = g_ref[:WIN, :]
-
+    turned_ref[...] = part_ref[...].T
     upper = upper_triangle()
     count = x_ref.shape[0]
     blocks = count // WIN
@@ -186,21 +185,29 @@
     return pl.pallas_call(
         front_kernel,
         grid=(width // PAIR,),
-        in_specs=[whole, whole, column, column, column, row],
-        out_specs=[pl.BlockSpec((WIN, width), lambda j: (0, 0))] * 2 + [out(h) for h in heights] + [out(rim)] * 4,
-        out_shape=[like(WIN)] * 2 + [like(h) for h in heights] + [like(rim, F32)] * 4,
+        in_specs=[whole, whole, column, column, column, row, out(count)],
+        out_specs=[row] + [out(h) for h in heights] + [out(rim)] * 4,
+        out_shape=[like(width)] + [like(h) for h in heights] + [like(rim, F32)] * 4,
         scratch_shapes=[pltpu.VMEM((count, PAIR), BF16)] * 4,
         compiler_params=pltpu.CompilerParams(vmem_limit_bytes=VMEM),
         cost_estimate=SMALL,
         name="front",
-    )(tokens, out_grad, w_query, w_key, w_value, w_output)
+    )(tokens, out_grad, w_query, w_key, w_value, w_output, tokens)
 
 
 def first_kernel(
-    core_ref, bias_ref, q_ref, k_ref, v_ref, a_ref, pk_ref, pv_ref, att_in, dq_in, g_ref, xl_ref, wk_ref, wv_ref,
-    x0, x1, x2, x3, dq_ref, dk_ref, dv_ref, sq_ref, kq_ref, so_ref, ko_ref, turned_ref, att_ref,
+    core_ref, bias_ref, q_ref, k_ref, v_ref, a_ref, pk_ref, pv_ref, att_in, dq_in, xl_ref, wk_ref, wv_ref,
+    x0, x1, x2, x3, g_hbm, dq_ref, dk_ref, dv_ref, sa_ref, sb_ref, keep_ref, att_ref, g_ref, g_sem,
 ):
-    keep_transposed((x0, x1, x2, x3), turned_ref)
+    step = pl.program_id(0)
+    fetch = pltpu.make_async_copy(g_hbm, g_ref, g_sem)
+
+    @pl.when(step == 0)
+    def _():
+        fetch.start()
+
+    side = lax.rem(step, 2)
+    att = att_ref.at[side]
     upper = upper_triangle()
     keys_l = bf(dot(xl_ref[...], wk_ref[...], 1, 0))
     values_l = bf(dot(xl_ref[...], wv_ref[...], 1, 0))
@@ -212,9 +219,9 @@
     deltas = []
     for i, c in enumerate(lanes()):
         attended, delta = delta_of(block[i], weights[i])
-        att_ref[:WIN, c] = attended
+        att[:WIN, c] = attended
         deltas.append(delta)
-    att_ref[WIN:, :] = att_in[...]
+    att[WIN:, :] = att_in[...]
     dq_ref[WIN:, :] = dq_in[...]
     for i, c in enumerate(lanes()):
         query, grad, key_l, _, key_r, _ = block[i]
@@ -222,33 +229,42 @@
         dq_ref[:WIN, c] = bf((dot(ds_l, key_l, 1, 0) + dot(ds_r, key_r, 1, 0)) * SCALE)
         dk_ref[:, c] = bf((pk_ref[:, c] + dot(ds_r, query, 0, 0)) * SCALE)
         dv_ref[:, c] = bf(pv_ref[:, c] + dot(weights[i][2], grad, 0, 0))
-    part = dot(turned_ref[...], dq_ref[...], 1, 0)
-    half = part.shape[0] // 2
-    sq_ref[...] = bf(part[:half])
-    kq_ref[...] = bf(part[half:])
-    part = bf(dot(att_ref[...], g_ref[...], 0, 0))
-    own = lax.rem(pl.program_id(0), 2) == core_ref[0]
-
-    @pl.when(own)
+    store_product((x0, x1, x2, x3), dq_ref[...], (sa_ref, sb_ref), keep_ref, step * PAIR)
+
+    @pl.when(step == 1)
     def _():
-        ko_ref[...] = part
-
-    @pl.when(jnp.logical_not(own))
+        fetch.wait()
+
+    @pl.when(side == 1)
     def _():
-        so_ref[...] = part
-
-
-def first_block(core, bias, own, partial, late, out_grad, tokens_l, w_key, w_value, tokens):
-    count, width = tokens.shape
+        width = g_ref.shape[1]
+        product = bf(dot(jnp.concatenate([att_ref[0], att_ref[1]], axis=1), g_ref[...], 0, 0))
+        rows = pl.ds(pl.multiple_of((step // 2) * PAIR, PAIR), PAIR)
+
+        mine = core_ref[0] == 0
+        keep_ref[rows, width:] = jnp.where(mine, product[:PAIR], product[PAIR:])
+        other = jnp.where(mine, product[PAIR:], product[:PAIR])
+
+        @pl.when(step == 1)
+        def _():
+            sa_ref[:, width:] = other
+
+        @pl.when(step == 3)
+        def _():
+            sb_ref[:, width:] = other
+
+
+def first_block(core, bias, own, partial, late, out_grad, tokens_l, w_key, w_value, turned):
+    width, count = turned.shape
     rim = pl.BlockSpec((WIN, PAIR), lambda j, c: (0, j))
     rest = pl.BlockSpec((count - WIN, PAIR), lambda j, c: (0, j))
     full = pl.BlockSpec((count, PAIR), lambda j, c: (0, j))
     left = pl.BlockSpec((WIN, width), lambda j, c: (0, 0))
-    whole = pl.BlockSpec((count, width), lambda j, c: (0, 0))
     column = pl.BlockSpec((width, PAIR), lambda j, c: (0, j))
-    half = pl.BlockSpec((width // 2, PAIR), lambda j, c: (0, j))
-    band = pl.BlockSpec((PAIR, width), lambda j, c: (j // 2, 0))
-    sums = jax.ShapeDtypeStruct((width // 2, width), BF16)
+    sums = pl.BlockSpec((width // 2, 2 * width), lambda j, c: (0, 0))
+    both = jax.ShapeDtypeStruct((width // 2, 2 * width), BF16)
+    half = pl.BlockSpec((width // 4, 2 * width), lambda j, c: (0, 0))
+    part_sum = jax.ShapeDtypeStruct((width // 4, 2 * width), BF16)
     part = jax.ShapeDtypeStruct((WIN, width), BF16)
     return pl.pallas_call(
         first_kernel,
@@ -257,23 +273,27 @@
             grid=(width // PAIR,),
             in_specs=[pl.BlockSpec(memory_space=pltpu.SMEM)]
             + [rim] * 6
-            + [rest, rest, whole, left, column, column]
-            + token_specs(count),
-            out_specs=[full, rim, rim, half, half, band, band],
-            scratch_shapes=[pltpu.VMEM((width, count), BF16), pltpu.VMEM((count, PAIR), BF16)],
+            + [rest, rest, left, column, column]
+            + turned_specs(width, count)
+            + [pl.BlockSpec(memory_space=pl.ANY)],
+            out_specs=[full, rim, rim, half, half, sums],
+            scratch_shapes=[
+                pltpu.VMEM((2, count, PAIR), BF16),
+                pltpu.VMEM((count, width), BF16),
+                pltpu.SemaphoreType.DMA,
+            ],
         ),
-        out_shape=[jax.ShapeDtypeStruct((count, width), BF16), part, part, sums, sums, sums, sums],
+        out_shape=[jax.ShapeDtypeStruct((count, width), BF16), part, part, part_sum, part_sum, both],
         compiler_params=pltpu.CompilerParams(vmem_limit_bytes=VMEM),
         cost_estimate=SMALL,
         name="first_block",
-    )(core, bias, *own, *partial, *late, out_grad, tokens_l, w_key, w_value, *[tokens] * 4)
+    )(core, bias, *own, *partial, *late, tokens_l, w_key, w_value, *[turned] * 4, out_grad)
 
 
 def last_kernel(
     core_ref, xn_ref, gn_ref, wq_ref, wk_ref, wv_ref, wo_ref, k_ref, v_ref, pk_ref, pv_ref, dk0_ref, dv0_ref,
-    dkm_ref, dvm_ref, x0, x1, x2, x3, dk_ref, dv_ref, sk_ref, kk_ref, sv_ref, kv_ref, turned_ref,
+    dkm_ref, dvm_ref, x0, x1, x2, x3, dk_ref, dv_ref, sa_ref, sb_ref, keep_ref,
 ):
-    keep_transposed((x0, x1, x2, x3), turned_ref)
     upper = upper_triangle()
     tokens = xn_ref[...]
     queries = bf(dot(tokens, wq_ref[...], 1, 0))
@@ -295,46 +315,42 @@
         ds_l = score_grads(scores[i], weights[i], deltas[i])[0]
         dk_ref[end:, c] = bf((pk_ref[:, c] + dot(ds_l, block[i][0], 0, 0)) * SCALE)
         dv_ref[end:, c] = bf(pv_ref[:, c] + dot(weights[i][1], block[i][1], 0, 0))
-    half = turned_ref.shape[0] // 2
-    part = dot(turned_ref[...], dk_ref[...], 1, 0)
-    sk_ref[...] = bf(part[:half])
-    kk_ref[...] = bf(part[half:])
-    part = dot(turned_ref[...], dv_ref[...], 1, 0)
-    sv_ref[...] = bf(part[:half])
-    kv_ref[...] = bf(part[half:])
-
-
-def last_block(core, tokens_n, grads_n, weights, last, partial, first, middle, tokens):
-    count, width = tokens.shape
+    start = pl.program_id(0) * PAIR
+    store_product((x0, x1, x2, x3), dk_ref[...], (sa_ref, sb_ref), keep_ref, start)
+    store_product((x0, x1, x2, x3), dv_ref[...], (sa_ref, sb_ref), keep_ref, start + keep_ref.shape[1] // 2)
+
+
+def last_block(core, tokens_n, grads_n, weights, last, partial, first, middle, turned):
+    width, count = turned.shape
     column = pl.BlockSpec((width, PAIR), lambda j, c: (0, j))
     row = pl.BlockSpec((PAIR, width), lambda j, c: (j, 0))
     rim = pl.BlockSpec((WIN, PAIR), lambda j, c: (0, j))
     near = pl.BlockSpec((WIN, width), lambda j, c: (0, 0))
     mid = pl.BlockSpec((count - 2 * WIN, PAIR), lambda j, c: (0, j))
     full = pl.BlockSpec((count, PAIR), lambda j, c: (0, j))
-    half = pl.BlockSpec((width // 2, PAIR), lambda j, c: (0, j))
+    sums = pl.BlockSpec((width // 2, 2 * width), lambda j, c: (0, 0))
     grad = jax.ShapeDtypeStruct((count, width), BF16)
-    sums = jax.ShapeDtypeStruct((width // 2, width), BF16)
+    both = jax.ShapeDtypeStruct((width // 2, 2 * width), BF16)
+    half = pl.BlockSpec((width // 4, 2 * width), lambda j, c: (0, 0))
+    part_sum = jax.ShapeDtypeStruct((width // 4, 2 * width), BF16)
     return pl.pallas_call(
         last_kernel,
         grid_spec=pltpu.PrefetchScalarGridSpec(
             num_scalar_prefetch=1,
             grid=(width // PAIR,),
-            in_specs=[near, near, column, column, column, row] + [rim] * 6 + [mid, mid] + token_specs(count),
-            out_specs=[full, full, half, half, half, half],
-            scratch_shapes=[pltpu.VMEM((width, count), BF16)],
+            in_specs=[near, near, column, column, column, row] + [rim] * 6 + [mid, mid] + turned_specs(width, count),
+            out_specs=[full, full, half, half, sums],
         ),
-        out_shape=[grad, grad, sums, sums, sums, sums],
+        out_shape=[grad, grad, part_sum, part_sum, both],
         compiler_params=pltpu.CompilerParams(vmem_limit_bytes=VMEM),
         cost_estimate=SMALL,
         name="last_block",
-    )(core, tokens_n, grads_n, *weights, *last, *partial, *first, *middle, *[tokens] * 4)
-
-
-def chip_sum(sends, keeps):
+    )(core, tokens_n, grads_n, *weights, *last, *partial, *first, *middle, *[turned] * 4)
+
+
+def chip_sum(sends, keep):
     got = [lax.ppermute(send, "co", [(0, 1), (1, 0)]) for send in sends]
-    both = [keep.astype(F32) + extra.astype(F32) for keep, extra in zip(keeps, got)]
-    return bf(jnp.concatenate(both, axis=1))
+    return bf(keep.astype(F32) + jnp.concatenate(got, axis=0).astype(F32))
 
 
 def passed_along(block, distance):
@@ -354,22 +370,22 @@
     first = (lax.axis_index("y") + lax.axis_index("z") + lax.axis_index("xl")) == 0
     bias = jnp.where(first, NEG, 0.0).astype(F32).reshape(1)
     tokens_l = passed_along(tokens[count - WIN :], 1)
+    tokens_n = passed_along(tokens[:WIN], -1)
+    grads_n = passed_along(out_grad[:WIN], -1)
     weights = (w_query, w_key, w_value, w_output)
-    head_x, head_g, *rest = front(tokens, out_grad, *weights)
+    turned, *rest = front(tokens, out_grad, *weights)
     own, last, late, middle, partial_0, partial_z = rest[:4], rest[4:6], rest[6:8], rest[8:10], rest[10:12], rest[12:]
-    tokens_n = passed_along(head_x, -1)
-    grads_n = passed_along(head_g, -1)
-    query_grad, key_0, value_0, send_q, keep_q, send_o, keep_o = first_block(
-        which, bias, own, partial_0, late, out_grad, tokens_l, w_key, w_value, tokens
-    )
-    send_q, send_o, tokens_n = lax.optimization_barrier((send_q, send_o, tokens_n))
-    both = chip_sum((send_q, send_o), (keep_q, keep_o))
+    query_grad, key_0, value_0, send_a, send_b, keep = first_block(
+        which, bias, own, partial_0, late, out_grad, tokens_l, w_key, w_value, turned
+    )
+    send_a, send_b, tokens_n, grads_n = lax.optimization_barrier((send_a, send_b, tokens_n, grads_n))
+    both = chip_sum((send_a, send_b), keep)
     pieces_qo = lax.all_to_all(both, CHIPS, 0, 0, tiled=True)
     tokens_n, _ = lax.optimization_barrier((tokens_n, both))
-    key_grad, value_grad, send_k, keep_k, send_v, keep_v = last_block(
-        which, tokens_n, grads_n, weights, last, partial_z, (key_0, value_0), middle, tokens
-    )
-    both = chip_sum((send_k, send_v), (keep_k, keep_v))
+    key_grad, value_grad, send_a, send_b, keep = last_block(
+        which, tokens_n, grads_n, weights, last, partial_z, (key_0, value_0), middle, turned
+    )
+    both = chip_sum((send_a, send_b), keep)
     pieces_kv = lax.all_to_all(both, CHIPS, 0, 0, tiled=True)
     in_grad = bf(
         dot(query_grad, w_query, 1, 1) + dot(key_grad, w_key, 1, 1) + dot(value_grad, w_value, 1, 1)

time: 140 us -> 144 us (1.029)
  waiting for transfers between devices: 25.3 us -> 28.9 us
    concatenate x6 -> x0, other arithmetic: 7.11 us -> none  [chip_sum(): return bf(jnp.concatenate(both, axis=1))]
    ppermute x4, waiting for transfers between devices: 3.43 us -> 7.72 us  [chip_sum(): got = [lax.ppermute(send, 'co', [(0, 1), (1, 0)]) for send in sends]]
    all_to_all x0 -> x1, other arithmetic: none -> 3.87 us  [on_device(): pieces_kv = lax.all_to_all(both, CHIPS, 0, 0, tiled=True)]
    convert_element_type x0 -> x1, other arithmetic: none -> 3.86 us  [bf(): return value.astype(BF16)]
    reduce_sum x2, other arithmetic: 3.84 us -> 2.21 us  [on_device(): jnp.sum(pieces.reshape(-1, 8, 2 * width).astype(F32), axis=0)]
  transfers between devices with their start and end apart: 9 -> 9, of which waited for: 4 -> 6; matrix products, arithmetic and copies ran while one was open for 14% -> 11% of each run, Pallas kernels for 42% -> 42%
where the time goes in v4:
time: 144 us
  Pallas kernels  59.8 us (42%)
  starting transfers between devices  29.6 us (21%)
  waiting for transfers between devices  28.9 us (20%)
  matrix products  10.8 us (8%)
  other arithmetic  10.6 us (7%)
  local copies, waits for them, and re-layouts  3.18 us (2%)
    pallas_call x1, Pallas kernels, front(): pl.pallas_call(front_kernel, grid=(width // PAIR,), in_specs=[whole, whol...  26 us
    all_to_all x1, waiting for transfers between devices, on_device(): pieces_kv = lax.all_to_all(both, CHIPS, 0, 0, tiled=True)  17.5 us
    pallas_call x1, Pallas kernels, last_block(): pl.pallas_call(last_kernel, grid_spec=pltpu.PrefetchScalarGridSpec(num_sc...  17 us
    pallas_call x1, Pallas kernels, first_block(): pl.pallas_call(first_kernel, grid_spec=pltpu.PrefetchScalarGridSpec(num_s...  16.8 us
    all_to_all x1, starting transfers between devices, on_device(): pieces_qo = lax.all_to_all(both, CHIPS, 0, 0, tiled=True)  14.8 us
    dot_general x3, matrix products, dot(): lax.dot_general(a, b, (((ca,), (cb,)), ((), ())), preferred_element_type=...  10.8 us
    ppermute x4, waiting for transfers between devices, chip_sum(): got = [lax.ppermute(send, 'co', [(0, 1), (1, 0)]) for send in sends]  7.72 us
    all_to_all x1, starting transfers between devices, on_device(): pieces_kv = lax.all_to_all(both, CHIPS, 0, 0, tiled=True)  7.52 us
  transfers between devices with their start and end apart: 9, of which 6 were waited for; matrix products, arithmetic and copies ran while one was open for 11% of the time, Pallas kernels for 42%

profile of v4, /device:TPU:0, one launch (start us, length us, event | category | flops | bytes accessed | tf_op | source)
XLA Modules:
  0.0 143.7 jit_solution(9132453837234719619)
XLA Ops:
  0.6 1.3 slice_bitcast_fusion.1
  1.9 3.5 %collective-permute-start = (bf16[256,1024]{1,0:T(8,128)(2,1)S(1)}, bf16[256,1024]{1,0:T(8,128)(2,1)S(1)}, u32[]{:S(2)}, u32[]{:S(2)}) collective-permute-start(bf16[256,1024]{1,0:T(8,128)(2,1)S(1)} %get-tuple-element.65), channel_id=1, source_target_pairs={{0,1},{1,2},{2,3},{3,4},{4,5},{5,6},{6,7},{7,8},{8,9},{9,10},{10,1... | collective-permute-start | bytes 1572872 | tf_op jit(solution)/shard_map/ppermute | solution.py:361
  5.4 1.3 collective-permute-start.1
  6.7 1.1 slice_bitcast_fusion
  7.8 1.3 collective-permute-start.2
  9.1 26.0 %front.1 = (bf16[1024,1024]{1,0:T(8,128)(2,1)}, bf16[256,1024]{1,0:T(8,128)(2,1)}, bf16[256,1024]{1,0:T(8,128)(2,1)}, bf16[256,1024]{1,0:T(8,128)(2,1)}, bf16[25...) custom-call(bf16[1024,1024]{1,0:T(8,128)(2,1)} %bitcast.21, ...), custom_call_target="tpu_custom_call" | custom-call | flops 100000000 | bytes 100000 | tf_op jit(solution)/shard_map/front/pallas_call | solution.py:185
  35.1 0.0 collective-permute-done.xl_ref
  35.1 0.8 copy-done.2
  35.9 16.8 %first_block.1 = (bf16[1024,1024]{1,0:T(8,128)(2,1)}, bf16[256,1024]{1,0:T(8,128)(2,1)}, bf16[256,1024]{1,0:T(8,128)(2,1)}, bf16[256,2048]{1,0:T(8,128)(2,1)}, b...) custom-call(s32[1]{0:T(128)} %bitcast.core_ref, f32[1]{0:T(128)} %bitcast.1.bias_ref, ...), custom_call_target="tpu_custom_call" | custom-call | flops 100000000 | bytes 100000 | tf_op jit(solution)/shard_map/first_block/pallas_call | solution.py:269
  52.8 0.1 collective-permute-start.3
  52.9 0.5 collective-permute-start.4
  53.3 2.4 %collective-permute-done.3 = bf16[256,2048]{1,0:T(8,128)(2,1)S(1)} collective-permute-done((bf16[256,2048]{1,0:T(8,128)(2,1)}, bf16[256,2048]{1,0:T(8,128)(2,1)S(1)}, u32[]{:S(2)}, u32[]{:S(2)}) %collective-permute-start.3) | collective-permute-done | bytes 1048608 | tf_op jit(solution)/shard_map/ppermute | solution.py:352
  55.7 1.5 %collective-permute-done.4 = bf16[256,2048]{1,0:T(8,128)(2,1)S(1)} collective-permute-done((bf16[256,2048]{1,0:T(8,128)(2,1)}, bf16[256,2048]{1,0:T(8,128)(2,1)S(1)}, u32[]{:S(2)}, u32[]{:S(2)}) %collective-permute-start.4) | collective-permute-done | bytes 1048608 | tf_op jit(solution)/shard_map/ppermute | solution.py:352
  57.2 3.9 %add_convert_fusion.2 = bf16[512,2048]{1,0:T(8,128)(2,1)} fusion(bf16[512,2048]{1,0:T(8,128)(2,1)} %get-tuple-element.46, bf16[256,2048]{1,0:T(8,128)(2,1)S(1)} %collective-permute-done.4, bf16[256,2048]{1,0:T(8,128)(2,1)S(1)} %collective-permute-done.3), kind=kLoop, calls=%fused_computation.4 | loop fusion | flops 7340032 | bytes 6291456 | tf_op jit(solution)/shard_map/convert_element_type | solution.py:32
  61.1 14.8 %all-to-all-start = ((bf16[64,8,2048]{2,1,0:T(8,128)(2,1)}), bf16[64,8,2048]{2,1,0:T(8,128)(2,1)S(1)}, u32[]{:S(2)}, u32[]{:S(2)}) async-start(bf16[64,8,2048]{2,1,0:T(8,128)(2,1)} %bitcast.8), calls=%async_computation | async-start | bytes 4194304 | tf_op jit(solution)/shard_map/all_to_all | solution.py:383
  75.9 17.0 %last_block.1 = (bf16[1024,1024]{1,0:T(8,128)(2,1)}, bf16[1024,1024]{1,0:T(8,128)(2,1)}, bf16[256,2048]{1,0:T(8,128)(2,1)}, bf16[256,2048]{1,0:T(8,128)(2,1)}, bf16[512,2048]{1,0:T(8,128)(2,1)}) custom-call(s32[1]{0:T(128)} %bitcast.core_ref, bf16[256,1024]{1,0:T(8,128)(2,1)} %copy-done.3, bf16[256,1024]{1,0:T(8,128)(2,1)} %copy-done.4, ...), custom_call_target="tpu_custom_call" | custom-call | flops 100000000 | bytes 100000 | tf_op jit(solution)/shard_map/last_block/pallas_call | solution.py:336
  92.9 0.1 collective-permute-start.5
  93.0 0.5 collective-permute-start.6
  93.5 2.4 %collective-permute-done.5 = bf16[256,2048]{1,0:T(8,128)(2,1)S(1)} collective-permute-done((bf16[256,2048]{1,0:T(8,128)(2,1)}, bf16[256,2048]{1,0:T(8,128)(2,1)S(1)}, u32[]{:S(2)}, u32[]{:S(2)}) %collective-permute-start.5) | collective-permute-done | bytes 1048608 | tf_op jit(solution)/shard_map/ppermute | solution.py:352
  95.8 1.5 %collective-permute-done.6 = bf16[256,2048]{1,0:T(8,128)(2,1)S(1)} collective-permute-done((bf16[256,2048]{1,0:T(8,128)(2,1)}, bf16[256,2048]{1,0:T(8,128)(2,1)S(1)}, u32[]{:S(2)}, u32[]{:S(2)}) %collective-permute-start.6) | collective-permute-done | bytes 1048608 | tf_op jit(solution)/shard_map/ppermute | solution.py:352
  97.3 3.9 %fusion.1 = bf16[64,8,2048]{2,1,0:T(8,128)(2,1)} fusion(bf16[512,2048]{1,0:T(8,128)(2,1)} %get-tuple-element.61, bf16[256,2048]{1,0:T(8,128)(2,1)S(1)} %collective-permute-done.6, bf16[256,2048]{1,0:T(8,128)(2,1)S(1)} %collective-permute-done.5), kind=kLoop, calls=%fused_computation.6 | loop fusion | flops 7340032 | bytes 6291456 | tf_op jit(solution)/shard_map/all_to_all | solution.py:389
  101.2 3.7 %all-to-all-done = bf16[64,8,2048]{2,1,0:T(8,128)(2,1)S(1)} async-done(((bf16[64,8,2048]{2,1,0:T(8,128)(2,1)}), bf16[64,8,2048]{2,1,0:T(8,128)(2,1)S(1)}, u32[]{:S(2)}, u32[]{:S(2)}) %all-to-all-start) | async-done | bytes 2097184 | tf_op jit(solution)/shard_map/all_to_all | solution.py:383
  104.9 7.5 %all-to-all-start.1 = ((bf16[64,8,2048]{2,1,0:T(8,128)(2,1)}), bf16[64,8,2048]{2,1,0:T(8,128)(2,1)}, u32[]{:S(2)}, u32[]{:S(2)}) async-start(bf16[64,8,2048]{2,1,0:T(8,128)(2,1)} %fusion.1), calls=%async_computation.1 | async-start | bytes 4194304 | tf_op jit(solution)/shard_map/all_to_all | solution.py:389
  112.4 0.0 copy-start
  112.4 4.7 %fusion.4 = f32[1024,1024]{1,0:T(8,128)S(1)} fusion(bf16[1024,1024]{1,0:T(8,128)(2,1)} %get-tuple-element.42, bf16[1024,1024]{1,0:T(8,128)(2,1)} %wq_ref.3), kind=kOutput, calls=%fused_computation.13 | convolution fusion | flops 2147483648 | bytes 8388608 | tf_op jit(solution)/shard_map/dot_general | solution.py:21
  117.2 0.0 copy-start.1
  117.2 2.4 %fusion.5 = f32[1024,1024]{1,0:T(8,128)S(1)} fusion(bf16[1024,1024]{1,0:T(8,128)(2,1)S(1)} %copy-done.7, bf16[1024,1024]{1,0:T(8,128)(2,1)S(1)} %copy-done), kind=kOutput, calls=%fused_computation.14 | convolution fusion | flops 2147483648 | bytes 8388608 | tf_op jit(solution)/shard_map/dot_general | solution.py:21
  119.6 3.7 %fusion = bf16[1,1024,1024]{2,1,0:T(8,128)(2,1)} fusion(f32[1024,1024]{1,0:T(8,128)S(1)} %fusion.4, f32[1024,1024]{1,0:T(8,128)S(1)} %fusion.5, bf16[1024,1024]{1,0:T(8,128)(2,1)S(1)} %copy-done.6, bf16[1024,1024]{1,0:T(8,128)(2,1)S(1)} %copy-done.1), kind=kOutput, calls=%fused_computation.5 | convolution fusion | flops 2150629376 | bytes 14680064 | tf_op jit(solution)/shard_map/dot_general | solution.py:21
  123.3 0.3 convert_reduce_fusion.1
  123.6 17.5 %all-to-all-done.1 = bf16[64,8,2048]{2,1,0:T(8,128)(2,1)} async-done(((bf16[64,8,2048]{2,1,0:T(8,128)(2,1)}), bf16[64,8,2048]{2,1,0:T(8,128)(2,1)}, u32[]{:S(2)}, u32[]{:S(2)}) %all-to-all-start.1) | async-done | bytes 2097184 | tf_op jit(solution)/shard_map/all_to_all | solution.py:389
  141.1 1.9 %convert_reduce_fusion = f32[8,2048]{1,0:T(8,128)S(1)} fusion(bf16[64,8,2048]{2,1,0:T(8,128)(2,1)} %all-to-all-done.1), kind=kLoop, calls=%fused_computation | loop fusion | flops 2080768 | bytes 2162688 | tf_op jit(solution)/shard_map/reduce_sum | solution.py:394
  143.0 0.7 fusion.2
  (16 shorter events, 0.0 us)
Async XLA Ops:
  1.9 33.2 %collective-permute-start = (bf16[256,1024]{1,0:T(8,128)(2,1)S(1)}, bf16[256,1024]{1,0:T(8,128)(2,1)S(1)}, u32[]{:S(2)}, u32[]{:S(2)}) collective-permute-start(bf16[256,1024]{1,0:T(8,128)(2,1)S(1)} %get-tuple-element.65), channel_id=1, source_target_pairs={{0,1},{1,2},{2,3},{3,4},{4,5},{5,6},{6,7},{7,8},{8,9},{9,10},{10,1... | collective-permute-start | bytes 1572872 | tf_op jit(solution)/shard_map/ppermute | solution.py:361
  5.4 47.3 %collective-permute-start.1 = (bf16[256,1024]{1,0:T(8,128)(2,1)S(1)}, bf16[256,1024]{1,0:T(8,128)(2,1)S(1)}, u32[]{:S(2)}, u32[]{:S(2)}) collective-permute-start(bf16[256,1024]{1,0:T(8,128)(2,1)S(1)} %get-tuple-element.64), channel_id=1, source_target_pairs={{1,0},{2,1},{3,2},{4,3},{5,4},{6,5},{7,6},{8,7},{9,8},{10,9},{11,1... | collective-permute-start | bytes 1572872 | tf_op jit(solution)/shard_map/ppermute | solution.py:361
  7.8 44.9 %collective-permute-start.2 = (bf16[256,1024]{1,0:T(8,128)(2,1)S(1)}, bf16[256,1024]{1,0:T(8,128)(2,1)S(1)}, u32[]{:S(2)}, u32[]{:S(2)}) collective-permute-start(bf16[256,1024]{1,0:T(8,128)(2,1)S(1)} %slice_bitcast_fusion), channel_id=1, source_target_pairs={{1,0},{2,1},{3,2},{4,3},{5,4},{6,5},{7,6},{8,7},{9,8},{10,9},{11,1... | collective-permute-start | bytes 1572872 | tf_op jit(solution)/shard_map/ppermute | solution.py:361
  35.1 0.8 copy-start.2
  52.7 8.3 %copy-start.3 = (bf16[256,1024]{1,0:T(8,128)(2,1)}, bf16[256,1024]{1,0:T(8,128)(2,1)S(1)}, u32[]{:S(2)}) copy-start(bf16[256,1024]{1,0:T(8,128)(2,1)S(1)} %collective-permute-done.1.xn_ref) | copy-start | bytes 1572868
  52.7 8.3 %copy-start.4 = (bf16[256,1024]{1,0:T(8,128)(2,1)}, bf16[256,1024]{1,0:T(8,128)(2,1)S(1)}, u32[]{:S(2)}) copy-start(bf16[256,1024]{1,0:T(8,128)(2,1)S(1)} %collective-permute-done.2.gn_ref) | copy-start | bytes 1572868
  52.8 3.0 %collective-permute-start.3 = (bf16[256,2048]{1,0:T(8,128)(2,1)}, bf16[256,2048]{1,0:T(8,128)(2,1)S(1)}, u32[]{:S(2)}, u32[]{:S(2)}) collective-permute-start(bf16[256,2048]{1,0:T(8,128)(2,1)} %get-tuple-element.47), channel_id=1, source_target_pairs={{0,32},{32,0},{1,33},{33,1},{2,34},{34,2},{3,35},{35,3},{4,36},{36... | collective-permute-start | bytes 3145736 | tf_op jit(solution)/shard_map/ppermute | solution.py:352
  52.9 4.4 %collective-permute-start.4 = (bf16[256,2048]{1,0:T(8,128)(2,1)}, bf16[256,2048]{1,0:T(8,128)(2,1)S(1)}, u32[]{:S(2)}, u32[]{:S(2)}) collective-permute-start(bf16[256,2048]{1,0:T(8,128)(2,1)} %get-tuple-element.48), channel_id=1, source_target_pairs={{0,32},{32,0},{1,33},{33,1},{2,34},{34,2},{3,35},{35,3},{4,36},{36... | collective-permute-start | bytes 3145736 | tf_op jit(solution)/shard_map/ppermute | solution.py:352
  61.1 43.8 %all-to-all-start = ((bf16[64,8,2048]{2,1,0:T(8,128)(2,1)}), bf16[64,8,2048]{2,1,0:T(8,128)(2,1)S(1)}, u32[]{:S(2)}, u32[]{:S(2)}) async-start(bf16[64,8,2048]{2,1,0:T(8,128)(2,1)} %bitcast.8), calls=%async_computation | async-start | bytes 4194304 | tf_op jit(solution)/shard_map/all_to_all | solution.py:383
  92.9 3.0 %collective-permute-start.5 = (bf16[256,2048]{1,0:T(8,128)(2,1)}, bf16[256,2048]{1,0:T(8,128)(2,1)S(1)}, u32[]{:S(2)}, u32[]{:S(2)}) collective-permute-start(bf16[256,2048]{1,0:T(8,128)(2,1)} %get-tuple-element.62), channel_id=1, source_target_pairs={{0,32},{32,0},{1,33},{33,1},{2,34},{34,2},{3,35},{35,3},{4,36},{36... | collective-permute-start | bytes 3145736 | tf_op jit(solution)/shard_map/ppermute | solution.py:352
  93.0 4.4 %collective-permute-start.6 = (bf16[256,2048]{1,0:T(8,128)(2,1)}, bf16[256,2048]{1,0:T(8,128)(2,1)S(1)}, u32[]{:S(2)}, u32[]{:S(2)}) collective-permute-start(bf16[256,2048]{1,0:T(8,128)(2,1)} %get-tuple-element.63), channel_id=1, source_target_pairs={{0,32},{32,0},{1,33},{33,1},{2,34},{34,2},{3,35},{35,3},{4,36},{36... | collective-permute-start | bytes 3145736 | tf_op jit(solution)/shard_map/ppermute | solution.py:352
  104.9 36.2 %all-to-all-start.1 = ((bf16[64,8,2048]{2,1,0:T(8,128)(2,1)}), bf16[64,8,2048]{2,1,0:T(8,128)(2,1)}, u32[]{:S(2)}, u32[]{:S(2)}) async-start(bf16[64,8,2048]{2,1,0:T(8,128)(2,1)} %fusion.1), calls=%async_computation.1 | async-start | bytes 4194304 | tf_op jit(solution)/shard_map/all_to_all | solution.py:389
  112.4 4.8 %copy-start = (bf16[1024,1024]{1,0:T(8,128)(2,1)S(1)}, bf16[1024,1024]{1,0:T(8,128)(2,1)}, u32[]{:S(2)}) copy-start(bf16[1024,1024]{1,0:T(8,128)(2,1)} %wk_ref.5) | copy-start | bytes 6291460
  112.4 4.8 %copy-start.7 = (bf16[1024,1024]{1,0:T(8,128)(2,1)S(1)}, bf16[1024,1024]{1,0:T(8,128)(2,1)}, u32[]{:S(2)}) copy-start(bf16[1024,1024]{1,0:T(8,128)(2,1)} %get-tuple-element.59) | copy-start | bytes 6291460
  117.2 2.4 %copy-start.1 = (bf16[1024,1024]{1,0:T(8,128)(2,1)S(1)}, bf16[1024,1024]{1,0:T(8,128)(2,1)}, u32[]{:S(2)}) copy-start(bf16[1024,1024]{1,0:T(8,128)(2,1)} %wv_ref.5) | copy-start | bytes 6291460
  117.2 2.4 %copy-start.6 = (bf16[1024,1024]{1,0:T(8,128)(2,1)S(1)}, bf16[1024,1024]{1,0:T(8,128)(2,1)}, u32[]{:S(2)}) copy-start(bf16[1024,1024]{1,0:T(8,128)(2,1)} %get-tuple-element.60) | copy-start | bytes 6291460
  123.3 19.7 %copy-start.5 = (f32[8,4096]{1,0:T(8,128)S(1)}, f32[8,4096]{1,0:T(8,128)}, u32[]{:S(2)}) copy-start(f32[8,4096]{1,0:T(8,128)} %param.13) | copy-start | bytes 393220

commit v5 on v4

--- a/solution.py
+++ b/solution.py
@@ -24,6 +24,7 @@
 SMALL = pl.CostEstimate(flops=10**8, bytes_accessed=10**5, transcendentals=0)
 VMEM = 60 * 2**20
 PAIR = 2 * HD
+FOUR = 4 * HD
 HALF = WIN // 2
 NEG = -1e30
 
@@ -103,15 +104,15 @@
 def store_product(turned, right, send_refs, keep_ref, start):
     product = bf(dot(jnp.concatenate([part[...] for part in turned], axis=0), right, 1, 0))
     half = product.shape[0] // 2
-    columns = pl.ds(pl.multiple_of(start, PAIR), PAIR)
-    quarter = half // 2
+    columns = pl.ds(pl.multiple_of(start, FOUR), FOUR)
+    piece = half // len(send_refs)
     for i, send_ref in enumerate(send_refs):
-        send_ref[:, columns] = product[i * quarter : (i + 1) * quarter]
+        send_ref[:, columns] = product[i * piece : (i + 1) * piece]
     keep_ref[:, columns] = product[half:]
 
 
-def lanes():
-    return [slice(h * HD, (h + 1) * HD) for h in range(PAIR // HD)]
+def lanes(width):
+    return [slice(h * HD, (h + 1) * HD) for h in range(width // HD)]
 
 
 def front_kernel(
@@ -134,38 +135,40 @@
     a0_ref[...] = a_ref[:WIN, :]
     kz_ref[...] = k_ref[count - WIN :, :]
     vz_ref[...] = v_ref[count - WIN :, :]
-    for c in lanes():
-        block = [
-            tuple(
-                ref[span[i], c]
-                for ref, i in ((q_ref, b), (a_ref, b), (k_ref, b - 1), (v_ref, b - 1), (k_ref, b), (v_ref, b))
-            )
-            for b in range(1, blocks)
-        ]
-        scores = [scores_of(entry, None) for entry in block]
-        weights = [probs_of(entry, upper) for entry in scores]
-        deltas = []
-        for i, entry in enumerate(block):
-            attended, delta = delta_of(entry, weights[i])
-            att_ref[span[i], c] = attended
-            deltas.append(delta)
-        sgrads = [score_grads(*entry) for entry in zip(scores, weights, deltas)]
-        for i, (query, grad, key_l, _, key_r, _) in enumerate(block):
-            ds_l, ds_r = sgrads[i]
-            _, pb_l, pb_r = weights[i]
-            dq_ref[span[i], c] = bf((dot(ds_l, key_l, 1, 0) + dot(ds_r, key_r, 1, 0)) * SCALE)
-            dk_l = dot(ds_l, query, 0, 0)
-            dv_l = dot(pb_l, grad, 0, 0)
-            if i == 0:
-                pk0_ref[:, c] = dk_l
-                pv0_ref[:, c] = dv_l
-            else:
-                dk_ref[span[i - 1], c] = bf((dk_open + dk_l) * SCALE)
-                dv_ref[span[i - 1], c] = bf(dv_open + dv_l)
-            dk_open = dot(ds_r, query, 0, 0)
-            dv_open = dot(pb_r, grad, 0, 0)
-        pkz_ref[:, c] = dk_open
-        pvz_ref[:, c] = dv_open
+    entries = [(c, b) for c in lanes(PAIR) for b in range(1, blocks)]
+    block = [
+        tuple(
+            ref[span[i], c]
+            for ref, i in ((q_ref, b), (a_ref, b), (k_ref, b - 1), (v_ref, b - 1), (k_ref, b), (v_ref, b))
+        )
+        for c, b in entries
+    ]
+    scores = [scores_of(entry, None) for entry in block]
+    weights = [probs_of(entry, upper) for entry in scores]
+    deltas = []
+    for i, (c, b) in enumerate(entries):
+        attended, delta = delta_of(block[i], weights[i])
+        att_ref[span[b - 1], c] = attended
+        deltas.append(delta)
+    sgrads = [score_grads(*entry) for entry in zip(scores, weights, deltas)]
+    for i, (c, b) in enumerate(entries):
+        query, grad, key_l, _, key_r, _ = block[i]
+        ds_l, ds_r = sgrads[i]
+        _, pb_l, pb_r = weights[i]
+        dq_ref[span[b - 1], c] = bf((dot(ds_l, key_l, 1, 0) + dot(ds_r, key_r, 1, 0)) * SCALE)
+        dk_l = dot(ds_l, query, 0, 0)
+        dv_l = dot(pb_l, grad, 0, 0)
+        if b == 1:
+            pk0_ref[:, c] = dk_l
+            pv0_ref[:, c] = dv_l
+        else:
+            dk_ref[span[b - 2], c] = bf((dk_open + dk_l) * SCALE)
+            dv_ref[span[b - 2], c] = bf(dv_open + dv_l)
+        dk_open = dot(ds_r, query, 0, 0)
+        dv_open = dot(pb_r, grad, 0, 0)
+        if b == blocks - 1:
+            pkz_ref[:, c] = dk_open
+            pvz_ref[:, c] = dv_open
 
 
 def front(tokens, out_grad, w_query, w_key, w_value, w_output):
@@ -197,7 +200,7 @@
 
 def first_kernel(
     core_ref, bias_ref, q_ref, k_ref, v_ref, a_ref, pk_ref, pv_ref, att_in, dq_in, xl_ref, wk_ref, wv_ref,
-    x0, x1, x2, x3, g_hbm, dq_ref, dk_ref, dv_ref, sa_ref, sb_ref, keep_ref, att_ref, g_ref, g_sem,
+    x0, x1, x2, x3, g_hbm, dq_ref, dk_ref, dv_ref, send_ref, keep_ref, att_ref, g_ref, g_sem,
 ):
     step = pl.program_id(0)
     fetch = pltpu.make_async_copy(g_hbm, g_ref, g_sem)
@@ -206,84 +209,69 @@
     def _():
         fetch.start()
 
-    side = lax.rem(step, 2)
-    att = att_ref.at[side]
     upper = upper_triangle()
     keys_l = bf(dot(xl_ref[...], wk_ref[...], 1, 0))
     values_l = bf(dot(xl_ref[...], wv_ref[...], 1, 0))
     block = [
-        (q_ref[:, c], a_ref[:, c], keys_l[:, c], values_l[:, c], k_ref[:, c], v_ref[:, c]) for c in lanes()
+        (q_ref[:, c], a_ref[:, c], keys_l[:, c], values_l[:, c], k_ref[:, c], v_ref[:, c]) for c in lanes(FOUR)
     ]
     scores = [scores_of(entry, bias_ref[0]) for entry in block]
     weights = [probs_of(entry, upper) for entry in scores]
     deltas = []
-    for i, c in enumerate(lanes()):
+    for i, c in enumerate(lanes(FOUR)):
         attended, delta = delta_of(block[i], weights[i])
-        att[:WIN, c] = attended
+        att_ref[:WIN, c] = attended
         deltas.append(delta)
-    att[WIN:, :] = att_in[...]
+    att_ref[WIN:, :] = att_in[...]
     dq_ref[WIN:, :] = dq_in[...]
-    for i, c in enumerate(lanes()):
+    for i, c in enumerate(lanes(FOUR)):
         query, grad, key_l, _, key_r, _ = block[i]
         ds_l, ds_r = score_grads(scores[i], weights[i], deltas[i])
         dq_ref[:WIN, c] = bf((dot(ds_l, key_l, 1, 0) + dot(ds_r, key_r, 1, 0)) * SCALE)
         dk_ref[:, c] = bf((pk_ref[:, c] + dot(ds_r, query, 0, 0)) * SCALE)
         dv_ref[:, c] = bf(pv_ref[:, c] + dot(weights[i][2], grad, 0, 0))
-    store_product((x0, x1, x2, x3), dq_ref[...], (sa_ref, sb_ref), keep_ref, step * PAIR)
-
-    @pl.when(step == 1)
+    store_product((x0, x1, x2, x3), dq_ref[...], (send_ref,), keep_ref, step * FOUR)
+
+    @pl.when(step == 0)
     def _():
         fetch.wait()
 
-    @pl.when(side == 1)
-    def _():
-        width = g_ref.shape[1]
-        product = bf(dot(jnp.concatenate([att_ref[0], att_ref[1]], axis=1), g_ref[...], 0, 0))
-        rows = pl.ds(pl.multiple_of((step // 2) * PAIR, PAIR), PAIR)
-
-        mine = core_ref[0] == 0
-        keep_ref[rows, width:] = jnp.where(mine, product[:PAIR], product[PAIR:])
-        other = jnp.where(mine, product[PAIR:], product[:PAIR])
-
-        @pl.when(step == 1)
-        def _():
-            sa_ref[:, width:] = other
-
-        @pl.when(step == 3)
-        def _():
-            sb_ref[:, width:] = other
+    product = bf(dot(att_ref[...], g_ref[...], 0, 0))
+    rows = pl.ds(pl.multiple_of(step * PAIR, PAIR), PAIR)
+    width = g_ref.shape[1]
+    mine = core_ref[0] == 0
+    keep_ref[rows, width:] = jnp.where(mine, product[:PAIR], product[PAIR:])
+    send_ref[rows, width:] = jnp.where(mine, product[PAIR:], product[:PAIR])
 
 
 def first_block(core, bias, own, partial, late, out_grad, tokens_l, w_key, w_value, turned):
     width, count = turned.shape
-    rim = pl.BlockSpec((WIN, PAIR), lambda j, c: (0, j))
-    rest = pl.BlockSpec((count - WIN, PAIR), lambda j, c: (0, j))
-    full = pl.BlockSpec((count, PAIR), lambda j, c: (0, j))
+    rim = pl.BlockSpec((WIN, FOUR), lambda j, c: (0, j))
+    rest = pl.BlockSpec((count - WIN, FOUR), lambda j, c: (0, j))
+    full = pl.BlockSpec((count, FOUR), lambda j, c: (0, j))
     left = pl.BlockSpec((WIN, width), lambda j, c: (0, 0))
-    column = pl.BlockSpec((width, PAIR), lambda j, c: (0, j))
+    column = pl.BlockSpec((width, FOUR), lambda j, c: (0, j))
     sums = pl.BlockSpec((width // 2, 2 * width), lambda j, c: (0, 0))
     both = jax.ShapeDtypeStruct((width // 2, 2 * width), BF16)
-    half = pl.BlockSpec((width // 4, 2 * width), lambda j, c: (0, 0))
-    part_sum = jax.ShapeDtypeStruct((width // 4, 2 * width), BF16)
     part = jax.ShapeDtypeStruct((WIN, width), BF16)
     return pl.pallas_call(
         first_kernel,
         grid_spec=pltpu.PrefetchScalarGridSpec(
             num_scalar_prefetch=1,
-            grid=(width // PAIR,),
+            grid=(width // FOUR,),
             in_specs=[pl.BlockSpec(memory_space=pltpu.SMEM)]
             + [rim] * 6
             + [rest, rest, left, column, column]
             + turned_specs(width, count)
             + [pl.BlockSpec(memory_space=pl.ANY)],
-            out_specs=[full, rim, rim, half, half, sums],
+            out_specs=[full, rim, rim, sums, sums],
             scratch_shapes=[
-                pltpu.VMEM((2, count, PAIR), BF16),
+                pltpu.VMEM((count, FOUR), BF16),
                 pltpu.VMEM((count, width), BF16),
                 pltpu.SemaphoreType.DMA,
             ],
         ),
-        out_shape=[jax.ShapeDtypeStruct((count, width), BF16), part, part, part_sum, part_sum, both],
+        out_shape=[jax.ShapeDtypeStruct((count, width), BF16), part, part, both, both],
         compiler_params=pltpu.CompilerParams(vmem_limit_bytes=VMEM),
         cost_estimate=SMALL,
         name="first_block",
@@ -291,17 +279,17 @@
 
 
 def last_kernel(
-    core_ref, xn_ref, gn_ref, wq_ref, wk_ref, wv_ref, wo_ref, k_ref, v_ref, pk_ref, pv_ref, dk0_ref, dv0_ref,
+    core_ref, ahead_ref, wq_ref, wk_ref, wv_ref, wo_ref, k_ref, v_ref, pk_ref, pv_ref, dk0_ref, dv0_ref,
     dkm_ref, dvm_ref, x0, x1, x2, x3, dk_ref, dv_ref, sa_ref, sb_ref, keep_ref,
 ):
     upper = upper_triangle()
-    tokens = xn_ref[...]
+    tokens = ahead_ref[:WIN, :]
     queries = bf(dot(tokens, wq_ref[...], 1, 0))
     keys = bf(dot(tokens, wk_ref[...], 1, 0))
     values = bf(dot(tokens, wv_ref[...], 1, 0))
-    grads = bf(dot(gn_ref[...], wo_ref[...], 1, 1))
+    grads = bf(dot(ahead_ref[WIN:, :], wo_ref[...], 1, 1))
     block = [
-        (queries[:, c], grads[:, c], k_ref[:, c], v_ref[:, c], keys[:, c], values[:, c]) for c in lanes()
+        (queries[:, c], grads[:, c], k_ref[:, c], v_ref[:, c], keys[:, c], values[:, c]) for c in lanes(FOUR)
     ]
     scores = [scores_of(entry, None) for entry in block]
     weights = [probs_of(entry, upper) for entry in scores]
@@ -311,23 +299,23 @@
     dv_ref[:WIN, :] = dv0_ref[...]
     dk_ref[WIN:end, :] = dkm_ref[...]
     dv_ref[WIN:end, :] = dvm_ref[...]
-    for i, c in enumerate(lanes()):
+    for i, c in enumerate(lanes(FOUR)):
         ds_l = score_grads(scores[i], weights[i], deltas[i])[0]
         dk_ref[end:, c] = bf((pk_ref[:, c] + dot(ds_l, block[i][0], 0, 0)) * SCALE)
         dv_ref[end:, c] = bf(pv_ref[:, c] + dot(weights[i][1], block[i][1], 0, 0))
-    start = pl.program_id(0) * PAIR
+    start = pl.program_id(0) * FOUR
     store_product((x0, x1, x2, x3), dk_ref[...], (sa_ref, sb_ref), keep_ref, start)
     store_product((x0, x1, x2, x3), dv_ref[...], (sa_ref, sb_ref), keep_ref, start + keep_ref.shape[1] // 2)
 
 
-def last_block(core, tokens_n, grads_n, weights, last, partial, first, middle, turned):
+def last_block(core, ahead, weights, last, partial, first, middle, turned):
     width, count = turned.shape
-    column = pl.BlockSpec((width, PAIR), lambda j, c: (0, j))
-    row = pl.BlockSpec((PAIR, width), lambda j, c: (j, 0))
-    rim = pl.BlockSpec((WIN, PAIR), lambda j, c: (0, j))
-    near = pl.BlockSpec((WIN, width), lambda j, c: (0, 0))
-    mid = pl.BlockSpec((count - 2 * WIN, PAIR), lambda j, c: (0, j))
-    full = pl.BlockSpec((count, PAIR), lambda j, c: (0, j))
+    column = pl.BlockSpec((width, FOUR), lambda j, c: (0, j))
+    row = pl.BlockSpec((FOUR, width), lambda j, c: (j, 0))
+    rim = pl.BlockSpec((WIN, FOUR), lambda j, c: (0, j))
+    near = pl.BlockSpec((2 * WIN, width), lambda j, c: (0, 0))
+    mid = pl.BlockSpec((count - 2 * WIN, FOUR), lambda j, c: (0, j))
+    full = pl.BlockSpec((count, FOUR), lambda j, c: (0, j))
     sums = pl.BlockSpec((width // 2, 2 * width), lambda j, c: (0, 0))
     grad = jax.ShapeDtypeStruct((count, width), BF16)
     both = jax.ShapeDtypeStruct((width // 2, 2 * width), BF16)
@@ -337,15 +325,15 @@
         last_kernel,
         grid_spec=pltpu.PrefetchScalarGridSpec(
             num_scalar_prefetch=1,
-            grid=(width // PAIR,),
-            in_specs=[near, near, column, column, column, row] + [rim] * 6 + [mid, mid] + turned_specs(width, count),
+            grid=(width // FOUR,),
+            in_specs=[near, column, column, column, row] + [rim] * 6 + [mid, mid] + turned_specs(width, count),
             out_specs=[full, full, half, half, sums],
         ),
         out_shape=[grad, grad, part_sum, part_sum, both],
         compiler_params=pltpu.CompilerParams(vmem_limit_bytes=VMEM),
         cost_estimate=SMALL,
         name="last_block",
-    )(core, tokens_n, grads_n, *weights, *last, *partial, *first, *middle, *[turned] * 4)
+    )(core, ahead, *weights, *last, *partial, *first, *middle, *[turned] * 4)
 
 
 def chip_sum(sends, keep):
@@ -370,20 +358,19 @@
     first = (lax.axis_index("y") + lax.axis_index("z") + lax.axis_index("xl")) == 0
     bias = jnp.where(first, NEG, 0.0).astype(F32).reshape(1)
     tokens_l = passed_along(tokens[count - WIN :], 1)
-    tokens_n = passed_along(tokens[:WIN], -1)
-    grads_n = passed_along(out_grad[:WIN], -1)
+    ahead = passed_along(jnp.concatenate([tokens[:WIN], out_grad[:WIN]], axis=0), -1)
     weights = (w_query, w_key, w_value, w_output)
     turned, *rest = front(tokens, out_grad, *weights)
     own, last, late, middle, partial_0, partial_z = rest[:4], rest[4:6], rest[6:8], rest[8:10], rest[10:12], rest[12:]
-    query_grad, key_0, value_0, send_a, send_b, keep = first_block(
+    query_grad, key_0, value_0, send, keep = first_block(
         which, bias, own, partial_0, late, out_grad, tokens_l, w_key, w_value, turned
     )
-    send_a, send_b, tokens_n, grads_n = lax.optimization_barrier((send_a, send_b, tokens_n, grads_n))
-    both = chip_sum((send_a, send_b), keep)
+    send, ahead = lax.optimization_barrier((send, ahead))
+    both = chip_sum((send,), keep)
     pieces_qo = lax.all_to_all(both, CHIPS, 0, 0, tiled=True)
-    tokens_n, _ = lax.optimization_barrier((tokens_n, both))
+    ahead, _ = lax.optimization_barrier((ahead, both))
     key_grad, value_grad, send_a, send_b, keep = last_block(
-        which, tokens_n, grads_n, weights, last, partial_z, (key_0, value_0), middle, turned
+        which, ahead, weights, last, partial_z, (key_0, value_0), middle, turned
     )
     both = chip_sum((send_a, send_b), keep)
     pieces_kv = lax.all_to_all(both, CHIPS, 0, 0, tiled=True)

time: 144 us -> 145 us (level)
  starting transfers between devices: 29.6 us -> 32.4 us
    all_to_all x1, starting transfers between devices: 14.8 us -> 18.2 us  [on_device(): pieces_qo = lax.all_to_all(both, CHIPS, 0, 0, tiled=True)]
    ppermute x4 -> x3, waiting for transfers between devices: 7.72 us -> 8.22 us  [chip_sum(): got = [lax.ppermute(send, 'co', [(0, 1), (1, 0)]) for send in sends]]
    ppermute x3 -> x2, starting transfers between devices: 6.1 us -> 5.87 us  [passed_along(): return lax.ppermute(block, SEQ, route)]
  transfers between devices with their start and end apart: 9 -> 7, of which waited for: 6 -> 5; matrix products, arithmetic and copies ran while one was open for 11% -> 10% of each run, Pallas kernels for 42% -> 41%
where the time goes in v5:
time: 145 us; the launch traced here: 144 us
  Pallas kernels  58.6 us (40%)
  starting transfers between devices  32.4 us (22%)
  waiting for transfers between devices  28.9 us (20%)
  matrix products  10.8 us (7%)
  other arithmetic  10.5 us (7%)
  local copies, waits for them, and re-layouts  2.32 us (2%)
    pallas_call x1, Pallas kernels, front(): pl.pallas_call(front_kernel, grid=(width // PAIR,), in_specs=[whole, whol...  25.6 us
    all_to_all x1, starting transfers between devices, on_device(): pieces_qo = lax.all_to_all(both, CHIPS, 0, 0, tiled=True)  18.2 us
    all_to_all x1, waiting for transfers between devices, on_device(): pieces_kv = lax.all_to_all(both, CHIPS, 0, 0, tiled=True)  17.3 us
    pallas_call x1, Pallas kernels, last_block(): pl.pallas_call(last_kernel, grid_spec=pltpu.PrefetchScalarGridSpec(num_sc...  17.2 us
    pallas_call x1, Pallas kernels, first_block(): pl.pallas_call(first_kernel, grid_spec=pltpu.PrefetchScalarGridSpec(num_s...  15.7 us
    dot_general x3, matrix products, dot(): lax.dot_general(a, b, (((ca,), (cb,)), ((), ())), preferred_element_type=...  10.8 us
    ppermute x3, waiting for transfers between devices, chip_sum(): got = [lax.ppermute(send, 'co', [(0, 1), (1, 0)]) for send in sends]  8.22 us
    all_to_all x1, starting transfers between devices, on_device(): pieces_kv = lax.all_to_all(both, CHIPS, 0, 0, tiled=True)  7.74 us
  transfers between devices with their start and end apart: 7, of which 5 were waited for; matrix products, arithmetic and copies ran while one was open for 10% of the time, Pallas kernels for 41%

profile of v5, /device:TPU:0, one launch (start us, length us, event | category | flops | bytes accessed | tf_op | source)
XLA Modules:
  0.0 144.4 jit_solution(11583333718138035927)
XLA Ops:
  0.6 1.5 %slice_bitcast_fusion.1 = (bf16[256,1024]{1,0:T(8,128)(2,1)S(1)}, bf16[256,1024]{1,0:T(8,128)(2,1)S(1)}, bf16[256,1024]{1,0:T(8,128)(2,1)S(1)}) fusion(bf16[1,1024,1024]{2,1,0:T(8,128)(2,1)} %param.7, bf16[1,1024,1024]{2,1,0:T(8,128)(2,1)} %param.8), kind=kLoop, calls=%fused_computation.9 | loop fusion | bytes 3145728 | tf_op jit(solution)/shard_map/slice | solution.py:361
  2.1 0.1 pad_maximum_fusion
  2.2 1.3 collective-permute-start.1
  3.5 4.6 %collective-permute-start = (bf16[256,1024]{1,0:T(8,128)(2,1)S(1)}, bf16[256,1024]{1,0:T(8,128)(2,1)S(1)}, u32[]{:S(2)}, u32[]{:S(2)}) collective-permute-start(bf16[256,1024]{1,0:T(8,128)(2,1)S(1)} %get-tuple-element.59), channel_id=1, source_target_pairs={{0,1},{1,2},{2,3},{3,4},{4,5},{5,6},{6,7},{7,8},{8,9},{9,10},{10,1... | collective-permute-start | bytes 1572872 | tf_op jit(solution)/shard_map/ppermute | solution.py:349
  8.1 25.6 %front.1 = (bf16[1024,1024]{1,0:T(8,128)(2,1)}, bf16[256,1024]{1,0:T(8,128)(2,1)}, bf16[256,1024]{1,0:T(8,128)(2,1)}, bf16[256,1024]{1,0:T(8,128)(2,1)}, bf16[25...) custom-call(bf16[1024,1024]{1,0:T(8,128)(2,1)} %bitcast.21, ...), custom_call_target="tpu_custom_call" | custom-call | flops 100000000 | bytes 100000 | tf_op jit(solution)/shard_map/front/pallas_call | solution.py:188
  33.7 0.0 collective-permute-done.xl_ref
  33.7 0.0 copy-start.3
  33.8 0.8 copy-done.3
  34.5 15.7 %first_block.1 = (bf16[1024,1024]{1,0:T(8,128)(2,1)}, bf16[256,1024]{1,0:T(8,128)(2,1)}, bf16[256,1024]{1,0:T(8,128)(2,1)}, bf16[512,2048]{1,0:T(8,128)(2,1)}, bf16[512,2048]{1,0:T(8,128)(2,1)}) custom-call(s32[1]{0:T(128)} %bitcast.core_ref, f32[1]{0:T(128)} %bitcast.1.bias_ref, bf16[256,1024]{1,0:T(8,128)(2,1)} %get-tuple-element.30.q_ref, ...), custom_call_target="tpu_custom_call" | custom-call | flops 100000000 | bytes 100000 | tf_op jit(solution)/shard_map/first_block/pallas_call | solution.py:257
  50.3 0.0 collective-permute-done.1.ahead_ref
  50.3 0.0 copy-start.2
  50.3 0.1 collective-permute-start.2
  50.4 4.4 %collective-permute-done.2 = bf16[512,2048]{1,0:T(8,128)(2,1)S(1)} collective-permute-done((bf16[512,2048]{1,0:T(8,128)(2,1)}, bf16[512,2048]{1,0:T(8,128)(2,1)S(1)}, u32[]{:S(2)}, u32[]{:S(2)}) %collective-permute-start.2) | collective-permute-done | bytes 2097184 | tf_op jit(solution)/shard_map/ppermute | solution.py:340
  54.8 3.7 %add_convert_fusion.2 = bf16[512,2048]{1,0:T(8,128)(2,1)} fusion(bf16[512,2048]{1,0:T(8,128)(2,1)S(1)} %collective-permute-done.2, bf16[512,2048]{1,0:T(8,128)(2,1)} %get-tuple-element.42), kind=kLoop, calls=%fused_computation.4 | loop fusion | flops 4194304 | bytes 6291456 | tf_op jit(solution)/shard_map/convert_element_type | solution.py:33
  58.5 18.2 %all-to-all-start = ((bf16[64,8,2048]{2,1,0:T(8,128)(2,1)}), bf16[64,8,2048]{2,1,0:T(8,128)(2,1)S(1)}, u32[]{:S(2)}, u32[]{:S(2)}) async-start(bf16[64,8,2048]{2,1,0:T(8,128)(2,1)} %bitcast.8), calls=%async_computation | async-start | bytes 4194304 | tf_op jit(solution)/shard_map/all_to_all | solution.py:370
  76.6 17.2 %last_block.1 = (bf16[1024,1024]{1,0:T(8,128)(2,1)}, bf16[1024,1024]{1,0:T(8,128)(2,1)}, bf16[256,2048]{1,0:T(8,128)(2,1)}, bf16[256,2048]{1,0:T(8,128)(2,1)}, bf16[512,2048]{1,0:T(8,128)(2,1)}) custom-call(s32[1]{0:T(128)} %bitcast.core_ref, bf16[512,1024]{1,0:T(8,128)(2,1)} %copy-done.2, bf16[1024,1024]{1,0:T(8,128)(2,1)} %wq_ref.3, ...), custom_call_target="tpu_custom_call" | custom-call | flops 100000000 | bytes 100000 | tf_op jit(solution)/shard_map/last_block/pallas_call | solution.py:324
  93.9 0.1 collective-permute-start.3
  93.9 0.5 collective-permute-start.4
  94.4 2.4 %collective-permute-done.3 = bf16[256,2048]{1,0:T(8,128)(2,1)S(1)} collective-permute-done((bf16[256,2048]{1,0:T(8,128)(2,1)}, bf16[256,2048]{1,0:T(8,128)(2,1)S(1)}, u32[]{:S(2)}, u32[]{:S(2)}) %collective-permute-start.3) | collective-permute-done | bytes 1048608 | tf_op jit(solution)/shard_map/ppermute | solution.py:340
  96.8 1.5 %collective-permute-done.4 = bf16[256,2048]{1,0:T(8,128)(2,1)S(1)} collective-permute-done((bf16[256,2048]{1,0:T(8,128)(2,1)}, bf16[256,2048]{1,0:T(8,128)(2,1)S(1)}, u32[]{:S(2)}, u32[]{:S(2)}) %collective-permute-start.4) | collective-permute-done | bytes 1048608 | tf_op jit(solution)/shard_map/ppermute | solution.py:340
  98.3 3.9 %fusion.1 = bf16[64,8,2048]{2,1,0:T(8,128)(2,1)} fusion(bf16[512,2048]{1,0:T(8,128)(2,1)} %get-tuple-element.55, bf16[256,2048]{1,0:T(8,128)(2,1)S(1)} %collective-permute-done.4, bf16[256,2048]{1,0:T(8,128)(2,1)S(1)} %collective-permute-done.3), kind=kLoop, calls=%fused_computation.6 | loop fusion | flops 7340032 | bytes 6291456 | tf_op jit(solution)/shard_map/all_to_all | solution.py:376
  102.2 3.4 %all-to-all-done = bf16[64,8,2048]{2,1,0:T(8,128)(2,1)S(1)} async-done(((bf16[64,8,2048]{2,1,0:T(8,128)(2,1)}), bf16[64,8,2048]{2,1,0:T(8,128)(2,1)S(1)}, u32[]{:S(2)}, u32[]{:S(2)}) %all-to-all-start) | async-done | bytes 2097184 | tf_op jit(solution)/shard_map/all_to_all | solution.py:370
  105.6 7.7 %all-to-all-start.1 = ((bf16[64,8,2048]{2,1,0:T(8,128)(2,1)}), bf16[64,8,2048]{2,1,0:T(8,128)(2,1)}, u32[]{:S(2)}, u32[]{:S(2)}) async-start(bf16[64,8,2048]{2,1,0:T(8,128)(2,1)} %fusion.1), calls=%async_computation.1 | async-start | bytes 4194304 | tf_op jit(solution)/shard_map/all_to_all | solution.py:376
  113.4 0.0 copy-start
  113.4 4.7 %fusion.4 = f32[1024,1024]{1,0:T(8,128)S(1)} fusion(bf16[1024,1024]{1,0:T(8,128)(2,1)} %get-tuple-element.39, bf16[1024,1024]{1,0:T(8,128)(2,1)} %wq_ref.3), kind=kOutput, calls=%fused_computation.14 | convolution fusion | flops 2147483648 | bytes 8388608 | tf_op jit(solution)/shard_map/dot_general | solution.py:21
  118.1 0.0 copy-start.1
  118.2 2.4 %fusion.5 = f32[1024,1024]{1,0:T(8,128)S(1)} fusion(bf16[1024,1024]{1,0:T(8,128)(2,1)S(1)} %copy-done.6, bf16[1024,1024]{1,0:T(8,128)(2,1)S(1)} %copy-done), kind=kOutput, calls=%fused_computation.15 | convolution fusion | flops 2147483648 | bytes 8388608 | tf_op jit(solution)/shard_map/dot_general | solution.py:21
  120.6 3.7 %fusion = bf16[1,1024,1024]{2,1,0:T(8,128)(2,1)} fusion(f32[1024,1024]{1,0:T(8,128)S(1)} %fusion.4, f32[1024,1024]{1,0:T(8,128)S(1)} %fusion.5, bf16[1024,1024]{1,0:T(8,128)(2,1)S(1)} %copy-done.5, bf16[1024,1024]{1,0:T(8,128)(2,1)S(1)} %copy-done.1), kind=kOutput, calls=%fused_computation.5 | convolution fusion | flops 2150629376 | bytes 14680064 | tf_op jit(solution)/shard_map/dot_general | solution.py:21
  124.3 0.3 convert_reduce_fusion.1
  124.6 17.3 %all-to-all-done.1 = bf16[64,8,2048]{2,1,0:T(8,128)(2,1)} async-done(((bf16[64,8,2048]{2,1,0:T(8,128)(2,1)}), bf16[64,8,2048]{2,1,0:T(8,128)(2,1)}, u32[]{:S(2)}, u32[]{:S(2)}) %all-to-all-start.1) | async-done | bytes 2097184 | tf_op jit(solution)/shard_map/all_to_all | solution.py:376
  141.9 1.9 %convert_reduce_fusion = f32[8,2048]{1,0:T(8,128)S(1)} fusion(bf16[64,8,2048]{2,1,0:T(8,128)(2,1)} %all-to-all-done.1), kind=kLoop, calls=%fused_computation | loop fusion | flops 2080768 | bytes 2162688 | tf_op jit(solution)/shard_map/reduce_sum | solution.py:381
  143.8 0.7 fusion.2
  (10 shorter events, 0.0 us)
Async XLA Ops:
  2.2 48.1 %collective-permute-start.1 = (bf16[512,1024]{1,0:T(8,128)(2,1)S(1)}, bf16[512,1024]{1,0:T(8,128)(2,1)S(1)}, u32[]{:S(2)}, u32[]{:S(2)}) collective-permute-start(bf16[512,1024]{1,0:T(8,128)(2,1)S(1)} %pad_maximum_fusion), channel_id=1, source_target_pairs={{1,0},{2,1},{3,2},{4,3},{5,4},{6,5},{7,6},{8,7},{9,8},{10,9},{11,1... | collective-permute-start | bytes 3145736 | tf_op jit(solution)/shard_map/ppermute | solution.py:349
  3.5 30.2 %collective-permute-start = (bf16[256,1024]{1,0:T(8,128)(2,1)S(1)}, bf16[256,1024]{1,0:T(8,128)(2,1)S(1)}, u32[]{:S(2)}, u32[]{:S(2)}) collective-permute-start(bf16[256,1024]{1,0:T(8,128)(2,1)S(1)} %get-tuple-element.59), channel_id=1, source_target_pairs={{0,1},{1,2},{2,3},{3,4},{4,5},{5,6},{6,7},{7,8},{8,9},{9,10},{10,1... | collective-permute-start | bytes 1572872 | tf_op jit(solution)/shard_map/ppermute | solution.py:349
  33.7 0.8 copy-start.3
  50.3 8.1 %copy-start.2 = (bf16[512,1024]{1,0:T(8,128)(2,1)}, bf16[512,1024]{1,0:T(8,128)(2,1)S(1)}, u32[]{:S(2)}) copy-start(bf16[512,1024]{1,0:T(8,128)(2,1)S(1)} %collective-permute-done.1.ahead_ref) | copy-start | bytes 3145732
  50.3 4.5 %collective-permute-start.2 = (bf16[512,2048]{1,0:T(8,128)(2,1)}, bf16[512,2048]{1,0:T(8,128)(2,1)S(1)}, u32[]{:S(2)}, u32[]{:S(2)}) collective-permute-start(bf16[512,2048]{1,0:T(8,128)(2,1)} %get-tuple-element.43), channel_id=1, source_target_pairs={{0,32},{32,0},{1,33},{33,1},{2,34},{34,2},{3,35},{35,3},{4,36},{36... | collective-permute-start | bytes 6291464 | tf_op jit(solution)/shard_map/ppermute | solution.py:340
  58.5 47.1 %all-to-all-start = ((bf16[64,8,2048]{2,1,0:T(8,128)(2,1)}), bf16[64,8,2048]{2,1,0:T(8,128)(2,1)S(1)}, u32[]{:S(2)}, u32[]{:S(2)}) async-start(bf16[64,8,2048]{2,1,0:T(8,128)(2,1)} %bitcast.8), calls=%async_computation | async-start | bytes 4194304 | tf_op jit(solution)/shard_map/all_to_all | solution.py:370
  93.9 3.0 %collective-permute-start.3 = (bf16[256,2048]{1,0:T(8,128)(2,1)}, bf16[256,2048]{1,0:T(8,128)(2,1)S(1)}, u32[]{:S(2)}, u32[]{:S(2)}) collective-permute-start(bf16[256,2048]{1,0:T(8,128)(2,1)} %get-tuple-element.56), channel_id=1, source_target_pairs={{0,32},{32,0},{1,33},{33,1},{2,34},{34,2},{3,35},{35,3},{4,36},{36... | collective-permute-start | bytes 3145736 | tf_op jit(solution)/shard_map/ppermute | solution.py:340
  93.9 4.4 %collective-permute-start.4 = (bf16[256,2048]{1,0:T(8,128)(2,1)}, bf16[256,2048]{1,0:T(8,128)(2,1)S(1)}, u32[]{:S(2)}, u32[]{:S(2)}) collective-permute-start(bf16[256,2048]{1,0:T(8,128)(2,1)} %get-tuple-element.57), channel_id=1, source_target_pairs={{0,32},{32,0},{1,33},{33,1},{2,34},{34,2},{3,35},{35,3},{4,36},{36... | collective-permute-start | bytes 3145736 | tf_op jit(solution)/shard_map/ppermute | solution.py:340
  105.6 36.2 %all-to-all-start.1 = ((bf16[64,8,2048]{2,1,0:T(8,128)(2,1)}), bf16[64,8,2048]{2,1,0:T(8,128)(2,1)}, u32[]{:S(2)}, u32[]{:S(2)}) async-start(bf16[64,8,2048]{2,1,0:T(8,128)(2,1)} %fusion.1), calls=%async_computation.1 | async-start | bytes 4194304 | tf_op jit(solution)/shard_map/all_to_all | solution.py:376
  113.4 4.8 %copy-start = (bf16[1024,1024]{1,0:T(8,128)(2,1)S(1)}, bf16[1024,1024]{1,0:T(8,128)(2,1)}, u32[]{:S(2)}) copy-start(bf16[1024,1024]{1,0:T(8,128)(2,1)} %wk_ref.5) | copy-start | bytes 6291460
  113.4 4.8 %copy-start.6 = (bf16[1024,1024]{1,0:T(8,128)(2,1)S(1)}, bf16[1024,1024]{1,0:T(8,128)(2,1)}, u32[]{:S(2)}) copy-start(bf16[1024,1024]{1,0:T(8,128)(2,1)} %get-tuple-element.53) | copy-start | bytes 6291460
  118.1 2.4 %copy-start.1 = (bf16[1024,1024]{1,0:T(8,128)(2,1)S(1)}, bf16[1024,1024]{1,0:T(8,128)(2,1)}, u32[]{:S(2)}) copy-start(bf16[1024,1024]{1,0:T(8,128)(2,1)} %wv_ref.5) | copy-start | bytes 6291460
  118.2 2.4 %copy-start.5 = (bf16[1024,1024]{1,0:T(8,128)(2,1)S(1)}, bf16[1024,1024]{1,0:T(8,128)(2,1)}, u32[]{:S(2)}) copy-start(bf16[1024,1024]{1,0:T(8,128)(2,1)} %get-tuple-element.54) | copy-start | bytes 6291460
  124.3 19.5 %copy-start.4 = (f32[8,4096]{1,0:T(8,128)S(1)}, f32[8,4096]{1,0:T(8,128)}, u32[]{:S(2)}) copy-start(f32[8,4096]{1,0:T(8,128)} %param.13) | copy-start | bytes 393220

commit v6 on v5

--- a/solution.py
+++ b/solution.py
@@ -33,10 +33,6 @@
     return value.astype(BF16)
 
 
-def quads(a, b, c, d):
-    return jnp.concatenate([jnp.concatenate([a, b], axis=1), jnp.concatenate([c, d], axis=1)], axis=0)
-
-
 def upper_triangle():
     rows = lax.broadcasted_iota(jnp.int32, (HALF, HALF), 0)
     cols = lax.broadcasted_iota(jnp.int32, (HALF, HALF), 1)
@@ -44,54 +40,53 @@
 
 
 def scores_of(block, bias):
-    query, grad, key_l, value_l, key_r, value_r = block
-    s_l = dot(query, key_l, 1, 1)
+    query, grad, key, value = block
+    scores = dot(query, key, 1, 1)
     if bias is not None:
-        s_l = s_l + bias
-    return s_l, dot(query, key_r, 1, 1), dot(grad, value_l, 1, 1), dot(grad, value_r, 1, 1)
+        scores = jnp.concatenate([scores[:, :WIN] + bias, scores[:, WIN:]], axis=1)
+    return scores, dot(grad, value, 1, 1)
+
+
+def runs_of(array):
+    return [
+        [array[h * HALF : (h + 1) * HALF, (h + i) * HALF : (h + i + 1) * HALF] for i in range(3)] for h in range(2)
+    ]
+
+
+def whole_of(runs):
+    zero = jnp.zeros((HALF, HALF), BF16)
+    top, bottom = [[bf(part) for part in run] for run in runs]
+    return jnp.concatenate(
+        [jnp.concatenate(top + [zero], axis=1), jnp.concatenate([zero] + bottom, axis=1)], axis=0
+    )
 
 
 def probs_of(scores, upper):
-    s_l, s_r = scores[:2]
-    low = slice(0, HALF)
-    high = slice(HALF, WIN)
-    runs = (
-        (jnp.where(upper, s_l[low, low], NEG), s_l[low, high], jnp.where(upper, NEG, s_r[low, low])),
-        (jnp.where(upper, s_l[high, high], NEG), s_r[high, low], jnp.where(upper, NEG, s_r[high, high])),
-    )
     probs = []
-    for run in runs:
+    for first, middle, last in runs_of(scores[0]):
+        run = [jnp.where(upper, first, NEG), middle, jnp.where(upper, NEG, last)]
         top = jnp.max(jnp.maximum(jnp.maximum(run[0], run[1]), run[2]), axis=1, keepdims=True)
         shift = top * (SCALE * LOG2E)
         e = [jnp.exp2(part * (SCALE * LOG2E) - shift) for part in run]
         inv = 1.0 / jnp.sum(e[0] + e[1] + e[2], axis=1, keepdims=True)
         probs.append([part * inv for part in e])
-    zero = jnp.zeros((HALF, HALF), BF16)
-    (t0, t1, t2), (b0, b1, b2) = probs
-    return probs, quads(bf(t0), bf(t1), zero, bf(b0)), quads(bf(t2), zero, bf(b1), bf(b2))
+    return probs, whole_of(probs)
 
 
 def delta_of(block, weights):
-    grad, value_l, value_r = block[1], block[3], block[5]
-    attended = bf(dot(weights[1], value_l, 1, 0) + dot(weights[2], value_r, 1, 0))
+    grad, value = block[1], block[3]
+    attended = bf(dot(weights[1], value, 1, 0))
     return attended, jnp.sum(grad.astype(F32) * attended.astype(F32), axis=1, keepdims=True)
 
 
 def score_grads(scores, weights, delta):
-    d_l, d_r = scores[2:]
-    low = slice(0, HALF)
-    high = slice(HALF, WIN)
-    (t0, t1, t2), (b0, b1, b2) = weights[0]
-    dt = delta[low]
-    db = delta[high]
-    zero = jnp.zeros((HALF, HALF), BF16)
-    left = quads(
-        bf(t0 * (d_l[low, low] - dt)), bf(t1 * (d_l[low, high] - dt)), zero, bf(b0 * (d_l[high, high] - db))
-    )
-    right = quads(
-        bf(t2 * (d_r[low, low] - dt)), zero, bf(b1 * (d_r[high, low] - db)), bf(b2 * (d_r[high, high] - db))
-    )
-    return left, right
+    halves = (delta[:HALF], delta[HALF:])
+    return whole_of(
+        [
+            [p * (d - half) for p, d in zip(probs, prob_grads)]
+            for probs, prob_grads, half in zip(weights[0], runs_of(scores[1]), halves)
+        ]
+    )
 
 
 def turned_specs(width, count):
@@ -117,10 +112,16 @@
 
 def front_kernel(
     x_ref, g_ref, wq_ref, wk_ref, wv_ref, wo_ref, part_ref,
-    turned_ref, q0_ref, k0_ref, v0_ref, a0_ref, kz_ref, vz_ref, att_ref, dq_ref, dk_ref, dv_ref,
+    turned_ref, xh_ref, gh_ref, q0_ref, k0_ref, v0_ref, a0_ref, kz_ref, vz_ref, att_ref, dq_ref, dk_ref, dv_ref,
     pk0_ref, pv0_ref, pkz_ref, pvz_ref, q_ref, k_ref, v_ref, a_ref,
 ):
     turned_ref[...] = part_ref[...].T
+
+    @pl.when(pl.program_id(0) == 0)
+    def _():
+        xh_ref[...] = x_ref[:WIN, :]
+        gh_ref[...] = g_ref[:WIN, :]
+
     upper = upper_triangle()
     count = x_ref.shape[0]
     blocks = count // WIN
@@ -135,11 +136,12 @@
     a0_ref[...] = a_ref[:WIN, :]
     kz_ref[...] = k_ref[count - WIN :, :]
     vz_ref[...] = v_ref[count - WIN :, :]
+    window = [slice((b - 1) * WIN, (b + 1) * WIN) for b in range(blocks)]
     entries = [(c, b) for c in lanes(PAIR) for b in range(1, blocks)]
     block = [
         tuple(
-            ref[span[i], c]
-            for ref, i in ((q_ref, b), (a_ref, b), (k_ref, b - 1), (v_ref, b - 1), (k_ref, b), (v_ref, b))
+            ref[rows, c]
+            for ref, rows in ((q_ref, span[b]), (a_ref, span[b]), (k_ref, window[b]), (v_ref, window[b]))
         )
         for c, b in entries
     ]
@@ -152,20 +154,20 @@
         deltas.append(delta)
     sgrads = [score_grads(*entry) for entry in zip(scores, weights, deltas)]
     for i, (c, b) in enumerate(entries):
-        query, grad, key_l, _, key_r, _ = block[i]
-        ds_l, ds_r = sgrads[i]
-        _, pb_l, pb_r = weights[i]
-        dq_ref[span[b - 1], c] = bf((dot(ds_l, key_l, 1, 0) + dot(ds_r, key_r, 1, 0)) * SCALE)
-        dk_l = dot(ds_l, query, 0, 0)
-        dv_l = dot(pb_l, grad, 0, 0)
+        query, grad, key, _ = block[i]
+        dq_ref[span[b - 1], c] = bf(dot(sgrads[i], key, 1, 0) * SCALE)
+        dk = dot(sgrads[i], query, 0, 0)
+        dv = dot(weights[i][1], grad, 0, 0)
+        dk_l = dk[:WIN]
+        dv_l = dv[:WIN]
         if b == 1:
             pk0_ref[:, c] = dk_l
             pv0_ref[:, c] = dv_l
         else:
             dk_ref[span[b - 2], c] = bf((dk_open + dk_l) * SCALE)
             dv_ref[span[b - 2], c] = bf(dv_open + dv_l)
-        dk_open = dot(ds_r, query, 0, 0)
-        dv_open = dot(pb_r, grad, 0, 0)
+        dk_open = dk[WIN:]
+        dv_open = dv[WIN:]
         if b == blocks - 1:
             pkz_ref[:, c] = dk_open
             pvz_ref[:, c] = dv_open
@@ -183,14 +185,15 @@
     def like(rows, dtype=BF16):
         return jax.ShapeDtypeStruct((rows, width), dtype)
 
+    head = pl.BlockSpec((WIN, width), lambda j: (0, 0))
     rim, late, mid = WIN, count - WIN, count - 2 * WIN
     heights = [rim] * 6 + [late, late, mid, mid]
     return pl.pallas_call(
         front_kernel,
         grid=(width // PAIR,),
         in_specs=[whole, whole, column, column, column, row, out(count)],
-        out_specs=[row] + [out(h) for h in heights] + [out(rim)] * 4,
-        out_shape=[like(width)] + [like(h) for h in heights] + [like(rim, F32)] * 4,
+        out_specs=[row, head, head] + [out(h) for h in heights] + [out(rim)] * 4,
+        out_shape=[like(width), like(rim), like(rim)] + [like(h) for h in heights] + [like(rim, F32)] * 4,
         scratch_shapes=[pltpu.VMEM((count, PAIR), BF16)] * 4,
         compiler_params=pltpu.CompilerParams(vmem_limit_bytes=VMEM),
         cost_estimate=SMALL,
@@ -212,9 +215,9 @@
     upper = upper_triangle()
     keys_l = bf(dot(xl_ref[...], wk_ref[...], 1, 0))
     values_l = bf(dot(xl_ref[...], wv_ref[...], 1, 0))
-    block = [
-        (q_ref[:, c], a_ref[:, c], keys_l[:, c], values_l[:, c], k_ref[:, c], v_ref[:, c]) for c in lanes(FOUR)
-    ]
+    keys = jnp.concatenate([keys_l, k_ref[...]], axis=0)
+    values = jnp.concatenate([values_l, v_ref[...]], axis=0)
+    block = [(q_ref[:, c], a_ref[:, c], keys[:, c], values[:, c]) for c in lanes(FOUR)]
     scores = [scores_of(entry, bias_ref[0]) for entry in block]
     weights = [probs_of(entry, upper) for entry in scores]
     deltas = []
@@ -225,11 +228,11 @@
     att_ref[WIN:, :] = att_in[...]
     dq_ref[WIN:, :] = dq_in[...]
     for i, c in enumerate(lanes(FOUR)):
-        query, grad, key_l, _, key_r, _ = block[i]
-        ds_l, ds_r = score_grads(scores[i], weights[i], deltas[i])
-        dq_ref[:WIN, c] = bf((dot(ds_l, key_l, 1, 0) + dot(ds_r, key_r, 1, 0)) * SCALE)
-        dk_ref[:, c] = bf((pk_ref[:, c] + dot(ds_r, query, 0, 0)) * SCALE)
-        dv_ref[:, c] = bf(pv_ref[:, c] + dot(weights[i][2], grad, 0, 0))
+        query, grad, key, _ = block[i]
+        ds = score_grads(scores[i], weights[i], deltas[i])
+        dq_ref[:WIN, c] = bf(dot(ds, key, 1, 0) * SCALE)
+        dk_ref[:, c] = bf((pk_ref[:, c] + dot(ds[:, WIN:], query, 0, 0)) * SCALE)
+        dv_ref[:, c] = bf(pv_ref[:, c] + dot(weights[i][1][:, WIN:], grad, 0, 0))
     store_product((x0, x1, x2, x3), dq_ref[...], (send_ref,), keep_ref, step * FOUR)
 
     @pl.when(step == 0)
@@ -279,18 +282,16 @@
 
 
 def last_kernel(
-    core_ref, ahead_ref, wq_ref, wk_ref, wv_ref, wo_ref, k_ref, v_ref, pk_ref, pv_ref, dk0_ref, dv0_ref,
+    core_ref, xn_ref, gn_ref, wq_ref, wk_ref, wv_ref, wo_ref, k_ref, v_ref, pk_ref, pv_ref, dk0_ref, dv0_ref,
     dkm_ref, dvm_ref, x0, x1, x2, x3, dk_ref, dv_ref, sa_ref, sb_ref, keep_ref,
 ):
     upper = upper_triangle()
-    tokens = ahead_ref[:WIN, :]
+    tokens = xn_ref[...]
     queries = bf(dot(tokens, wq_ref[...], 1, 0))
-    keys = bf(dot(tokens, wk_ref[...], 1, 0))
-    values = bf(dot(tokens, wv_ref[...], 1, 0))
-    grads = bf(dot(ahead_ref[WIN:, :], wo_ref[...], 1, 1))
-    block = [
-        (queries[:, c], grads[:, c], k_ref[:, c], v_ref[:, c], keys[:, c], values[:, c]) for c in lanes(FOUR)
-    ]
+    keys = jnp.concatenate([k_ref[...], bf(dot(tokens, wk_ref[...], 1, 0))], axis=0)
+    values = jnp.concatenate([v_ref[...], bf(dot(tokens, wv_ref[...], 1, 0))], axis=0)
+    grads = bf(dot(gn_ref[...], wo_ref[...], 1, 1))
+    block = [(queries[:, c], grads[:, c], keys[:, c], values[:, c]) for c in lanes(FOUR)]
     scores = [scores_of(entry, None) for entry in block]
     weights = [probs_of(entry, upper) for entry in scores]
     deltas = [delta_of(*entry)[1] for entry in zip(block, weights)]
@@ -300,20 +301,20 @@
     dk_ref[WIN:end, :] = dkm_ref[...]
     dv_ref[WIN:end, :] = dvm_ref[...]
     for i, c in enumerate(lanes(FOUR)):
-        ds_l = score_grads(scores[i], weights[i], deltas[i])[0]
-        dk_ref[end:, c] = bf((pk_ref[:, c] + dot(ds_l, block[i][0], 0, 0)) * SCALE)
-        dv_ref[end:, c] = bf(pv_ref[:, c] + dot(weights[i][1], block[i][1], 0, 0))
+        ds = score_grads(scores[i], weights[i], deltas[i])
+        dk_ref[end:, c] = bf((pk_ref[:, c] + dot(ds[:, :WIN], block[i][0], 0, 0)) * SCALE)
+        dv_ref[end:, c] = bf(pv_ref[:, c] + dot(weights[i][1][:, :WIN], block[i][1], 0, 0))
     start = pl.program_id(0) * FOUR
     store_product((x0, x1, x2, x3), dk_ref[...], (sa_ref, sb_ref), keep_ref, start)
     store_product((x0, x1, x2, x3), dv_ref[...], (sa_ref, sb_ref), keep_ref, start + keep_ref.shape[1] // 2)
 
 
-def last_block(core, ahead, weights, last, partial, first, middle, turned):
+def last_block(core, tokens_n, grads_n, weights, last, partial, first, middle, turned):
     width, count = turned.shape
     column = pl.BlockSpec((width, FOUR), lambda j, c: (0, j))
     row = pl.BlockSpec((FOUR, width), lambda j, c: (j, 0))
     rim = pl.BlockSpec((WIN, FOUR), lambda j, c: (0, j))
-    near = pl.BlockSpec((2 * WIN, width), lambda j, c: (0, 0))
+    near = pl.BlockSpec((WIN, width), lambda j, c: (0, 0))
     mid = pl.BlockSpec((count - 2 * WIN, FOUR), lambda j, c: (0, j))
     full = pl.BlockSpec((count, FOUR), lambda j, c: (0, j))
     sums = pl.BlockSpec((width // 2, 2 * width), lambda j, c: (0, 0))
@@ -326,19 +327,25 @@
         grid_spec=pltpu.PrefetchScalarGridSpec(
             num_scalar_prefetch=1,
             grid=(width // FOUR,),
-            in_specs=[near, column, column, column, row] + [rim] * 6 + [mid, mid] + turned_specs(width, count),
+            in_specs=[near, near, column, column, column, row] + [rim] * 6 + [mid, mid] + turned_specs(width, count),
             out_specs=[full, full, half, half, sums],
         ),
         out_shape=[grad, grad, part_sum, part_sum, both],
         compiler_params=pltpu.CompilerParams(vmem_limit_bytes=VMEM),
         cost_estimate=SMALL,
         name="last_block",
-    )(core, ahead, *weights, *last, *partial, *first, *middle, *[turned] * 4)
-
-
-def chip_sum(sends, keep):
+    )(core, tokens_n, grads_n, *weights, *last, *partial, *first, *middle, *[turned] * 4)
+
+
+def chip_sum(sends, keep, meanwhile=None):
     got = [lax.ppermute(send, "co", [(0, 1), (1, 0)]) for send in sends]
-    return bf(keep.astype(F32) + jnp.concatenate(got, axis=0).astype(F32))
+    if meanwhile is not None:
+        *got, meanwhile = lax.optimization_barrier((*got, meanwhile))
+    return bf(keep.astype(F32) + jnp.concatenate(got, axis=0).astype(F32)), meanwhile
+
+
+def piece_sum(pieces, width):
+    return jnp.sum(pieces.reshape(-1, 8, width).astype(F32), axis=0)
 
 
 def passed_along(block, distance):
@@ -358,34 +365,36 @@
     first = (lax.axis_index("y") + lax.axis_index("z") + lax.axis_index("xl")) == 0
     bias = jnp.where(first, NEG, 0.0).astype(F32).reshape(1)
     tokens_l = passed_along(tokens[count - WIN :], 1)
-    ahead = passed_along(jnp.concatenate([tokens[:WIN], out_grad[:WIN]], axis=0), -1)
     weights = (w_query, w_key, w_value, w_output)
-    turned, *rest = front(tokens, out_grad, *weights)
+    turned, head_x, head_g, *rest = front(tokens, out_grad, *weights)
+    tokens_n = passed_along(head_x, -1)
+    grads_n = passed_along(head_g, -1)
     own, last, late, middle, partial_0, partial_z = rest[:4], rest[4:6], rest[6:8], rest[8:10], rest[10:12], rest[12:]
     query_grad, key_0, value_0, send, keep = first_block(
         which, bias, own, partial_0, late, out_grad, tokens_l, w_key, w_value, turned
     )
-    send, ahead = lax.optimization_barrier((send, ahead))
-    both = chip_sum((send,), keep)
+    send, tokens_n = lax.optimization_barrier((send, tokens_n))
+    both, _ = chip_sum((send,), keep)
     pieces_qo = lax.all_to_all(both, CHIPS, 0, 0, tiled=True)
-    ahead, _ = lax.optimization_barrier((ahead, both))
+    tokens_n, _ = lax.optimization_barrier((tokens_n, both))
     key_grad, value_grad, send_a, send_b, keep = last_block(
-        which, ahead, weights, last, partial_z, (key_0, value_0), middle, turned
-    )
-    both = chip_sum((send_a, send_b), keep)
-    pieces_kv = lax.all_to_all(both, CHIPS, 0, 0, tiled=True)
+        which, tokens_n, grads_n, weights, last, partial_z, (key_0, value_0), middle, turned
+    )
     in_grad = bf(
         dot(query_grad, w_query, 1, 1) + dot(key_grad, w_key, 1, 1) + dot(value_grad, w_value, 1, 1)
     )
-    sum_qo, sum_kv = [
-        jnp.sum(pieces.reshape(-1, 8, 2 * width).astype(F32), axis=0) for pieces in (pieces_qo, pieces_kv)
-    ]
+    both, in_grad = chip_sum((send_a, send_b), keep, in_grad)
     total = count
     for axis in AXES:
         total *= lax.axis_size(axis)
     factor = 1.0 / total**0.5
-    summed = jnp.concatenate([sum_qo[:, :width], sum_kv, sum_qo[:, width:]], axis=1)
-    return in_grad[None], grad_accum + summed * factor
+    sum_qo = piece_sum(pieces_qo, 2 * width) * factor
+    new_q = grad_accum[:, :width] + sum_qo[:, :width]
+    new_o = grad_accum[:, 3 * width :] + sum_qo[:, width:]
+    rest = grad_accum[:, width : 3 * width]
+    both, new_q, new_o, rest = lax.optimization_barrier((both, new_q, new_o, rest))
+    sum_kv = piece_sum(lax.all_to_all(both, CHIPS, 0, 0, tiled=True), 2 * width) * factor
+    return in_grad[None], jnp.concatenate([new_q, rest + sum_kv, new_o], axis=1)
 
 
 def solution(mesh):

time: 145 us -> 148 us (1.021)
  blocking collectives: 0 us -> 39.1 us
  waiting for transfers between devices: 28.9 us -> 3.07 us
  starting transfers between devices: 32.4 us -> 20.8 us
  other arithmetic: 10.5 us -> 7.52 us
  matrix products: 10.8 us -> 13.7 us
    all_to_all x0 -> x1, blocking collectives: none -> 39.1 us  [on_device(): lax.all_to_all(both, CHIPS, 0, 0, tiled=True)]
    all_to_all x1 -> x0, waiting for transfers between devices: 17.3 us -> none  [on_device(): pieces_kv = lax.all_to_all(both, CHIPS, 0, 0, tiled=True)]
    all_to_all x1 -> x0, starting transfers between devices: 7.74 us -> none  [on_device(): pieces_kv = lax.all_to_all(both, CHIPS, 0, 0, tiled=True)]
    ppermute x3, waiting for transfers between devices: 8.22 us -> 3.06 us  [chip_sum(): got = [lax.ppermute(send, 'co', [(0, 1), (1, 0)]) for send in sends]]
    all_to_all x1, starting transfers between devices: 18.2 us -> 14 us  [on_device(): pieces_qo = lax.all_to_all(both, CHIPS, 0, 0, tiled=True)]
    all_to_all x1 -> x0, other arithmetic: 3.87 us -> none  [on_device(): pieces_kv = lax.all_to_all(both, CHIPS, 0, 0, tiled=True)]
    all_to_all x1, waiting for transfers between devices: 3.43 us -> 0.01 us  [on_device(): pieces_qo = lax.all_to_all(both, CHIPS, 0, 0, tiled=True)]
    dot_general x3, matrix products: 10.8 us -> 13.7 us  [dot(): lax.dot_general(a, b, (((ca,), (cb,)), ((), ())), preferred_element_type=...]
  transfers between devices with their start and end apart: 7 -> 7, of which waited for: 5 -> 1; matrix products, arithmetic and copies ran while one was open for 10% -> 12% of each run, Pallas kernels for 41% -> 40%
where the time goes in v6:
time: 148 us
  Pallas kernels  59.2 us (40%)
  blocking collectives  39.1 us (26%)
  starting transfers between devices  20.8 us (14%)
  matrix products  13.7 us (9%)
  other arithmetic  7.52 us (5%)
  local copies, waits for them, and re-layouts  3.25 us (2%)
  waiting for transfers between devices  3.07 us (2%)
    all_to_all x1, blocking collectives, on_device(): lax.all_to_all(both, CHIPS, 0, 0, tiled=True)  39.1 us
    pallas_call x1, Pallas kernels, front(): pl.pallas_call(front_kernel, grid=(width // PAIR,), in_specs=[whole, whol...  26.5 us
    pallas_call x1, Pallas kernels, last_block(): pl.pallas_call(last_kernel, grid_spec=pltpu.PrefetchScalarGridSpec(num_sc...  17 us
    pallas_call x1, Pallas kernels, first_block(): pl.pallas_call(first_kernel, grid_spec=pltpu.PrefetchScalarGridSpec(num_s...  15.7 us
    all_to_all x1, starting transfers between devices, on_device(): pieces_qo = lax.all_to_all(both, CHIPS, 0, 0, tiled=True)  14 us
    dot_general x3, matrix products, dot(): lax.dot_general(a, b, (((ca,), (cb,)), ((), ())), preferred_element_type=...  13.7 us
    ppermute x3, starting transfers between devices, passed_along(): return lax.ppermute(block, SEQ, route)  6.1 us
    convert_element_type x2, other arithmetic, bf(): return value.astype(BF16)  4.58 us
  transfers between devices with their start and end apart: 7, of which 1 were waited for; matrix products, arithmetic and copies ran while one was open for 12% of the time, Pallas kernels for 40%

profile of v6, /device:TPU:0, one launch (start us, length us, event | category | flops | bytes accessed | tf_op | source)
XLA Modules:
  0.0 147.5 jit_solution(10704364224593848001)
XLA Ops:
  0.6 1.1 slice_bitcast_fusion
  1.7 3.5 %collective-permute-start = (bf16[256,1024]{1,0:T(8,128)(2,1)S(1)}, bf16[256,1024]{1,0:T(8,128)(2,1)S(1)}, u32[]{:S(2)}, u32[]{:S(2)}) collective-permute-start(bf16[256,1024]{1,0:T(8,128)(2,1)S(1)} %slice_bitcast_fusion), channel_id=1, source_target_pairs={{0,1},{1,2},{2,3},{3,4},{4,5},{5,6},{6,7},{7,8},{8,9},{9,10},{10,1... | collective-permute-start | bytes 1572872 | tf_op jit(solution)/shard_map/ppermute | solution.py:356
  5.2 26.5 %front.1 = (bf16[1024,1024]{1,0:T(8,128)(2,1)}, bf16[256,1024]{1,0:T(8,128)(2,1)}, bf16[256,1024]{1,0:T(8,128)(2,1)}, bf16[256,1024]{1,0:T(8,128)(2,1)}, bf16[25...) custom-call(bf16[1024,1024]{1,0:T(8,128)(2,1)} %bitcast.15, ...), custom_call_target="tpu_custom_call" | custom-call | flops 100000000 | bytes 100000 | tf_op jit(solution)/shard_map/front/pallas_call | solution.py:191
  31.7 1.3 collective-permute-start.1
  33.1 0.0 collective-permute-done.xl_ref
  33.1 0.0 copy-start.4
  33.1 0.8 copy-done.4
  33.9 15.7 %first_block.1 = (bf16[1024,1024]{1,0:T(8,128)(2,1)}, bf16[256,1024]{1,0:T(8,128)(2,1)}, bf16[256,1024]{1,0:T(8,128)(2,1)}, bf16[512,2048]{1,0:T(8,128)(2,1)}, bf16[512,2048]{1,0:T(8,128)(2,1)}) custom-call(s32[1]{0:T(128)} %bitcast.core_ref, f32[1]{0:T(128)} %bitcast.1.bias_ref, bf16[256,1024]{1,0:T(8,128)(2,1)} %get-tuple-element.39.q_ref, ...), custom_call_target="tpu_custom_call" | custom-call | flops 100000000 | bytes 100000 | tf_op jit(solution)/shard_map/first_block/pallas_call | solution.py:260
  49.6 0.0 collective-permute-done.1.xn_ref
  49.6 0.1 collective-permute-start.2
  49.7 1.3 collective-permute-start.3
  51.0 3.1 %collective-permute-done.2 = bf16[512,2048]{1,0:T(8,128)(2,1)S(1)} collective-permute-done((bf16[512,2048]{1,0:T(8,128)(2,1)}, bf16[512,2048]{1,0:T(8,128)(2,1)S(1)}, u32[]{:S(2)}, u32[]{:S(2)}) %collective-permute-start.2) | collective-permute-done | bytes 2097184 | tf_op jit(solution)/shard_map/ppermute | solution.py:341
  54.1 3.7 %add_convert_fusion.2 = bf16[512,2048]{1,0:T(8,128)(2,1)} fusion(bf16[512,2048]{1,0:T(8,128)(2,1)S(1)} %collective-permute-done.2, bf16[512,2048]{1,0:T(8,128)(2,1)} %get-tuple-element.51), kind=kLoop, calls=%fused_computation.4 | loop fusion | flops 4194304 | bytes 6291456 | tf_op jit(solution)/shard_map/convert_element_type | solution.py:33
  57.8 14.0 %all-to-all-start = ((bf16[64,8,2048]{2,1,0:T(8,128)(2,1)}), bf16[64,8,2048]{2,1,0:T(8,128)(2,1)}, u32[]{:S(2)}, u32[]{:S(2)}) async-start(bf16[64,8,2048]{2,1,0:T(8,128)(2,1)} %bitcast.6), calls=%async_computation | async-start | bytes 4194304 | tf_op jit(solution)/shard_map/all_to_all | solution.py:378
  71.8 5.9 %fusion = f32[1024,1024]{1,0:T(8,128)} fusion(bf16[1024,1024]{1,0:T(8,128)(2,1)} %get-tuple-element.65, bf16[1024,1024]{1,0:T(8,128)(2,1)S(1)} %copy-done.2), kind=kOutput, calls=%fused_computation.11 | convolution fusion | flops 2147483648 | bytes 8388608 | tf_op jit(solution)/shard_map/dot_general | solution.py:21
  77.8 0.0 collective-permute-done.3.gn_ref
  77.8 0.8 copy-done.6
  78.6 17.0 %last_block.1 = (bf16[1024,1024]{1,0:T(8,128)(2,1)}, bf16[1024,1024]{1,0:T(8,128)(2,1)}, bf16[256,2048]{1,0:T(8,128)(2,1)}, bf16[256,2048]{1,0:T(8,128)(2,1)}, bf16[512,2048]{1,0:T(8,128)(2,1)}) custom-call(s32[1]{0:T(128)} %bitcast.core_ref, bf16[256,1024]{1,0:T(8,128)(2,1)} %copy-done.5, bf16[256,1024]{1,0:T(8,128)(2,1)} %copy-done.6, ...), custom_call_target="tpu_custom_call" | custom-call | flops 100000000 | bytes 100000 | tf_op jit(solution)/shard_map/last_block/pallas_call | solution.py:325
  95.6 0.1 collective-permute-start.4
  95.7 0.5 collective-permute-start.5
  96.2 4.1 %fusion.1 = f32[1024,1024]{1,0:T(8,128)S(1)} fusion(bf16[1024,1024]{1,0:T(8,128)(2,1)} %get-tuple-element.66, bf16[1024,1024]{1,0:T(8,128)(2,1)S(1)} %copy-done), kind=kOutput, calls=%fused_computation.12 | convolution fusion | flops 2147483648 | bytes 8388608 | tf_op jit(solution)/shard_map/dot_general | solution.py:21
  100.3 3.7 %add_convert_fusion.1 = bf16[1024,1024]{1,0:T(8,128)(2,1)} fusion(f32[1024,1024]{1,0:T(8,128)S(1)} %copy-done.9, f32[1024,1024]{1,0:T(8,128)S(1)} %fusion.1, bf16[1024,1024]{1,0:T(8,128)(2,1)S(1)} %copy-done.8, bf16[1024,1024]{1,0:T(8,128)(2,1)S(1)} %copy-done.1), kind=kOutput, calls=%fused_computation.3 | convolution fusion | flops 2150629376 | bytes 14680064 | tf_op jit(solution)/shard_map/dot_general | solution.py:21
  104.0 0.0 collective-permute-done.4
  104.0 0.0 collective-permute-done.5
  104.0 0.8 add_convert_fusion
  104.9 0.0 copy-start.7
  104.9 0.0 all-to-all-done
  104.9 1.9 %convert_reduce_fusion.1 = f32[8,2048]{1,0:T(8,128)S(1)} fusion(bf16[64,8,2048]{2,1,0:T(8,128)(2,1)} %all-to-all-done), kind=kLoop, calls=%fused_computation.1 | loop fusion | flops 2080768 | bytes 2162688 | tf_op jit(solution)/shard_map/reduce_sum | solution.py:348
  106.9 39.1 %all_to_all.18 = bf16[64,8,2048]{2,1,0:T(8,128)(2,1)S(1)} all-to-all(bf16[64,8,2048]{2,1,0:T(8,128)(2,1)S(1)} %bitcast.17), channel_id=1, replica_groups=mesh['xh'=2,'co'=2,'y'=4,'z'=4,'xl'=2] {'xh','y','z','xl'}, dimensions={0} | all-to-all | bytes 4194304 | tf_op jit(solution)/shard_map/all_to_all | solution.py:396
  146.0 0.3 convert_reduce_fusion
  146.3 0.5 slice-done
  146.9 0.7 pad_maximum_fusion
  (20 shorter events, 0.1 us)
Async XLA Ops:
  1.7 31.3 %collective-permute-start = (bf16[256,1024]{1,0:T(8,128)(2,1)S(1)}, bf16[256,1024]{1,0:T(8,128)(2,1)S(1)}, u32[]{:S(2)}, u32[]{:S(2)}) collective-permute-start(bf16[256,1024]{1,0:T(8,128)(2,1)S(1)} %slice_bitcast_fusion), channel_id=1, source_target_pairs={{0,1},{1,2},{2,3},{3,4},{4,5},{5,6},{6,7},{7,8},{8,9},{9,10},{10,1... | collective-permute-start | bytes 1572872 | tf_op jit(solution)/shard_map/ppermute | solution.py:356
  31.7 17.9 %collective-permute-start.1 = (bf16[256,1024]{1,0:T(8,128)(2,1)}, bf16[256,1024]{1,0:T(8,128)(2,1)S(1)}, u32[]{:S(2)}, u32[]{:S(2)}) collective-permute-start(bf16[256,1024]{1,0:T(8,128)(2,1)} %get-tuple-element.49), channel_id=1, source_target_pairs={{1,0},{2,1},{3,2},{4,3},{5,4},{6,5},{7,6},{8,7},{9,8},{10,9},{11,1... | collective-permute-start | bytes 1572872 | tf_op jit(solution)/shard_map/ppermute | solution.py:356
  33.1 0.8 copy-start.4
  49.6 8.2 %copy-start.5 = (bf16[256,1024]{1,0:T(8,128)(2,1)}, bf16[256,1024]{1,0:T(8,128)(2,1)S(1)}, u32[]{:S(2)}) copy-start(bf16[256,1024]{1,0:T(8,128)(2,1)S(1)} %collective-permute-done.1.xn_ref) | copy-start | bytes 1572868
  49.6 4.5 %collective-permute-start.2 = (bf16[512,2048]{1,0:T(8,128)(2,1)}, bf16[512,2048]{1,0:T(8,128)(2,1)S(1)}, u32[]{:S(2)}, u32[]{:S(2)}) collective-permute-start(bf16[512,2048]{1,0:T(8,128)(2,1)} %get-tuple-element.52), channel_id=1, source_target_pairs={{0,32},{32,0},{1,33},{33,1},{2,34},{34,2},{3,35},{35,3},{4,36},{36... | collective-permute-start | bytes 6291464 | tf_op jit(solution)/shard_map/ppermute | solution.py:341
  49.7 28.0 %collective-permute-start.3 = (bf16[256,1024]{1,0:T(8,128)(2,1)}, bf16[256,1024]{1,0:T(8,128)(2,1)S(1)}, u32[]{:S(2)}, u32[]{:S(2)}) collective-permute-start(bf16[256,1024]{1,0:T(8,128)(2,1)} %get-tuple-element.54), channel_id=1, source_target_pairs={{1,0},{2,1},{3,2},{4,3},{5,4},{6,5},{7,6},{8,7},{9,8},{10,9},{11,1... | collective-permute-start | bytes 1572872 | tf_op jit(solution)/shard_map/ppermute | solution.py:356
  57.8 14.0 %copy-start.2 = (bf16[1024,1024]{1,0:T(8,128)(2,1)S(1)}, bf16[1024,1024]{1,0:T(8,128)(2,1)}, u32[]{:S(2)}) copy-start(bf16[1024,1024]{1,0:T(8,128)(2,1)} %wq_ref.3) | copy-start | bytes 6291460
  57.8 47.1 %all-to-all-start = ((bf16[64,8,2048]{2,1,0:T(8,128)(2,1)}), bf16[64,8,2048]{2,1,0:T(8,128)(2,1)}, u32[]{:S(2)}, u32[]{:S(2)}) async-start(bf16[64,8,2048]{2,1,0:T(8,128)(2,1)} %bitcast.6), calls=%async_computation | async-start | bytes 4194304 | tf_op jit(solution)/shard_map/all_to_all | solution.py:378
  77.8 0.8 copy-start.6
  78.6 17.6 %copy-start = (bf16[1024,1024]{1,0:T(8,128)(2,1)S(1)}, bf16[1024,1024]{1,0:T(8,128)(2,1)}, u32[]{:S(2)}) copy-start(bf16[1024,1024]{1,0:T(8,128)(2,1)} %wk_ref.5) | copy-start | bytes 6291460
  95.6 8.5 %collective-permute-start.4 = (bf16[256,2048]{1,0:T(8,128)(2,1)}, bf16[256,2048]{1,0:T(8,128)(2,1)S(1)}, u32[]{:S(2)}, u32[]{:S(2)}) collective-permute-start(bf16[256,2048]{1,0:T(8,128)(2,1)} %get-tuple-element.63), channel_id=1, source_target_pairs={{0,32},{32,0},{1,33},{33,1},{2,34},{34,2},{3,35},{35,3},{4,36},{36... | collective-permute-start | bytes 3145736 | tf_op jit(solution)/shard_map/ppermute | solution.py:341
  95.7 8.4 %collective-permute-start.5 = (bf16[256,2048]{1,0:T(8,128)(2,1)}, bf16[256,2048]{1,0:T(8,128)(2,1)S(1)}, u32[]{:S(2)}, u32[]{:S(2)}) collective-permute-start(bf16[256,2048]{1,0:T(8,128)(2,1)} %get-tuple-element.64), channel_id=1, source_target_pairs={{0,32},{32,0},{1,33},{33,1},{2,34},{34,2},{3,35},{35,3},{4,36},{36... | collective-permute-start | bytes 3145736 | tf_op jit(solution)/shard_map/ppermute | solution.py:341
  96.2 4.1 %copy-start.1 = (bf16[1024,1024]{1,0:T(8,128)(2,1)S(1)}, bf16[1024,1024]{1,0:T(8,128)(2,1)}, u32[]{:S(2)}) copy-start(bf16[1024,1024]{1,0:T(8,128)(2,1)} %wv_ref.5) | copy-start | bytes 6291460
  96.2 4.1 %copy-start.8 = (bf16[1024,1024]{1,0:T(8,128)(2,1)S(1)}, bf16[1024,1024]{1,0:T(8,128)(2,1)}, u32[]{:S(2)}) copy-start(bf16[1024,1024]{1,0:T(8,128)(2,1)} %get-tuple-element.67) | copy-start | bytes 6291460
  96.2 4.1 %copy-start.9 = (f32[1024,1024]{1,0:T(8,128)S(1)}, f32[1024,1024]{1,0:T(8,128)}, u32[]{:S(2)}) copy-start(f32[1024,1024]{1,0:T(8,128)} %fusion) | copy-start | bytes 12582916
  100.3 3.7 %copy-start.3 = (bf16[512,2048]{1,0:T(8,128)(2,1)S(1)}, bf16[512,2048]{1,0:T(8,128)(2,1)}, u32[]{:S(2)}) copy-start(bf16[512,2048]{1,0:T(8,128)(2,1)} %get-tuple-element.69) | copy-start | bytes 6291460
  104.9 2.0 %copy-start.7 = (f32[8,4096]{1,0:T(8,128)S(1)}, f32[8,4096]{1,0:T(8,128)}, u32[]{:S(2)}) copy-start(f32[8,4096]{1,0:T(8,128)} %param.13) | copy-start | bytes 393220
  146.0 0.8 slice-start

commit v7 on v6

--- a/solution.py
+++ b/solution.py
@@ -380,21 +380,18 @@
     key_grad, value_grad, send_a, send_b, keep = last_block(
         which, tokens_n, grads_n, weights, last, partial_z, (key_0, value_0), middle, turned
     )
-    in_grad = bf(
-        dot(query_grad, w_query, 1, 1) + dot(key_grad, w_key, 1, 1) + dot(value_grad, w_value, 1, 1)
-    )
-    both, in_grad = chip_sum((send_a, send_b), keep, in_grad)
+    send_a, send_b, query_grad = lax.optimization_barrier((send_a, send_b, query_grad))
+    both, in_query = chip_sum((send_a, send_b), keep, dot(query_grad, w_query, 1, 1))
+    pieces_kv = lax.all_to_all(both, CHIPS, 0, 0, tiled=True)
+    in_grad = bf(in_query + dot(key_grad, w_key, 1, 1) + dot(value_grad, w_value, 1, 1))
     total = count
     for axis in AXES:
         total *= lax.axis_size(axis)
     factor = 1.0 / total**0.5
-    sum_qo = piece_sum(pieces_qo, 2 * width) * factor
-    new_q = grad_accum[:, :width] + sum_qo[:, :width]
-    new_o = grad_accum[:, 3 * width :] + sum_qo[:, width:]
-    rest = grad_accum[:, width : 3 * width]
-    both, new_q, new_o, rest = lax.optimization_barrier((both, new_q, new_o, rest))
-    sum_kv = piece_sum(lax.all_to_all(both, CHIPS, 0, 0, tiled=True), 2 * width) * factor
-    return in_grad[None], jnp.concatenate([new_q, rest + sum_kv, new_o], axis=1)
+    sum_qo = piece_sum(pieces_qo, 2 * width)
+    sum_kv = piece_sum(pieces_kv, 2 * width)
+    summed = jnp.concatenate([sum_qo[:, :width], sum_kv, sum_qo[:, width:]], axis=1)
+    return in_grad[None], grad_accum + summed * factor
 
 
 def solution(mesh):

time: 148 us -> 141 us (0.953)
  blocking collectives: 39.1 us -> 0 us
  waiting for transfers between devices: 3.07 us -> 24.2 us
  starting transfers between devices: 20.8 us -> 29.1 us
  other arithmetic: 7.52 us -> 10.5 us
    all_to_all x1 -> x0, blocking collectives: 39.1 us -> none  [on_device(): lax.all_to_all(both, CHIPS, 0, 0, tiled=True)]
    all_to_all x0 -> x1, waiting for transfers between devices: none -> 18.9 us  [on_device(): pieces_kv = lax.all_to_all(both, CHIPS, 0, 0, tiled=True)]
    all_to_all x0 -> x1, starting transfers between devices: none -> 8.5 us  [on_device(): pieces_kv = lax.all_to_all(both, CHIPS, 0, 0, tiled=True)]
    all_to_all x0 -> x1, other arithmetic: none -> 2.31 us  [on_device(): pieces_kv = lax.all_to_all(both, CHIPS, 0, 0, tiled=True)]
    all_to_all x1, waiting for transfers between devices: 0.01 us -> 2.28 us  [on_device(): pieces_qo = lax.all_to_all(both, CHIPS, 0, 0, tiled=True)]
    reduce_sum x2, other arithmetic: 2.25 us -> 3.84 us  [piece_sum(): return jnp.sum(pieces.reshape(-1, 8, width).astype(F32), axis=0)]
    convert_element_type x2 -> x1, other arithmetic: 4.58 us -> 3.71 us  [bf(): return value.astype(BF16)]
  transfers between devices with their start and end apart: 7 -> 8, of which waited for: 1 -> 3; matrix products, arithmetic and copies ran while one was open for 12% -> 15% of each run, Pallas kernels for 40% -> 42%
where the time goes in v7:
time: 141 us; the launch traced here: 140 us
  Pallas kernels  59.1 us (42%)
  starting transfers between devices  29.1 us (21%)
  waiting for transfers between devices  24.2 us (17%)
  matrix products  13.8 us (10%)
  other arithmetic  10.5 us (7%)
  local copies, waits for them, and re-layouts  2.71 us (2%)
    pallas_call x1, Pallas kernels, front(): pl.pallas_call(front_kernel, grid=(width // PAIR,), in_specs=[whole, whol...  26.5 us
    all_to_all x1, waiting for transfers between devices, on_device(): pieces_kv = lax.all_to_all(both, CHIPS, 0, 0, tiled=True)  18.9 us
    pallas_call x1, Pallas kernels, last_block(): pl.pallas_call(last_kernel, grid_spec=pltpu.PrefetchScalarGridSpec(num_sc...  16.8 us
    pallas_call x1, Pallas kernels, first_block(): pl.pallas_call(first_kernel, grid_spec=pltpu.PrefetchScalarGridSpec(num_s...  15.8 us
    all_to_all x1, starting transfers between devices, on_device(): pieces_qo = lax.all_to_all(both, CHIPS, 0, 0, tiled=True)  13.9 us
    dot_general x3, matrix products, dot(): lax.dot_general(a, b, (((ca,), (cb,)), ((), ())), preferred_element_type=...  13.8 us
    all_to_all x1, starting transfers between devices, on_device(): pieces_kv = lax.all_to_all(both, CHIPS, 0, 0, tiled=True)  8.5 us
    ppermute x3, starting transfers between devices, passed_along(): return lax.ppermute(block, SEQ, route)  6.1 us
  transfers between devices with their start and end apart: 8, of which 3 were waited for; matrix products, arithmetic and copies ran while one was open for 15% of the time, Pallas kernels for 42%

profile of v7, /device:TPU:0, one launch (start us, length us, event | category | flops | bytes accessed | tf_op | source)
XLA Modules:
  0.0 140.4 jit_solution(16930241507957195675)
XLA Ops:
  0.6 1.1 slice_bitcast_fusion
  1.7 3.5 %collective-permute-start = (bf16[256,1024]{1,0:T(8,128)(2,1)S(1)}, bf16[256,1024]{1,0:T(8,128)(2,1)S(1)}, u32[]{:S(2)}, u32[]{:S(2)}) collective-permute-start(bf16[256,1024]{1,0:T(8,128)(2,1)S(1)} %slice_bitcast_fusion), channel_id=1, source_target_pairs={{0,1},{1,2},{2,3},{3,4},{4,5},{5,6},{6,7},{7,8},{8,9},{9,10},{10,1... | collective-permute-start | bytes 1572872 | tf_op jit(solution)/shard_map/ppermute | solution.py:356
  5.2 26.5 %front.1 = (bf16[1024,1024]{1,0:T(8,128)(2,1)}, bf16[256,1024]{1,0:T(8,128)(2,1)}, bf16[256,1024]{1,0:T(8,128)(2,1)}, bf16[256,1024]{1,0:T(8,128)(2,1)}, bf16[25...) custom-call(bf16[1024,1024]{1,0:T(8,128)(2,1)} %bitcast.17, ...), custom_call_target="tpu_custom_call" | custom-call | flops 100000000 | bytes 100000 | tf_op jit(solution)/shard_map/front/pallas_call | solution.py:191
  31.7 1.3 collective-permute-start.1
  33.0 0.0 collective-permute-done.xl_ref
  33.1 0.8 copy-done.4
  33.9 15.8 %first_block.1 = (bf16[1024,1024]{1,0:T(8,128)(2,1)}, bf16[256,1024]{1,0:T(8,128)(2,1)}, bf16[256,1024]{1,0:T(8,128)(2,1)}, bf16[512,2048]{1,0:T(8,128)(2,1)}, bf16[512,2048]{1,0:T(8,128)(2,1)}) custom-call(s32[1]{0:T(128)} %bitcast.core_ref, f32[1]{0:T(128)} %bitcast.1.bias_ref, bf16[256,1024]{1,0:T(8,128)(2,1)} %get-tuple-element.38.q_ref, ...), custom_call_target="tpu_custom_call" | custom-call | flops 100000000 | bytes 100000 | tf_op jit(solution)/shard_map/first_block/pallas_call | solution.py:260
  49.7 0.0 collective-permute-done.1.xn_ref
  49.7 0.1 collective-permute-start.2
  49.8 0.0 copy-done.9
  49.8 1.3 collective-permute-start.3
  51.1 3.0 %collective-permute-done.2 = bf16[512,2048]{1,0:T(8,128)(2,1)S(1)} collective-permute-done((bf16[512,2048]{1,0:T(8,128)(2,1)}, bf16[512,2048]{1,0:T(8,128)(2,1)S(1)}, u32[]{:S(2)}, u32[]{:S(2)}) %collective-permute-start.2) | collective-permute-done | bytes 2097184 | tf_op jit(solution)/shard_map/ppermute | solution.py:341
  54.1 3.7 %add_convert_fusion.2 = bf16[512,2048]{1,0:T(8,128)(2,1)} fusion(bf16[512,2048]{1,0:T(8,128)(2,1)S(1)} %collective-permute-done.2, bf16[512,2048]{1,0:T(8,128)(2,1)} %get-tuple-element.50), kind=kLoop, calls=%fused_computation.4 | loop fusion | flops 4194304 | bytes 6291456 | tf_op jit(solution)/shard_map/convert_element_type | solution.py:33
  57.8 13.9 %all-to-all-start = ((bf16[64,8,2048]{2,1,0:T(8,128)(2,1)}), bf16[64,8,2048]{2,1,0:T(8,128)(2,1)}, u32[]{:S(2)}, u32[]{:S(2)}) async-start(bf16[64,8,2048]{2,1,0:T(8,128)(2,1)} %bitcast.6), calls=%async_computation | async-start | bytes 4194304 | tf_op jit(solution)/shard_map/all_to_all | solution.py:378
  71.7 0.0 collective-permute-done.3.gn_ref
  71.8 0.8 copy-done.6
  72.5 16.8 %last_block.1 = (bf16[1024,1024]{1,0:T(8,128)(2,1)}, bf16[1024,1024]{1,0:T(8,128)(2,1)}, bf16[256,2048]{1,0:T(8,128)(2,1)}, bf16[256,2048]{1,0:T(8,128)(2,1)}, bf16[512,2048]{1,0:T(8,128)(2,1)}) custom-call(s32[1]{0:T(128)} %bitcast.core_ref, bf16[256,1024]{1,0:T(8,128)(2,1)} %copy-done.5, bf16[256,1024]{1,0:T(8,128)(2,1)} %copy-done.6, ...), custom_call_target="tpu_custom_call" | custom-call | flops 100000000 | bytes 100000 | tf_op jit(solution)/shard_map/last_block/pallas_call | solution.py:325
  89.4 0.1 collective-permute-start.4
  89.5 0.5 collective-permute-start.5
  90.0 6.0 %fusion.4 = f32[1024,1024]{1,0:T(8,128)} fusion(bf16[1024,1024]{1,0:T(8,128)(2,1)} %get-tuple-element.67, bf16[1024,1024]{1,0:T(8,128)(2,1)S(1)} %copy-done.2), kind=kOutput, calls=%fused_computation.11 | convolution fusion | flops 2147483648 | bytes 8388608 | tf_op jit(solution)/shard_map/dot_general | solution.py:21
  95.9 0.0 collective-permute-done.4
  96.0 0.0 collective-permute-done.5
  96.0 2.3 %fusion.1 = bf16[64,8,2048]{2,1,0:T(8,128)(2,1)} fusion(bf16[512,2048]{1,0:T(8,128)(2,1)S(1)} %copy-done.3, bf16[256,2048]{1,0:T(8,128)(2,1)S(1)} %collective-permute-done.5, bf16[256,2048]{1,0:T(8,128)(2,1)S(1)} %collective-permute-done.4), kind=kLoop, calls=%fused_computation.6 | loop fusion | flops 7340032 | bytes 6291456 | tf_op jit(solution)/shard_map/all_to_all | solution.py:385
  98.3 2.3 %all-to-all-done = bf16[64,8,2048]{2,1,0:T(8,128)(2,1)} async-done(((bf16[64,8,2048]{2,1,0:T(8,128)(2,1)}), bf16[64,8,2048]{2,1,0:T(8,128)(2,1)}, u32[]{:S(2)}, u32[]{:S(2)}) %all-to-all-start) | async-done | bytes 2097184 | tf_op jit(solution)/shard_map/all_to_all | solution.py:378
  100.6 8.5 %all-to-all-start.1 = ((bf16[64,8,2048]{2,1,0:T(8,128)(2,1)}), bf16[64,8,2048]{2,1,0:T(8,128)(2,1)}, u32[]{:S(2)}, u32[]{:S(2)}) async-start(bf16[64,8,2048]{2,1,0:T(8,128)(2,1)} %fusion.1), calls=%async_computation.1 | async-start | bytes 4194304 | tf_op jit(solution)/shard_map/all_to_all | solution.py:385
  109.1 0.0 copy-start.1
  109.1 4.1 %fusion.5 = f32[1024,1024]{1,0:T(8,128)S(1)} fusion(bf16[1024,1024]{1,0:T(8,128)(2,1)} %get-tuple-element.69, bf16[1024,1024]{1,0:T(8,128)(2,1)S(1)} %copy-done), kind=kOutput, calls=%fused_computation.12 | convolution fusion | flops 2147483648 | bytes 8388608 | tf_op jit(solution)/shard_map/dot_general | solution.py:21
  113.2 3.7 %fusion = bf16[1,1024,1024]{2,1,0:T(8,128)(2,1)} fusion(f32[1024,1024]{1,0:T(8,128)S(1)} %copy-done.10, f32[1024,1024]{1,0:T(8,128)S(1)} %fusion.5, bf16[1024,1024]{1,0:T(8,128)(2,1)S(1)} %copy-done.8, bf16[1024,1024]{1,0:T(8,128)(2,1)S(1)} %copy-done.1), kind=kOutput, calls=%fused_computation.5 | convolution fusion | flops 2150629376 | bytes 14680064 | tf_op jit(solution)/shard_map/dot_general | solution.py:21
  117.0 1.9 %convert_reduce_fusion.1 = f32[8,2048]{1,0:T(8,128)S(1)} fusion(bf16[64,8,2048]{2,1,0:T(8,128)(2,1)} %all-to-all-done), kind=kLoop, calls=%fused_computation.2 | loop fusion | flops 2080768 | bytes 2162688 | tf_op jit(solution)/shard_map/reduce_sum | solution.py:348
  118.9 18.9 %all-to-all-done.1 = bf16[64,8,2048]{2,1,0:T(8,128)(2,1)} async-done(((bf16[64,8,2048]{2,1,0:T(8,128)(2,1)}), bf16[64,8,2048]{2,1,0:T(8,128)(2,1)}, u32[]{:S(2)}, u32[]{:S(2)}) %all-to-all-start.1) | async-done | bytes 2097184 | tf_op jit(solution)/shard_map/all_to_all | solution.py:385
  137.8 1.9 %convert_reduce_fusion = f32[8,2048]{1,0:T(8,128)S(1)} fusion(bf16[64,8,2048]{2,1,0:T(8,128)(2,1)} %all-to-all-done.1), kind=kLoop, calls=%fused_computation | loop fusion | flops 2080768 | bytes 2162688 | tf_op jit(solution)/shard_map/reduce_sum | solution.py:348
  139.7 0.7 fusion.2
  (19 shorter events, 0.0 us)
Async XLA Ops:
  1.7 31.3 %collective-permute-start = (bf16[256,1024]{1,0:T(8,128)(2,1)S(1)}, bf16[256,1024]{1,0:T(8,128)(2,1)S(1)}, u32[]{:S(2)}, u32[]{:S(2)}) collective-permute-start(bf16[256,1024]{1,0:T(8,128)(2,1)S(1)} %slice_bitcast_fusion), channel_id=1, source_target_pairs={{0,1},{1,2},{2,3},{3,4},{4,5},{5,6},{6,7},{7,8},{8,9},{9,10},{10,1... | collective-permute-start | bytes 1572872 | tf_op jit(solution)/shard_map/ppermute | solution.py:356
  31.7 17.9 %collective-permute-start.1 = (bf16[256,1024]{1,0:T(8,128)(2,1)}, bf16[256,1024]{1,0:T(8,128)(2,1)S(1)}, u32[]{:S(2)}, u32[]{:S(2)}) collective-permute-start(bf16[256,1024]{1,0:T(8,128)(2,1)} %get-tuple-element.48), channel_id=1, source_target_pairs={{1,0},{2,1},{3,2},{4,3},{5,4},{6,5},{7,6},{8,7},{9,8},{10,9},{11,1... | collective-permute-start | bytes 1572872 | tf_op jit(solution)/shard_map/ppermute | solution.py:356
  33.1 0.8 copy-start.4
  33.9 15.9 %copy-start.9 = (bf16[256,1024]{1,0:T(8,128)(2,1)S(1)}, bf16[256,1024]{1,0:T(8,128)(2,1)}, u32[]{:S(2)}) copy-start(bf16[256,1024]{1,0:T(8,128)(2,1)} %get-tuple-element.53) | copy-start | bytes 1572868
  49.7 8.2 %copy-start.5 = (bf16[256,1024]{1,0:T(8,128)(2,1)}, bf16[256,1024]{1,0:T(8,128)(2,1)S(1)}, u32[]{:S(2)}) copy-start(bf16[256,1024]{1,0:T(8,128)(2,1)S(1)} %collective-permute-done.1.xn_ref) | copy-start | bytes 1572868
  49.7 4.5 %collective-permute-start.2 = (bf16[512,2048]{1,0:T(8,128)(2,1)}, bf16[512,2048]{1,0:T(8,128)(2,1)S(1)}, u32[]{:S(2)}, u32[]{:S(2)}) collective-permute-start(bf16[512,2048]{1,0:T(8,128)(2,1)} %get-tuple-element.51), channel_id=1, source_target_pairs={{0,32},{32,0},{1,33},{33,1},{2,34},{34,2},{3,35},{35,3},{4,36},{36... | collective-permute-start | bytes 6291464 | tf_op jit(solution)/shard_map/ppermute | solution.py:341
  49.8 22.0 %collective-permute-start.3 = (bf16[256,1024]{1,0:T(8,128)(2,1)S(1)}, bf16[256,1024]{1,0:T(8,128)(2,1)S(1)}, u32[]{:S(2)}, u32[]{:S(2)}) collective-permute-start(bf16[256,1024]{1,0:T(8,128)(2,1)S(1)} %copy-done.9), channel_id=1, source_target_pairs={{1,0},{2,1},{3,2},{4,3},{5,4},{6,5},{7,6},{8,7},{9,8},{10,9},{11,1... | collective-permute-start | bytes 1572872 | tf_op jit(solution)/shard_map/ppermute | solution.py:356
  57.8 42.7 %all-to-all-start = ((bf16[64,8,2048]{2,1,0:T(8,128)(2,1)}), bf16[64,8,2048]{2,1,0:T(8,128)(2,1)}, u32[]{:S(2)}, u32[]{:S(2)}) async-start(bf16[64,8,2048]{2,1,0:T(8,128)(2,1)} %bitcast.6), calls=%async_computation | async-start | bytes 4194304 | tf_op jit(solution)/shard_map/all_to_all | solution.py:378
  71.7 0.8 copy-start.6
  72.5 17.5 %copy-start.2 = (bf16[1024,1024]{1,0:T(8,128)(2,1)S(1)}, bf16[1024,1024]{1,0:T(8,128)(2,1)}, u32[]{:S(2)}) copy-start(bf16[1024,1024]{1,0:T(8,128)(2,1)} %wq_ref.3) | copy-start | bytes 6291460
  89.4 6.6 %copy-start.3 = (bf16[512,2048]{1,0:T(8,128)(2,1)S(1)}, bf16[512,2048]{1,0:T(8,128)(2,1)}, u32[]{:S(2)}) copy-start(bf16[512,2048]{1,0:T(8,128)(2,1)} %get-tuple-element.71) | copy-start | bytes 6291460
  89.4 6.5 %collective-permute-start.4 = (bf16[256,2048]{1,0:T(8,128)(2,1)}, bf16[256,2048]{1,0:T(8,128)(2,1)S(1)}, u32[]{:S(2)}, u32[]{:S(2)}) collective-permute-start(bf16[256,2048]{1,0:T(8,128)(2,1)} %get-tuple-element.65), channel_id=1, source_target_pairs={{0,32},{32,0},{1,33},{33,1},{2,34},{34,2},{3,35},{35,3},{4,36},{36... | collective-permute-start | bytes 3145736 | tf_op jit(solution)/shard_map/ppermute | solution.py:341
  89.5 6.5 %collective-permute-start.5 = (bf16[256,2048]{1,0:T(8,128)(2,1)}, bf16[256,2048]{1,0:T(8,128)(2,1)S(1)}, u32[]{:S(2)}, u32[]{:S(2)}) collective-permute-start(bf16[256,2048]{1,0:T(8,128)(2,1)} %get-tuple-element.66), channel_id=1, source_target_pairs={{0,32},{32,0},{1,33},{33,1},{2,34},{34,2},{3,35},{35,3},{4,36},{36... | collective-permute-start | bytes 3145736 | tf_op jit(solution)/shard_map/ppermute | solution.py:341
  98.3 10.8 %copy-start = (bf16[1024,1024]{1,0:T(8,128)(2,1)S(1)}, bf16[1024,1024]{1,0:T(8,128)(2,1)}, u32[]{:S(2)}) copy-start(bf16[1024,1024]{1,0:T(8,128)(2,1)} %wk_ref.5) | copy-start | bytes 6291460
  100.6 37.3 %all-to-all-start.1 = ((bf16[64,8,2048]{2,1,0:T(8,128)(2,1)}), bf16[64,8,2048]{2,1,0:T(8,128)(2,1)}, u32[]{:S(2)}, u32[]{:S(2)}) async-start(bf16[64,8,2048]{2,1,0:T(8,128)(2,1)} %fusion.1), calls=%async_computation.1 | async-start | bytes 4194304 | tf_op jit(solution)/shard_map/all_to_all | solution.py:385
  109.1 4.2 %copy-start.1 = (bf16[1024,1024]{1,0:T(8,128)(2,1)S(1)}, bf16[1024,1024]{1,0:T(8,128)(2,1)}, u32[]{:S(2)}) copy-start(bf16[1024,1024]{1,0:T(8,128)(2,1)} %wv_ref.5) | copy-start | bytes 6291460
  109.1 4.1 %copy-start.8 = (bf16[1024,1024]{1,0:T(8,128)(2,1)S(1)}, bf16[1024,1024]{1,0:T(8,128)(2,1)}, u32[]{:S(2)}) copy-start(bf16[1024,1024]{1,0:T(8,128)(2,1)} %get-tuple-element.70) | copy-start | bytes 6291460
  109.1 4.1 %copy-start.10 = (f32[1024,1024]{1,0:T(8,128)S(1)}, f32[1024,1024]{1,0:T(8,128)}, u32[]{:S(2)}) copy-start(f32[1024,1024]{1,0:T(8,128)} %fusion.4) | copy-start | bytes 12582916
  117.0 22.8 %copy-start.7 = (f32[8,4096]{1,0:T(8,128)S(1)}, f32[8,4096]{1,0:T(8,128)}, u32[]{:S(2)}) copy-start(f32[8,4096]{1,0:T(8,128)} %param.13) | copy-start | bytes 393220

commit v8 on v7

--- a/solution.py
+++ b/solution.py
@@ -23,6 +23,7 @@
 
 SMALL = pl.CostEstimate(flops=10**8, bytes_accessed=10**5, transcendentals=0)
 VMEM = 60 * 2**20
+ROOM = 57 * 2**20
 PAIR = 2 * HD
 FOUR = 4 * HD
 HALF = WIN // 2
@@ -254,8 +255,8 @@
     full = pl.BlockSpec((count, FOUR), lambda j, c: (0, j))
     left = pl.BlockSpec((WIN, width), lambda j, c: (0, 0))
     column = pl.BlockSpec((width, FOUR), lambda j, c: (0, j))
-    sums = pl.BlockSpec((width // 2, 2 * width), lambda j, c: (0, 0))
-    both = jax.ShapeDtypeStruct((width // 2, 2 * width), BF16)
+    sums = pl.BlockSpec(memory_space=pltpu.VMEM)
+    both = pltpu.VMEM((width // 2, 2 * width), BF16)
     part = jax.ShapeDtypeStruct((WIN, width), BF16)
     return pl.pallas_call(
         first_kernel,
@@ -275,7 +276,7 @@
             ],
         ),
         out_shape=[jax.ShapeDtypeStruct((count, width), BF16), part, part, both, both],
-        compiler_params=pltpu.CompilerParams(vmem_limit_bytes=VMEM),
+        compiler_params=pltpu.CompilerParams(vmem_limit_bytes=ROOM),
         cost_estimate=SMALL,
         name="first_block",
     )(core, bias, *own, *partial, *late, tokens_l, w_key, w_value, *[turned] * 4, out_grad)
@@ -317,11 +318,11 @@
     near = pl.BlockSpec((WIN, width), lambda j, c: (0, 0))
     mid = pl.BlockSpec((count - 2 * WIN, FOUR), lambda j, c: (0, j))
     full = pl.BlockSpec((count, FOUR), lambda j, c: (0, j))
-    sums = pl.BlockSpec((width // 2, 2 * width), lambda j, c: (0, 0))
+    sums = pl.BlockSpec(memory_space=pltpu.VMEM)
     grad = jax.ShapeDtypeStruct((count, width), BF16)
-    both = jax.ShapeDtypeStruct((width // 2, 2 * width), BF16)
-    half = pl.BlockSpec((width // 4, 2 * width), lambda j, c: (0, 0))
-    part_sum = jax.ShapeDtypeStruct((width // 4, 2 * width), BF16)
+    both = pltpu.VMEM((width // 2, 2 * width), BF16)
+    half = pl.BlockSpec(memory_space=pltpu.VMEM)
+    part_sum = pltpu.VMEM((width // 4, 2 * width), BF16)
     return pl.pallas_call(
         last_kernel,
         grid_spec=pltpu.PrefetchScalarGridSpec(
@@ -331,7 +332,7 @@
             out_specs=[full, full, half, half, sums],
         ),
         out_shape=[grad, grad, part_sum, part_sum, both],
-        compiler_params=pltpu.CompilerParams(vmem_limit_bytes=VMEM),
+        compiler_params=pltpu.CompilerParams(vmem_limit_bytes=ROOM),
         cost_estimate=SMALL,
         name="last_block",
     )(core, tokens_n, grads_n, *weights, *last, *partial, *first, *middle, *[turned] * 4)

time: 141 us -> 139 us (0.986)
  Pallas kernels: 59.1 us -> 55.9 us
  starting transfers between devices: 29.1 us -> 30.8 us
  other arithmetic: 10.5 us -> 9.02 us
    pallas_call x1, Pallas kernels: 15.8 us -> 14.1 us  [first_block(): pl.pallas_call(first_kernel, grid_spec=pltpu.PrefetchScalarGridSpec(num_s...]
    all_to_all x1, starting transfers between devices: 8.5 us -> 10.2 us  [on_device(): pieces_kv = lax.all_to_all(both, CHIPS, 0, 0, tiled=True)]
    pallas_call x1, Pallas kernels: 16.8 us -> 15.2 us  [last_block(): pl.pallas_call(last_kernel, grid_spec=pltpu.PrefetchScalarGridSpec(num_sc...]
    all_to_all x1, waiting for transfers between devices: 2.28 us -> 3.83 us  [on_device(): pieces_qo = lax.all_to_all(both, CHIPS, 0, 0, tiled=True)]
    convert_element_type x1, other arithmetic: 3.71 us -> 2.2 us  [bf(): return value.astype(BF16)]
  transfers between devices with their start and end apart: 8 -> 8, of which waited for: 3 -> 3; matrix products, arithmetic and copies ran while one was open for 15% -> 15% of each run, Pallas kernels for 42% -> 40%
where the time goes in v8:
time: 139 us
  Pallas kernels  55.9 us (40%)
  starting transfers between devices  30.8 us (22%)
  waiting for transfers between devices  25.6 us (18%)
  matrix products  13.8 us (10%)
  other arithmetic  9.02 us (6%)
  local copies, waits for them, and re-layouts  2.74 us (2%)
    pallas_call x1, Pallas kernels, front(): pl.pallas_call(front_kernel, grid=(width // PAIR,), in_specs=[whole, whol...  26.6 us
    all_to_all x1, waiting for transfers between devices, on_device(): pieces_kv = lax.all_to_all(both, CHIPS, 0, 0, tiled=True)  18.9 us
    pallas_call x1, Pallas kernels, last_block(): pl.pallas_call(last_kernel, grid_spec=pltpu.PrefetchScalarGridSpec(num_sc...  15.2 us
    pallas_call x1, Pallas kernels, first_block(): pl.pallas_call(first_kernel, grid_spec=pltpu.PrefetchScalarGridSpec(num_s...  14.1 us
    all_to_all x1, starting transfers between devices, on_device(): pieces_qo = lax.all_to_all(both, CHIPS, 0, 0, tiled=True)  13.9 us
    dot_general x3, matrix products, dot(): lax.dot_general(a, b, (((ca,), (cb,)), ((), ())), preferred_element_type=...  13.8 us
    all_to_all x1, starting transfers between devices, on_device(): pieces_kv = lax.all_to_all(both, CHIPS, 0, 0, tiled=True)  10.2 us
    ppermute x3, starting transfers between devices, passed_along(): return lax.ppermute(block, SEQ, route)  6.1 us
  transfers between devices with their start and end apart: 8, of which 3 were waited for; matrix products, arithmetic and copies ran while one was open for 15% of the time, Pallas kernels for 40%

profile of v8, /device:TPU:0, one launch (start us, length us, event | category | flops | bytes accessed | tf_op | source)
XLA Modules:
  0.0 138.7 jit_solution(18219896336205963893)
XLA Ops:
  0.6 1.1 slice_bitcast_fusion
  1.7 3.5 %collective-permute-start = (bf16[256,1024]{1,0:T(8,128)(2,1)S(1)}, bf16[256,1024]{1,0:T(8,128)(2,1)S(1)}, u32[]{:S(2)}, u32[]{:S(2)}) collective-permute-start(bf16[256,1024]{1,0:T(8,128)(2,1)S(1)} %slice_bitcast_fusion), channel_id=1, source_target_pairs={{0,1},{1,2},{2,3},{3,4},{4,5},{5,6},{6,7},{7,8},{8,9},{9,10},{10,1... | collective-permute-start | bytes 1572872 | tf_op jit(solution)/shard_map/ppermute | solution.py:357
  5.2 26.6 %front.1 = (bf16[1024,1024]{1,0:T(8,128)(2,1)}, bf16[256,1024]{1,0:T(8,128)(2,1)}, bf16[256,1024]{1,0:T(8,128)(2,1)}, bf16[256,1024]{1,0:T(8,128)(2,1)}, bf16[25...) custom-call(bf16[1024,1024]{1,0:T(8,128)(2,1)} %bitcast.17, ...), custom_call_target="tpu_custom_call" | custom-call | flops 100000000 | bytes 100000 | tf_op jit(solution)/shard_map/front/pallas_call | solution.py:192
  31.8 1.3 collective-permute-start.1
  33.1 0.0 collective-permute-done.xl_ref
  33.2 0.8 copy-done.3
  33.9 14.1 %first_block.1 = (bf16[1024,1024]{1,0:T(8,128)(2,1)}, bf16[256,1024]{1,0:T(8,128)(2,1)}, bf16[256,1024]{1,0:T(8,128)(2,1)}, bf16[512,2048]{1,0:T(8,128)(2,1)S(1)}, bf16[512,2048]{1,0:T(8,128)(2,1)S(1)}) custom-call(s32[1]{0:T(128)} %bitcast.core_ref, f32[1]{0:T(128)} %bitcast.1.bias_ref, bf16[256,1024]{1,0:T(8,128)(2,1)} %get-tuple-element.38.q_ref, ...), custom_call_target="tpu_custom_call" | custom-call | flops 100000000 | bytes 100000 | tf_op jit(solution)/shard_map/first_block/pallas_call | solution.py:261
  48.0 0.0 collective-permute-done.1.xn_ref
  48.0 0.1 collective-permute-start.2
  48.1 1.3 collective-permute-start.3
  49.4 2.8 %collective-permute-done.2 = bf16[512,2048]{1,0:T(8,128)(2,1)S(1)} collective-permute-done((bf16[512,2048]{1,0:T(8,128)(2,1)S(1)}, bf16[512,2048]{1,0:T(8,128)(2,1)S(1)}, u32[]{:S(2)}, u32[]{:S(2)}) %collective-permute-start.2) | collective-permute-done | bytes 2097184 | tf_op jit(solution)/shard_map/ppermute | solution.py:342
  52.3 2.2 %add_convert_fusion.2 = bf16[512,2048]{1,0:T(8,128)(2,1)} fusion(bf16[512,2048]{1,0:T(8,128)(2,1)S(1)} %collective-permute-done.2, bf16[512,2048]{1,0:T(8,128)(2,1)S(1)} %get-tuple-element.50), kind=kLoop, calls=%fused_computation.4 | loop fusion | flops 4194304 | bytes 6291456 | tf_op jit(solution)/shard_map/convert_element_type | solution.py:34
  54.5 13.9 %all-to-all-start = ((bf16[64,8,2048]{2,1,0:T(8,128)(2,1)}), bf16[64,8,2048]{2,1,0:T(8,128)(2,1)}, u32[]{:S(2)}, u32[]{:S(2)}) async-start(bf16[64,8,2048]{2,1,0:T(8,128)(2,1)} %bitcast.6), calls=%async_computation | async-start | bytes 4194304 | tf_op jit(solution)/shard_map/all_to_all | solution.py:379
  68.4 0.0 collective-permute-done.3.gn_ref
  68.4 0.8 copy-done.5
  69.2 15.2 %last_block.1 = (bf16[1024,1024]{1,0:T(8,128)(2,1)}, bf16[1024,1024]{1,0:T(8,128)(2,1)}, bf16[256,2048]{1,0:T(8,128)(2,1)S(1)}, bf16[256,2048]{1,0:T(8,128)(2,1)S(1)}, bf16[512,2048]{1,0:T(8,128)(2,1)S(1)}) custom-call(s32[1]{0:T(128)} %bitcast.core_ref, bf16[256,1024]{1,0:T(8,128)(2,1)} %copy-done.4, bf16[256,1024]{1,0:T(8,128)(2,1)} %copy-done.5, ...), custom_call_target="tpu_custom_call" | custom-call | flops 100000000 | bytes 100000 | tf_op jit(solution)/shard_map/last_block/pallas_call | solution.py:326
  84.5 0.1 collective-permute-start.4
  84.6 0.5 collective-permute-start.5
  85.1 0.0 copy-done.2
  85.1 6.0 %fusion.4 = f32[1024,1024]{1,0:T(8,128)} fusion(bf16[1024,1024]{1,0:T(8,128)(2,1)} %get-tuple-element.67, bf16[1024,1024]{1,0:T(8,128)(2,1)S(1)} %copy-done.2), kind=kOutput, calls=%fused_computation.11 | convolution fusion | flops 2147483648 | bytes 8388608 | tf_op jit(solution)/shard_map/dot_general | solution.py:21
  91.1 0.0 collective-permute-done.4
  91.1 0.0 collective-permute-done.5
  91.1 2.3 %fusion.1 = bf16[64,8,2048]{2,1,0:T(8,128)(2,1)} fusion(bf16[512,2048]{1,0:T(8,128)(2,1)S(1)} %get-tuple-element.71, bf16[256,2048]{1,0:T(8,128)(2,1)S(1)} %collective-permute-done.5, bf16[256,2048]{1,0:T(8,128)(2,1)S(1)} %collective-permute-done.4), kind=kLoop, calls=%fused_computation.6 | loop fusion | flops 7340032 | bytes 6291456 | tf_op jit(solution)/shard_map/all_to_all | solution.py:386
  93.4 3.8 %all-to-all-done = bf16[64,8,2048]{2,1,0:T(8,128)(2,1)} async-done(((bf16[64,8,2048]{2,1,0:T(8,128)(2,1)}), bf16[64,8,2048]{2,1,0:T(8,128)(2,1)}, u32[]{:S(2)}, u32[]{:S(2)}) %all-to-all-start) | async-done | bytes 2097184 | tf_op jit(solution)/shard_map/all_to_all | solution.py:379
  97.2 10.2 %all-to-all-start.1 = ((bf16[64,8,2048]{2,1,0:T(8,128)(2,1)}), bf16[64,8,2048]{2,1,0:T(8,128)(2,1)}, u32[]{:S(2)}, u32[]{:S(2)}) async-start(bf16[64,8,2048]{2,1,0:T(8,128)(2,1)} %fusion.1), calls=%async_computation.1 | async-start | bytes 4194304 | tf_op jit(solution)/shard_map/all_to_all | solution.py:386
  107.4 0.0 copy-start.1
  107.4 4.1 %fusion.5 = f32[1024,1024]{1,0:T(8,128)S(1)} fusion(bf16[1024,1024]{1,0:T(8,128)(2,1)} %get-tuple-element.69, bf16[1024,1024]{1,0:T(8,128)(2,1)S(1)} %copy-done), kind=kOutput, calls=%fused_computation.12 | convolution fusion | flops 2147483648 | bytes 8388608 | tf_op jit(solution)/shard_map/dot_general | solution.py:21
  111.6 3.7 %fusion = bf16[1,1024,1024]{2,1,0:T(8,128)(2,1)} fusion(f32[1024,1024]{1,0:T(8,128)S(1)} %copy-done.8, f32[1024,1024]{1,0:T(8,128)S(1)} %fusion.5, bf16[1024,1024]{1,0:T(8,128)(2,1)S(1)} %copy-done.7, bf16[1024,1024]{1,0:T(8,128)(2,1)S(1)} %copy-done.1), kind=kOutput, calls=%fused_computation.5 | convolution fusion | flops 2150629376 | bytes 14680064 | tf_op jit(solution)/shard_map/dot_general | solution.py:21
  115.3 1.9 %convert_reduce_fusion.1 = f32[8,2048]{1,0:T(8,128)S(1)} fusion(bf16[64,8,2048]{2,1,0:T(8,128)(2,1)} %all-to-all-done), kind=kLoop, calls=%fused_computation.2 | loop fusion | flops 2080768 | bytes 2162688 | tf_op jit(solution)/shard_map/reduce_sum | solution.py:349
  117.2 18.9 %all-to-all-done.1 = bf16[64,8,2048]{2,1,0:T(8,128)(2,1)} async-done(((bf16[64,8,2048]{2,1,0:T(8,128)(2,1)}), bf16[64,8,2048]{2,1,0:T(8,128)(2,1)}, u32[]{:S(2)}, u32[]{:S(2)}) %all-to-all-start.1) | async-done | bytes 2097184 | tf_op jit(solution)/shard_map/all_to_all | solution.py:386
  136.1 1.9 %convert_reduce_fusion = f32[8,2048]{1,0:T(8,128)S(1)} fusion(bf16[64,8,2048]{2,1,0:T(8,128)(2,1)} %all-to-all-done.1), kind=kLoop, calls=%fused_computation | loop fusion | flops 2080768 | bytes 2162688 | tf_op jit(solution)/shard_map/reduce_sum | solution.py:349
  138.0 0.7 fusion.2
  (15 shorter events, 0.0 us)
Async XLA Ops:
  1.7 31.4 %collective-permute-start = (bf16[256,1024]{1,0:T(8,128)(2,1)S(1)}, bf16[256,1024]{1,0:T(8,128)(2,1)S(1)}, u32[]{:S(2)}, u32[]{:S(2)}) collective-permute-start(bf16[256,1024]{1,0:T(8,128)(2,1)S(1)} %slice_bitcast_fusion), channel_id=1, source_target_pairs={{0,1},{1,2},{2,3},{3,4},{4,5},{5,6},{6,7},{7,8},{8,9},{9,10},{10,1... | collective-permute-start | bytes 1572872 | tf_op jit(solution)/shard_map/ppermute | solution.py:357
  31.8 16.2 %collective-permute-start.1 = (bf16[256,1024]{1,0:T(8,128)(2,1)}, bf16[256,1024]{1,0:T(8,128)(2,1)S(1)}, u32[]{:S(2)}, u32[]{:S(2)}) collective-permute-start(bf16[256,1024]{1,0:T(8,128)(2,1)} %get-tuple-element.48), channel_id=1, source_target_pairs={{1,0},{2,1},{3,2},{4,3},{5,4},{6,5},{7,6},{8,7},{9,8},{10,9},{11,1... | collective-permute-start | bytes 1572872 | tf_op jit(solution)/shard_map/ppermute | solution.py:357
  33.2 0.8 copy-start.3
  48.0 6.5 %copy-start.4 = (bf16[256,1024]{1,0:T(8,128)(2,1)}, bf16[256,1024]{1,0:T(8,128)(2,1)S(1)}, u32[]{:S(2)}) copy-start(bf16[256,1024]{1,0:T(8,128)(2,1)S(1)} %collective-permute-done.1.xn_ref) | copy-start | bytes 1572868
  48.0 4.2 %collective-permute-start.2 = (bf16[512,2048]{1,0:T(8,128)(2,1)S(1)}, bf16[512,2048]{1,0:T(8,128)(2,1)S(1)}, u32[]{:S(2)}, u32[]{:S(2)}) collective-permute-start(bf16[512,2048]{1,0:T(8,128)(2,1)S(1)} %get-tuple-element.51), channel_id=1, source_target_pairs={{0,32},{32,0},{1,33},{33,1},{2,34},{34,2},{3,35},{35,3},{4,36},{36... | collective-permute-start | bytes 6291464 | tf_op jit(solution)/shard_map/ppermute | solution.py:342
  48.1 20.2 %collective-permute-start.3 = (bf16[256,1024]{1,0:T(8,128)(2,1)}, bf16[256,1024]{1,0:T(8,128)(2,1)S(1)}, u32[]{:S(2)}, u32[]{:S(2)}) collective-permute-start(bf16[256,1024]{1,0:T(8,128)(2,1)} %get-tuple-element.53), channel_id=1, source_target_pairs={{1,0},{2,1},{3,2},{4,3},{5,4},{6,5},{7,6},{8,7},{9,8},{10,9},{11,1... | collective-permute-start | bytes 1572872 | tf_op jit(solution)/shard_map/ppermute | solution.py:357
  54.5 42.7 %all-to-all-start = ((bf16[64,8,2048]{2,1,0:T(8,128)(2,1)}), bf16[64,8,2048]{2,1,0:T(8,128)(2,1)}, u32[]{:S(2)}, u32[]{:S(2)}) async-start(bf16[64,8,2048]{2,1,0:T(8,128)(2,1)} %bitcast.6), calls=%async_computation | async-start | bytes 4194304 | tf_op jit(solution)/shard_map/all_to_all | solution.py:379
  68.4 0.8 copy-start.5
  69.2 15.8 %copy-start.2 = (bf16[1024,1024]{1,0:T(8,128)(2,1)S(1)}, bf16[1024,1024]{1,0:T(8,128)(2,1)}, u32[]{:S(2)}) copy-start(bf16[1024,1024]{1,0:T(8,128)(2,1)} %wq_ref.3) | copy-start | bytes 6291460
  84.5 6.6 %collective-permute-start.4 = (bf16[256,2048]{1,0:T(8,128)(2,1)S(1)}, bf16[256,2048]{1,0:T(8,128)(2,1)S(1)}, u32[]{:S(2)}, u32[]{:S(2)}) collective-permute-start(bf16[256,2048]{1,0:T(8,128)(2,1)S(1)} %get-tuple-element.65), channel_id=1, source_target_pairs={{0,32},{32,0},{1,33},{33,1},{2,34},{34,2},{3,35},{35,3},{4,36},{36... | collective-permute-start | bytes 3145736 | tf_op jit(solution)/shard_map/ppermute | solution.py:342
  84.6 6.5 %collective-permute-start.5 = (bf16[256,2048]{1,0:T(8,128)(2,1)S(1)}, bf16[256,2048]{1,0:T(8,128)(2,1)S(1)}, u32[]{:S(2)}, u32[]{:S(2)}) collective-permute-start(bf16[256,2048]{1,0:T(8,128)(2,1)S(1)} %get-tuple-element.66), channel_id=1, source_target_pairs={{0,32},{32,0},{1,33},{33,1},{2,34},{34,2},{3,35},{35,3},{4,36},{36... | collective-permute-start | bytes 3145736 | tf_op jit(solution)/shard_map/ppermute | solution.py:342
  93.4 14.0 %copy-start = (bf16[1024,1024]{1,0:T(8,128)(2,1)S(1)}, bf16[1024,1024]{1,0:T(8,128)(2,1)}, u32[]{:S(2)}) copy-start(bf16[1024,1024]{1,0:T(8,128)(2,1)} %wk_ref.5) | copy-start | bytes 6291460
  97.2 38.9 %all-to-all-start.1 = ((bf16[64,8,2048]{2,1,0:T(8,128)(2,1)}), bf16[64,8,2048]{2,1,0:T(8,128)(2,1)}, u32[]{:S(2)}, u32[]{:S(2)}) async-start(bf16[64,8,2048]{2,1,0:T(8,128)(2,1)} %fusion.1), calls=%async_computation.1 | async-start | bytes 4194304 | tf_op jit(solution)/shard_map/all_to_all | solution.py:386
  107.4 4.1 %copy-start.1 = (bf16[1024,1024]{1,0:T(8,128)(2,1)S(1)}, bf16[1024,1024]{1,0:T(8,128)(2,1)}, u32[]{:S(2)}) copy-start(bf16[1024,1024]{1,0:T(8,128)(2,1)} %wv_ref.5) | copy-start | bytes 6291460
  107.4 4.1 %copy-start.7 = (bf16[1024,1024]{1,0:T(8,128)(2,1)S(1)}, bf16[1024,1024]{1,0:T(8,128)(2,1)}, u32[]{:S(2)}) copy-start(bf16[1024,1024]{1,0:T(8,128)(2,1)} %get-tuple-element.70) | copy-start | bytes 6291460
  107.4 4.1 %copy-start.8 = (f32[1024,1024]{1,0:T(8,128)S(1)}, f32[1024,1024]{1,0:T(8,128)}, u32[]{:S(2)}) copy-start(f32[1024,1024]{1,0:T(8,128)} %fusion.4) | copy-start | bytes 12582916
  115.3 22.8 %copy-start.6 = (f32[8,4096]{1,0:T(8,128)S(1)}, f32[8,4096]{1,0:T(8,128)}, u32[]{:S(2)}) copy-start(f32[8,4096]{1,0:T(8,128)} %param.13) | copy-start | bytes 393220

commit v9 on v8

--- a/solution.py
+++ b/solution.py
@@ -338,11 +338,9 @@
     )(core, tokens_n, grads_n, *weights, *last, *partial, *first, *middle, *[turned] * 4)
 
 
-def chip_sum(sends, keep, meanwhile=None):
+def chip_sum(sends, keep):
     got = [lax.ppermute(send, "co", [(0, 1), (1, 0)]) for send in sends]
-    if meanwhile is not None:
-        *got, meanwhile = lax.optimization_barrier((*got, meanwhile))
-    return bf(keep.astype(F32) + jnp.concatenate(got, axis=0).astype(F32)), meanwhile
+    return bf(keep.astype(F32) + jnp.concatenate(got, axis=0).astype(F32))
 
 
 def piece_sum(pieces, width):
@@ -375,21 +373,23 @@
         which, bias, own, partial_0, late, out_grad, tokens_l, w_key, w_value, turned
     )
     send, tokens_n = lax.optimization_barrier((send, tokens_n))
-    both, _ = chip_sum((send,), keep)
+    both = chip_sum((send,), keep)
     pieces_qo = lax.all_to_all(both, CHIPS, 0, 0, tiled=True)
     tokens_n, _ = lax.optimization_barrier((tokens_n, both))
     key_grad, value_grad, send_a, send_b, keep = last_block(
         which, tokens_n, grads_n, weights, last, partial_z, (key_0, value_0), middle, turned
     )
-    send_a, send_b, query_grad = lax.optimization_barrier((send_a, send_b, query_grad))
-    both, in_query = chip_sum((send_a, send_b), keep, dot(query_grad, w_query, 1, 1))
+    both = chip_sum((send_a, send_b), keep)
+    sum_qo = piece_sum(pieces_qo, 2 * width)
+    query_grad, both, sum_qo = lax.optimization_barrier((query_grad, both, sum_qo))
     pieces_kv = lax.all_to_all(both, CHIPS, 0, 0, tiled=True)
-    in_grad = bf(in_query + dot(key_grad, w_key, 1, 1) + dot(value_grad, w_value, 1, 1))
+    in_grad = bf(
+        dot(query_grad, w_query, 1, 1) + dot(key_grad, w_key, 1, 1) + dot(value_grad, w_value, 1, 1)
+    )
     total = count
     for axis in AXES:
         total *= lax.axis_size(axis)
     factor = 1.0 / total**0.5
-    sum_qo = piece_sum(pieces_qo, 2 * width)
     sum_kv = piece_sum(pieces_kv, 2 * width)
     summed = jnp.concatenate([sum_qo[:, :width], sum_kv, sum_qo[:, width:]], axis=1)
     return in_grad[None], grad_accum + summed * factor

time: 139 us -> 137 us (0.986)
  waiting for transfers between devices: 25.6 us -> 31.8 us
  matrix products: 13.8 us -> 10.2 us
  starting transfers between devices: 30.8 us -> 28.3 us
  other arithmetic: 9.02 us -> 7.36 us
    ppermute x3, waiting for transfers between devices: 2.85 us -> 6.49 us  [chip_sum(): got = [lax.ppermute(send, 'co', [(0, 1), (1, 0)]) for send in sends]]
    dot_general x3, matrix products: 13.8 us -> 10.2 us  [dot(): lax.dot_general(a, b, (((ca,), (cb,)), ((), ())), preferred_element_type=...]
    all_to_all x1, waiting for transfers between devices: 3.83 us -> 7.09 us  [on_device(): pieces_qo = lax.all_to_all(both, CHIPS, 0, 0, tiled=True)]
    all_to_all x1 -> x0, other arithmetic: 2.3 us -> none  [on_device(): pieces_kv = lax.all_to_all(both, CHIPS, 0, 0, tiled=True)]
    all_to_all x1, starting transfers between devices: 10.2 us -> 7.88 us  [on_device(): pieces_kv = lax.all_to_all(both, CHIPS, 0, 0, tiled=True)]
    convert_element_type x1 -> x2, other arithmetic: 2.2 us -> 4.47 us  [bf(): return value.astype(BF16)]
    reduce_sum x2, other arithmetic: 3.84 us -> 2.21 us  [piece_sum(): return jnp.sum(pieces.reshape(-1, 8, width).astype(F32), axis=0)]
  transfers between devices with their start and end apart: 8 -> 8, of which waited for: 3 -> 5; matrix products, arithmetic and copies ran while one was open for 15% -> 11% of each run, Pallas kernels for 40% -> 41%
where the time goes in v9:
time: 137 us; the launch traced here: 136 us
  Pallas kernels  55.9 us (41%)
  waiting for transfers between devices  31.8 us (23%)
  starting transfers between devices  28.3 us (21%)
  matrix products  10.2 us (7%)
  other arithmetic  7.36 us (5%)
  local copies, waits for them, and re-layouts  1.91 us (1%)
    pallas_call x1, Pallas kernels, front(): pl.pallas_call(front_kernel, grid=(width // PAIR,), in_specs=[whole, whol...  26.5 us
    all_to_all x1, waiting for transfers between devices, on_device(): pieces_kv = lax.all_to_all(both, CHIPS, 0, 0, tiled=True)  18.2 us
    pallas_call x1, Pallas kernels, last_block(): pl.pallas_call(last_kernel, grid_spec=pltpu.PrefetchScalarGridSpec(num_sc...  15.3 us
    pallas_call x1, Pallas kernels, first_block(): pl.pallas_call(first_kernel, grid_spec=pltpu.PrefetchScalarGridSpec(num_s...  14.1 us
    all_to_all x1, starting transfers between devices, on_device(): pieces_qo = lax.all_to_all(both, CHIPS, 0, 0, tiled=True)  13.6 us
    dot_general x3, matrix products, dot(): lax.dot_general(a, b, (((ca,), (cb,)), ((), ())), preferred_element_type=...  10.2 us
    all_to_all x1, starting transfers between devices, on_device(): pieces_kv = lax.all_to_all(both, CHIPS, 0, 0, tiled=True)  7.88 us
    all_to_all x1, waiting for transfers between devices, on_device(): pieces_qo = lax.all_to_all(both, CHIPS, 0, 0, tiled=True)  7.09 us
  transfers between devices with their start and end apart: 8, of which 5 were waited for; matrix products, arithmetic and copies ran while one was open for 11% of the time, Pallas kernels for 41%

profile of v9, /device:TPU:0, one launch (start us, length us, event | category | flops | bytes accessed | tf_op | source)
XLA Modules:
  0.0 136.2 jit_solution(8634393019543783185)
XLA Ops:
  0.6 1.1 slice_bitcast_fusion
  1.7 3.5 %collective-permute-start = (bf16[256,1024]{1,0:T(8,128)(2,1)S(1)}, bf16[256,1024]{1,0:T(8,128)(2,1)S(1)}, u32[]{:S(2)}, u32[]{:S(2)}) collective-permute-start(bf16[256,1024]{1,0:T(8,128)(2,1)S(1)} %slice_bitcast_fusion), channel_id=1, source_target_pairs={{0,1},{1,2},{2,3},{3,4},{4,5},{5,6},{6,7},{7,8},{8,9},{9,10},{10,1... | collective-permute-start | bytes 1572872 | tf_op jit(solution)/shard_map/ppermute | solution.py:355
  5.2 26.5 %front.1 = (bf16[1024,1024]{1,0:T(8,128)(2,1)}, bf16[256,1024]{1,0:T(8,128)(2,1)}, bf16[256,1024]{1,0:T(8,128)(2,1)}, bf16[256,1024]{1,0:T(8,128)(2,1)}, bf16[25...) custom-call(bf16[1024,1024]{1,0:T(8,128)(2,1)} %bitcast.16, ...), custom_call_target="tpu_custom_call" | custom-call | flops 100000000 | bytes 100000 | tf_op jit(solution)/shard_map/front/pallas_call | solution.py:192
  31.7 1.3 collective-permute-start.1
  33.0 0.0 collective-permute-done.xl_ref
  33.1 0.0 copy-start.3
  33.1 0.8 copy-done.3
  33.9 14.1 %first_block.1 = (bf16[1024,1024]{1,0:T(8,128)(2,1)}, bf16[256,1024]{1,0:T(8,128)(2,1)}, bf16[256,1024]{1,0:T(8,128)(2,1)}, bf16[512,2048]{1,0:T(8,128)(2,1)S(1)}, bf16[512,2048]{1,0:T(8,128)(2,1)S(1)}) custom-call(s32[1]{0:T(128)} %bitcast.core_ref, f32[1]{0:T(128)} %bitcast.1.bias_ref, bf16[256,1024]{1,0:T(8,128)(2,1)} %get-tuple-element.35.q_ref, ...), custom_call_target="tpu_custom_call" | custom-call | flops 100000000 | bytes 100000 | tf_op jit(solution)/shard_map/first_block/pallas_call | solution.py:261
  47.9 0.0 collective-permute-done.1.xn_ref
  47.9 0.1 collective-permute-start.2
  48.0 1.3 collective-permute-start.3
  49.3 2.8 %collective-permute-done.2 = bf16[512,2048]{1,0:T(8,128)(2,1)S(1)} collective-permute-done((bf16[512,2048]{1,0:T(8,128)(2,1)S(1)}, bf16[512,2048]{1,0:T(8,128)(2,1)S(1)}, u32[]{:S(2)}, u32[]{:S(2)}) %collective-permute-start.2) | collective-permute-done | bytes 2097184 | tf_op jit(solution)/shard_map/ppermute | solution.py:342
  52.2 2.1 %add_convert_fusion.2 = bf16[512,2048]{1,0:T(8,128)(2,1)} fusion(bf16[512,2048]{1,0:T(8,128)(2,1)S(1)} %collective-permute-done.2, bf16[512,2048]{1,0:T(8,128)(2,1)S(1)} %get-tuple-element.48), kind=kLoop, calls=%fused_computation.4 | loop fusion | flops 4194304 | bytes 6291456 | tf_op jit(solution)/shard_map/convert_element_type | solution.py:34
  54.3 13.6 %all-to-all-start = ((bf16[64,8,2048]{2,1,0:T(8,128)(2,1)}), bf16[64,8,2048]{2,1,0:T(8,128)(2,1)S(1)}, u32[]{:S(2)}, u32[]{:S(2)}) async-start(bf16[64,8,2048]{2,1,0:T(8,128)(2,1)} %bitcast.5), calls=%async_computation | async-start | bytes 4194304 | tf_op jit(solution)/shard_map/all_to_all | solution.py:377
  68.0 0.0 collective-permute-done.3.gn_ref
  68.0 15.3 %last_block.1 = (bf16[1024,1024]{1,0:T(8,128)(2,1)}, bf16[1024,1024]{1,0:T(8,128)(2,1)}, bf16[256,2048]{1,0:T(8,128)(2,1)S(1)}, bf16[256,2048]{1,0:T(8,128)(2,1)S(1)}, bf16[512,2048]{1,0:T(8,128)(2,1)S(1)}) custom-call(s32[1]{0:T(128)} %bitcast.core_ref, bf16[256,1024]{1,0:T(8,128)(2,1)} %copy-done.4, bf16[256,1024]{1,0:T(8,128)(2,1)} %collective-permute-done.3.gn_ref, ...), custom_call_target="tpu_custom_call" | custom-call | flops 100000000 | bytes 100000 | tf_op jit(solution)/shard_map/last_block/pallas_call | solution.py:326
  83.3 0.1 collective-permute-start.4
  83.4 0.5 collective-permute-start.5
  83.9 2.1 %collective-permute-done.4 = bf16[256,2048]{1,0:T(8,128)(2,1)S(1)} collective-permute-done((bf16[256,2048]{1,0:T(8,128)(2,1)S(1)}, bf16[256,2048]{1,0:T(8,128)(2,1)S(1)}, u32[]{:S(2)}, u32[]{:S(2)}) %collective-permute-start.4) | collective-permute-done | bytes 1048608 | tf_op jit(solution)/shard_map/ppermute | solution.py:342
  86.0 1.5 %collective-permute-done.5 = bf16[256,2048]{1,0:T(8,128)(2,1)S(1)} collective-permute-done((bf16[256,2048]{1,0:T(8,128)(2,1)S(1)}, bf16[256,2048]{1,0:T(8,128)(2,1)S(1)}, u32[]{:S(2)}, u32[]{:S(2)}) %collective-permute-start.5) | collective-permute-done | bytes 1048608 | tf_op jit(solution)/shard_map/ppermute | solution.py:342
  87.5 2.3 %add_convert_fusion.1 = bf16[512,2048]{1,0:T(8,128)(2,1)} fusion(bf16[512,2048]{1,0:T(8,128)(2,1)S(1)} %get-tuple-element.60, bf16[256,2048]{1,0:T(8,128)(2,1)S(1)} %collective-permute-done.5, bf16[256,2048]{1,0:T(8,128)(2,1)S(1)} %collective-permute-done.4), kind=kLoop, calls=%fused_computation.3 | loop fusion | flops 7340032 | bytes 6291456 | tf_op jit(solution)/shard_map/convert_element_type | solution.py:34
  89.8 7.1 %all-to-all-done = bf16[64,8,2048]{2,1,0:T(8,128)(2,1)S(1)} async-done(((bf16[64,8,2048]{2,1,0:T(8,128)(2,1)}), bf16[64,8,2048]{2,1,0:T(8,128)(2,1)S(1)}, u32[]{:S(2)}, u32[]{:S(2)}) %all-to-all-start) | async-done | bytes 2097184 | tf_op jit(solution)/shard_map/all_to_all | solution.py:377
  96.9 0.3 convert_reduce_fusion.1
  97.3 7.9 %all-to-all-start.1 = ((bf16[64,8,2048]{2,1,0:T(8,128)(2,1)}), bf16[64,8,2048]{2,1,0:T(8,128)(2,1)}, u32[]{:S(2)}, u32[]{:S(2)}) async-start(bf16[64,8,2048]{2,1,0:T(8,128)(2,1)} %bitcast.18), calls=%async_computation.1 | async-start | bytes 4194304 | tf_op jit(solution)/shard_map/all_to_all | solution.py:385
  105.2 0.0 copy-start.2
  105.2 4.1 %fusion.4 = f32[1024,1024]{1,0:T(8,128)S(1)} fusion(bf16[1024,1024]{1,0:T(8,128)(2,1)} %get-tuple-element.64, bf16[1024,1024]{1,0:T(8,128)(2,1)S(1)} %copy-done), kind=kOutput, calls=%fused_computation.11 | convolution fusion | flops 2147483648 | bytes 8388608 | tf_op jit(solution)/shard_map/dot_general | solution.py:21
  109.3 0.0 copy-start.1
  109.3 2.4 %fusion.3 = f32[1024,1024]{1,0:T(8,128)S(1)} fusion(bf16[1024,1024]{1,0:T(8,128)(2,1)S(1)} %copy-done.6, bf16[1024,1024]{1,0:T(8,128)(2,1)S(1)} %copy-done.2), kind=kOutput, calls=%fused_computation.10 | convolution fusion | flops 2147483648 | bytes 8388608 | tf_op jit(solution)/shard_map/dot_general | solution.py:21
  111.7 3.7 %fusion = bf16[1,1024,1024]{2,1,0:T(8,128)(2,1)} fusion(f32[1024,1024]{1,0:T(8,128)S(1)} %fusion.3, f32[1024,1024]{1,0:T(8,128)S(1)} %fusion.4, bf16[1024,1024]{1,0:T(8,128)(2,1)S(1)} %copy-done.7, bf16[1024,1024]{1,0:T(8,128)(2,1)S(1)} %copy-done.1), kind=kOutput, calls=%fused_computation.5 | convolution fusion | flops 2150629376 | bytes 14680064 | tf_op jit(solution)/shard_map/dot_general | solution.py:21
  115.5 18.2 %all-to-all-done.1 = bf16[64,8,2048]{2,1,0:T(8,128)(2,1)} async-done(((bf16[64,8,2048]{2,1,0:T(8,128)(2,1)}), bf16[64,8,2048]{2,1,0:T(8,128)(2,1)}, u32[]{:S(2)}, u32[]{:S(2)}) %all-to-all-start.1) | async-done | bytes 2097184 | tf_op jit(solution)/shard_map/all_to_all | solution.py:385
  133.6 1.9 %convert_reduce_fusion = f32[8,2048]{1,0:T(8,128)S(1)} fusion(bf16[64,8,2048]{2,1,0:T(8,128)(2,1)} %all-to-all-done.1), kind=kLoop, calls=%fused_computation | loop fusion | flops 2080768 | bytes 2162688 | tf_op jit(solution)/shard_map/reduce_sum | solution.py:347
  135.6 0.7 fusion.1
  (13 shorter events, 0.0 us)
Async XLA Ops:
  1.7 31.3 %collective-permute-start = (bf16[256,1024]{1,0:T(8,128)(2,1)S(1)}, bf16[256,1024]{1,0:T(8,128)(2,1)S(1)}, u32[]{:S(2)}, u32[]{:S(2)}) collective-permute-start(bf16[256,1024]{1,0:T(8,128)(2,1)S(1)} %slice_bitcast_fusion), channel_id=1, source_target_pairs={{0,1},{1,2},{2,3},{3,4},{4,5},{5,6},{6,7},{7,8},{8,9},{9,10},{10,1... | collective-permute-start | bytes 1572872 | tf_op jit(solution)/shard_map/ppermute | solution.py:355
  31.7 16.2 %collective-permute-start.1 = (bf16[256,1024]{1,0:T(8,128)(2,1)}, bf16[256,1024]{1,0:T(8,128)(2,1)S(1)}, u32[]{:S(2)}, u32[]{:S(2)}) collective-permute-start(bf16[256,1024]{1,0:T(8,128)(2,1)} %get-tuple-element.46), channel_id=1, source_target_pairs={{1,0},{2,1},{3,2},{4,3},{5,4},{6,5},{7,6},{8,7},{9,8},{10,9},{11,1... | collective-permute-start | bytes 1572872 | tf_op jit(solution)/shard_map/ppermute | solution.py:355
  33.1 0.8 copy-start.3
  47.9 6.4 %copy-start.4 = (bf16[256,1024]{1,0:T(8,128)(2,1)}, bf16[256,1024]{1,0:T(8,128)(2,1)S(1)}, u32[]{:S(2)}) copy-start(bf16[256,1024]{1,0:T(8,128)(2,1)S(1)} %collective-permute-done.1.xn_ref) | copy-start | bytes 1572868
  47.9 4.2 %collective-permute-start.2 = (bf16[512,2048]{1,0:T(8,128)(2,1)S(1)}, bf16[512,2048]{1,0:T(8,128)(2,1)S(1)}, u32[]{:S(2)}, u32[]{:S(2)}) collective-permute-start(bf16[512,2048]{1,0:T(8,128)(2,1)S(1)} %get-tuple-element.49), channel_id=1, source_target_pairs={{0,32},{32,0},{1,33},{33,1},{2,34},{34,2},{3,35},{35,3},{4,36},{36... | collective-permute-start | bytes 6291464 | tf_op jit(solution)/shard_map/ppermute | solution.py:342
  48.0 19.9 %collective-permute-start.3 = (bf16[256,1024]{1,0:T(8,128)(2,1)}, bf16[256,1024]{1,0:T(8,128)(2,1)}, u32[]{:S(2)}, u32[]{:S(2)}) collective-permute-start(bf16[256,1024]{1,0:T(8,128)(2,1)} %get-tuple-element.51), channel_id=1, source_target_pairs={{1,0},{2,1},{3,2},{4,3},{5,4},{6,5},{7,6},{8,7},{9,8},{10,9},{11,1... | collective-permute-start | bytes 1572872 | tf_op jit(solution)/shard_map/ppermute | solution.py:355
  54.3 42.6 %all-to-all-start = ((bf16[64,8,2048]{2,1,0:T(8,128)(2,1)}), bf16[64,8,2048]{2,1,0:T(8,128)(2,1)S(1)}, u32[]{:S(2)}, u32[]{:S(2)}) async-start(bf16[64,8,2048]{2,1,0:T(8,128)(2,1)} %bitcast.5), calls=%async_computation | async-start | bytes 4194304 | tf_op jit(solution)/shard_map/all_to_all | solution.py:377
  83.3 2.7 %collective-permute-start.4 = (bf16[256,2048]{1,0:T(8,128)(2,1)S(1)}, bf16[256,2048]{1,0:T(8,128)(2,1)S(1)}, u32[]{:S(2)}, u32[]{:S(2)}) collective-permute-start(bf16[256,2048]{1,0:T(8,128)(2,1)S(1)} %get-tuple-element.61), channel_id=1, source_target_pairs={{0,32},{32,0},{1,33},{33,1},{2,34},{34,2},{3,35},{35,3},{4,36},{36... | collective-permute-start | bytes 3145736 | tf_op jit(solution)/shard_map/ppermute | solution.py:342
  83.4 4.1 %collective-permute-start.5 = (bf16[256,2048]{1,0:T(8,128)(2,1)S(1)}, bf16[256,2048]{1,0:T(8,128)(2,1)S(1)}, u32[]{:S(2)}, u32[]{:S(2)}) collective-permute-start(bf16[256,2048]{1,0:T(8,128)(2,1)S(1)} %get-tuple-element.62), channel_id=1, source_target_pairs={{0,32},{32,0},{1,33},{33,1},{2,34},{34,2},{3,35},{35,3},{4,36},{36... | collective-permute-start | bytes 3145736 | tf_op jit(solution)/shard_map/ppermute | solution.py:342
  97.2 7.9 %copy-start = (bf16[1024,1024]{1,0:T(8,128)(2,1)S(1)}, bf16[1024,1024]{1,0:T(8,128)(2,1)}, u32[]{:S(2)}) copy-start(bf16[1024,1024]{1,0:T(8,128)(2,1)} %wk_ref.5) | copy-start | bytes 6291460
  97.3 36.4 %all-to-all-start.1 = ((bf16[64,8,2048]{2,1,0:T(8,128)(2,1)}), bf16[64,8,2048]{2,1,0:T(8,128)(2,1)}, u32[]{:S(2)}, u32[]{:S(2)}) async-start(bf16[64,8,2048]{2,1,0:T(8,128)(2,1)} %bitcast.18), calls=%async_computation.1 | async-start | bytes 4194304 | tf_op jit(solution)/shard_map/all_to_all | solution.py:385
  105.2 4.1 %copy-start.2 = (bf16[1024,1024]{1,0:T(8,128)(2,1)S(1)}, bf16[1024,1024]{1,0:T(8,128)(2,1)}, u32[]{:S(2)}) copy-start(bf16[1024,1024]{1,0:T(8,128)(2,1)} %wq_ref.3) | copy-start | bytes 6291460
  105.2 4.1 %copy-start.6 = (bf16[1024,1024]{1,0:T(8,128)(2,1)S(1)}, bf16[1024,1024]{1,0:T(8,128)(2,1)}, u32[]{:S(2)}) copy-start(bf16[1024,1024]{1,0:T(8,128)(2,1)} %get-tuple-element.63) | copy-start | bytes 6291460
  109.3 2.4 %copy-start.1 = (bf16[1024,1024]{1,0:T(8,128)(2,1)S(1)}, bf16[1024,1024]{1,0:T(8,128)(2,1)}, u32[]{:S(2)}) copy-start(bf16[1024,1024]{1,0:T(8,128)(2,1)} %wv_ref.5) | copy-start | bytes 6291460
  109.3 2.4 %copy-start.7 = (bf16[1024,1024]{1,0:T(8,128)(2,1)S(1)}, bf16[1024,1024]{1,0:T(8,128)(2,1)}, u32[]{:S(2)}) copy-start(bf16[1024,1024]{1,0:T(8,128)(2,1)} %get-tuple-element.65) | copy-start | bytes 6291460
  115.5 20.1 %copy-start.5 = (f32[8,4096]{1,0:T(8,128)S(1)}, f32[8,4096]{1,0:T(8,128)}, u32[]{:S(2)}) copy-start(f32[8,4096]{1,0:T(8,128)} %param.13) | copy-start | bytes 393220

commit v10 on v9

--- a/solution.py
+++ b/solution.py
@@ -23,6 +23,7 @@
 
 SMALL = pl.CostEstimate(flops=10**8, bytes_accessed=10**5, transcendentals=0)
 VMEM = 60 * 2**20
+FULL = 127 * 2**19
 ROOM = 57 * 2**20
 PAIR = 2 * HD
 FOUR = 4 * HD
@@ -196,7 +197,7 @@
         out_specs=[row, head, head] + [out(h) for h in heights] + [out(rim)] * 4,
         out_shape=[like(width), like(rim), like(rim)] + [like(h) for h in heights] + [like(rim, F32)] * 4,
         scratch_shapes=[pltpu.VMEM((count, PAIR), BF16)] * 4,
-        compiler_params=pltpu.CompilerParams(vmem_limit_bytes=VMEM),
+        compiler_params=pltpu.CompilerParams(vmem_limit_bytes=FULL),
         cost_estimate=SMALL,
         name="front",
     )(tokens, out_grad, w_query, w_key, w_value, w_output, tokens)

time: 137 us -> 137 us (level)
  no operation moved by 1% of the time
where the time goes in v10:
time: 137 us
  Pallas kernels  55.9 us (41%)
  waiting for transfers between devices  32.1 us (23%)
  starting transfers between devices  28.7 us (21%)
  matrix products  10.2 us (7%)
  other arithmetic  7.36 us (5%)
  local copies, waits for them, and re-layouts  1.92 us (1%)
    pallas_call x1, Pallas kernels, front(): pl.pallas_call(front_kernel, grid=(width // PAIR,), in_specs=[whole, whol...  26.5 us
    all_to_all x1, waiting for transfers between devices, on_device(): pieces_kv = lax.all_to_all(both, CHIPS, 0, 0, tiled=True)  18.5 us
    pallas_call x1, Pallas kernels, last_block(): pl.pallas_call(last_kernel, grid_spec=pltpu.PrefetchScalarGridSpec(num_sc...  15.3 us
    pallas_call x1, Pallas kernels, first_block(): pl.pallas_call(first_kernel, grid_spec=pltpu.PrefetchScalarGridSpec(num_s...  14.1 us
    all_to_all x1, starting transfers between devices, on_device(): pieces_qo = lax.all_to_all(both, CHIPS, 0, 0, tiled=True)  12.9 us
    dot_general x3, matrix products, dot(): lax.dot_general(a, b, (((ca,), (cb,)), ((), ())), preferred_element_type=...  10.2 us
    all_to_all x1, starting transfers between devices, on_device(): pieces_kv = lax.all_to_all(both, CHIPS, 0, 0, tiled=True)  8.33 us
    all_to_all x1, waiting for transfers between devices, on_device(): pieces_qo = lax.all_to_all(both, CHIPS, 0, 0, tiled=True)  7.1 us
  transfers between devices with their start and end apart: 8, of which 5 were waited for; matrix products, arithmetic and copies ran while one was open for 11% of the time, Pallas kernels for 41%

profile of v10, /device:TPU:0, one launch (start us, length us, event | category | flops | bytes accessed | tf_op | source)
XLA Modules:
  0.0 137.0 jit_solution(15071955851882673618)
XLA Ops:
  0.6 1.9 %slice_bitcast_fusion = bf16[256,1024]{1,0:T(8,128)(2,1)} fusion(bf16[1,1024,1024]{2,1,0:T(8,128)(2,1)} %param.7), kind=kLoop, calls=%fused_computation.6 | loop fusion | bytes 1048576 | tf_op jit(solution)/shard_map/slice | solution.py:367
  2.5 4.3 %collective-permute-start = (bf16[256,1024]{1,0:T(8,128)(2,1)}, bf16[256,1024]{1,0:T(8,128)(2,1)}, u32[]{:S(2)}, u32[]{:S(2)}) collective-permute-start(bf16[256,1024]{1,0:T(8,128)(2,1)} %slice_bitcast_fusion), channel_id=1, source_target_pairs={{0,1},{1,2},{2,3},{3,4},{4,5},{5,6},{6,7},{7,8},{8,9},{9,10},{10,1... | collective-permute-start | bytes 1572872 | tf_op jit(solution)/shard_map/ppermute | solution.py:356
  6.8 26.5 %front.1 = (bf16[1024,1024]{1,0:T(8,128)(2,1)}, bf16[256,1024]{1,0:T(8,128)(2,1)}, bf16[256,1024]{1,0:T(8,128)(2,1)}, bf16[256,1024]{1,0:T(8,128)(2,1)}, bf16[25...) custom-call(bf16[1024,1024]{1,0:T(8,128)(2,1)} %bitcast.16, ...), custom_call_target="tpu_custom_call" | custom-call | flops 100000000 | bytes 100000 | tf_op jit(solution)/shard_map/front/pallas_call | solution.py:193
  33.3 1.3 collective-permute-start.1
  34.6 0.0 collective-permute-done.xl_ref
  34.6 0.0 copy-start.7
  34.6 14.1 %first_block.1 = (bf16[1024,1024]{1,0:T(8,128)(2,1)}, bf16[256,1024]{1,0:T(8,128)(2,1)}, bf16[256,1024]{1,0:T(8,128)(2,1)}, bf16[512,2048]{1,0:T(8,128)(2,1)S(1)}, bf16[512,2048]{1,0:T(8,128)(2,1)S(1)}) custom-call(s32[1]{0:T(128)} %bitcast.core_ref, f32[1]{0:T(128)} %bitcast.1.bias_ref, bf16[256,1024]{1,0:T(8,128)(2,1)} %get-tuple-element.35.q_ref, ...), custom_call_target="tpu_custom_call" | custom-call | flops 100000000 | bytes 100000 | tf_op jit(solution)/shard_map/first_block/pallas_call | solution.py:262
  48.7 0.0 collective-permute-done.1.xn_ref
  48.7 0.1 collective-permute-start.2
  48.8 1.3 collective-permute-start.3
  50.1 2.8 %collective-permute-done.2 = bf16[512,2048]{1,0:T(8,128)(2,1)S(1)} collective-permute-done((bf16[512,2048]{1,0:T(8,128)(2,1)S(1)}, bf16[512,2048]{1,0:T(8,128)(2,1)S(1)}, u32[]{:S(2)}, u32[]{:S(2)}) %collective-permute-start.2) | collective-permute-done | bytes 2097184 | tf_op jit(solution)/shard_map/ppermute | solution.py:343
  53.0 2.1 %add_convert_fusion.2 = bf16[512,2048]{1,0:T(8,128)(2,1)} fusion(bf16[512,2048]{1,0:T(8,128)(2,1)S(1)} %collective-permute-done.2, bf16[512,2048]{1,0:T(8,128)(2,1)S(1)} %get-tuple-element.48), kind=kLoop, calls=%fused_computation.4 | loop fusion | flops 4194304 | bytes 6291456 | tf_op jit(solution)/shard_map/convert_element_type | solution.py:35
  55.1 12.9 %all-to-all-start = ((bf16[64,8,2048]{2,1,0:T(8,128)(2,1)}), bf16[64,8,2048]{2,1,0:T(8,128)(2,1)S(1)}, u32[]{:S(2)}, u32[]{:S(2)}) async-start(bf16[64,8,2048]{2,1,0:T(8,128)(2,1)} %bitcast.5), calls=%async_computation | async-start | bytes 4194304 | tf_op jit(solution)/shard_map/all_to_all | solution.py:378
  68.0 0.0 collective-permute-done.3.gn_ref
  68.0 15.3 %last_block.1 = (bf16[1024,1024]{1,0:T(8,128)(2,1)}, bf16[1024,1024]{1,0:T(8,128)(2,1)}, bf16[256,2048]{1,0:T(8,128)(2,1)S(1)}, bf16[256,2048]{1,0:T(8,128)(2,1)S(1)}, bf16[512,2048]{1,0:T(8,128)(2,1)S(1)}) custom-call(s32[1]{0:T(128)} %bitcast.core_ref, bf16[256,1024]{1,0:T(8,128)(2,1)} %copy-done.3, bf16[256,1024]{1,0:T(8,128)(2,1)} %collective-permute-done.3.gn_ref, ...), custom_call_target="tpu_custom_call" | custom-call | flops 100000000 | bytes 100000 | tf_op jit(solution)/shard_map/last_block/pallas_call | solution.py:327
  83.3 0.1 collective-permute-start.4
  83.4 0.5 collective-permute-start.5
  83.9 2.1 %collective-permute-done.4 = bf16[256,2048]{1,0:T(8,128)(2,1)S(1)} collective-permute-done((bf16[256,2048]{1,0:T(8,128)(2,1)S(1)}, bf16[256,2048]{1,0:T(8,128)(2,1)S(1)}, u32[]{:S(2)}, u32[]{:S(2)}) %collective-permute-start.4) | collective-permute-done | bytes 1048608 | tf_op jit(solution)/shard_map/ppermute | solution.py:343
  86.1 1.5 %collective-permute-done.5 = bf16[256,2048]{1,0:T(8,128)(2,1)S(1)} collective-permute-done((bf16[256,2048]{1,0:T(8,128)(2,1)S(1)}, bf16[256,2048]{1,0:T(8,128)(2,1)S(1)}, u32[]{:S(2)}, u32[]{:S(2)}) %collective-permute-start.5) | collective-permute-done | bytes 1048608 | tf_op jit(solution)/shard_map/ppermute | solution.py:343
  87.6 2.3 %add_convert_fusion.1 = bf16[512,2048]{1,0:T(8,128)(2,1)} fusion(bf16[512,2048]{1,0:T(8,128)(2,1)S(1)} %get-tuple-element.60, bf16[256,2048]{1,0:T(8,128)(2,1)S(1)} %collective-permute-done.5, bf16[256,2048]{1,0:T(8,128)(2,1)S(1)} %collective-permute-done.4), kind=kLoop, calls=%fused_computation.3 | loop fusion | flops 7340032 | bytes 6291456 | tf_op jit(solution)/shard_map/convert_element_type | solution.py:35
  89.9 7.1 %all-to-all-done = bf16[64,8,2048]{2,1,0:T(8,128)(2,1)S(1)} async-done(((bf16[64,8,2048]{2,1,0:T(8,128)(2,1)}), bf16[64,8,2048]{2,1,0:T(8,128)(2,1)S(1)}, u32[]{:S(2)}, u32[]{:S(2)}) %all-to-all-start) | async-done | bytes 2097184 | tf_op jit(solution)/shard_map/all_to_all | solution.py:378
  97.0 0.3 convert_reduce_fusion.1
  97.3 8.3 %all-to-all-start.1 = ((bf16[64,8,2048]{2,1,0:T(8,128)(2,1)}), bf16[64,8,2048]{2,1,0:T(8,128)(2,1)}, u32[]{:S(2)}, u32[]{:S(2)}) async-start(bf16[64,8,2048]{2,1,0:T(8,128)(2,1)} %bitcast.18), calls=%async_computation.1 | async-start | bytes 4194304 | tf_op jit(solution)/shard_map/all_to_all | solution.py:386
  105.7 0.0 copy-start.2
  105.7 4.1 %fusion.4 = f32[1024,1024]{1,0:T(8,128)S(1)} fusion(bf16[1024,1024]{1,0:T(8,128)(2,1)} %get-tuple-element.64, bf16[1024,1024]{1,0:T(8,128)(2,1)S(1)} %copy-done), kind=kOutput, calls=%fused_computation.11 | convolution fusion | flops 2147483648 | bytes 8388608 | tf_op jit(solution)/shard_map/dot_general | solution.py:21
  109.8 0.0 copy-start.1
  109.8 0.0 copy-start.6
  109.8 2.4 %fusion.3 = f32[1024,1024]{1,0:T(8,128)S(1)} fusion(bf16[1024,1024]{1,0:T(8,128)(2,1)S(1)} %copy-done.5, bf16[1024,1024]{1,0:T(8,128)(2,1)S(1)} %copy-done.2), kind=kOutput, calls=%fused_computation.10 | convolution fusion | flops 2147483648 | bytes 8388608 | tf_op jit(solution)/shard_map/dot_general | solution.py:21
  112.3 3.7 %fusion = bf16[1,1024,1024]{2,1,0:T(8,128)(2,1)} fusion(f32[1024,1024]{1,0:T(8,128)S(1)} %fusion.3, f32[1024,1024]{1,0:T(8,128)S(1)} %fusion.4, bf16[1024,1024]{1,0:T(8,128)(2,1)S(1)} %copy-done.6, bf16[1024,1024]{1,0:T(8,128)(2,1)S(1)} %copy-done.1), kind=kOutput, calls=%fused_computation.5 | convolution fusion | flops 2150629376 | bytes 14680064 | tf_op jit(solution)/shard_map/dot_general | solution.py:21
  116.0 18.5 %all-to-all-done.1 = bf16[64,8,2048]{2,1,0:T(8,128)(2,1)} async-done(((bf16[64,8,2048]{2,1,0:T(8,128)(2,1)}), bf16[64,8,2048]{2,1,0:T(8,128)(2,1)}, u32[]{:S(2)}, u32[]{:S(2)}) %all-to-all-start.1) | async-done | bytes 2097184 | tf_op jit(solution)/shard_map/all_to_all | solution.py:386
  134.4 1.9 %convert_reduce_fusion = f32[8,2048]{1,0:T(8,128)S(1)} fusion(bf16[64,8,2048]{2,1,0:T(8,128)(2,1)} %all-to-all-done.1), kind=kLoop, calls=%fused_computation | loop fusion | flops 2080768 | bytes 2162688 | tf_op jit(solution)/shard_map/reduce_sum | solution.py:348
  136.3 0.7 fusion.1
  (13 shorter events, 0.0 us)
Async XLA Ops:
  2.5 32.1 %collective-permute-start = (bf16[256,1024]{1,0:T(8,128)(2,1)}, bf16[256,1024]{1,0:T(8,128)(2,1)}, u32[]{:S(2)}, u32[]{:S(2)}) collective-permute-start(bf16[256,1024]{1,0:T(8,128)(2,1)} %slice_bitcast_fusion), channel_id=1, source_target_pairs={{0,1},{1,2},{2,3},{3,4},{4,5},{5,6},{6,7},{7,8},{8,9},{9,10},{10,1... | collective-permute-start | bytes 1572872 | tf_op jit(solution)/shard_map/ppermute | solution.py:356
  33.3 15.5 %collective-permute-start.1 = (bf16[256,1024]{1,0:T(8,128)(2,1)}, bf16[256,1024]{1,0:T(8,128)(2,1)S(1)}, u32[]{:S(2)}, u32[]{:S(2)}) collective-permute-start(bf16[256,1024]{1,0:T(8,128)(2,1)} %get-tuple-element.46), channel_id=1, source_target_pairs={{1,0},{2,1},{3,2},{4,3},{5,4},{6,5},{7,6},{8,7},{9,8},{10,9},{11,1... | collective-permute-start | bytes 1572872 | tf_op jit(solution)/shard_map/ppermute | solution.py:356
  34.6 14.2 %copy-start.7 = (bf16[256,1024]{1,0:T(8,128)(2,1)S(1)}, bf16[256,1024]{1,0:T(8,128)(2,1)}, u32[]{:S(2)}) copy-start(bf16[256,1024]{1,0:T(8,128)(2,1)} %get-tuple-element.51) | copy-start | bytes 1572868
  48.7 6.4 %copy-start.3 = (bf16[256,1024]{1,0:T(8,128)(2,1)}, bf16[256,1024]{1,0:T(8,128)(2,1)S(1)}, u32[]{:S(2)}) copy-start(bf16[256,1024]{1,0:T(8,128)(2,1)S(1)} %collective-permute-done.1.xn_ref) | copy-start | bytes 1572868
  48.7 4.2 %collective-permute-start.2 = (bf16[512,2048]{1,0:T(8,128)(2,1)S(1)}, bf16[512,2048]{1,0:T(8,128)(2,1)S(1)}, u32[]{:S(2)}, u32[]{:S(2)}) collective-permute-start(bf16[512,2048]{1,0:T(8,128)(2,1)S(1)} %get-tuple-element.49), channel_id=1, source_target_pairs={{0,32},{32,0},{1,33},{33,1},{2,34},{34,2},{3,35},{35,3},{4,36},{36... | collective-permute-start | bytes 6291464 | tf_op jit(solution)/shard_map/ppermute | solution.py:343
  48.8 19.2 %collective-permute-start.3 = (bf16[256,1024]{1,0:T(8,128)(2,1)S(1)}, bf16[256,1024]{1,0:T(8,128)(2,1)}, u32[]{:S(2)}, u32[]{:S(2)}) collective-permute-start(bf16[256,1024]{1,0:T(8,128)(2,1)S(1)} %copy-done.7), channel_id=1, source_target_pairs={{1,0},{2,1},{3,2},{4,3},{5,4},{6,5},{7,6},{8,7},{9,8},{10,9},{11,1... | collective-permute-start | bytes 1572872 | tf_op jit(solution)/shard_map/ppermute | solution.py:356
  55.1 41.9 %all-to-all-start = ((bf16[64,8,2048]{2,1,0:T(8,128)(2,1)}), bf16[64,8,2048]{2,1,0:T(8,128)(2,1)S(1)}, u32[]{:S(2)}, u32[]{:S(2)}) async-start(bf16[64,8,2048]{2,1,0:T(8,128)(2,1)} %bitcast.5), calls=%async_computation | async-start | bytes 4194304 | tf_op jit(solution)/shard_map/all_to_all | solution.py:378
  83.3 2.7 %collective-permute-start.4 = (bf16[256,2048]{1,0:T(8,128)(2,1)S(1)}, bf16[256,2048]{1,0:T(8,128)(2,1)S(1)}, u32[]{:S(2)}, u32[]{:S(2)}) collective-permute-start(bf16[256,2048]{1,0:T(8,128)(2,1)S(1)} %get-tuple-element.61), channel_id=1, source_target_pairs={{0,32},{32,0},{1,33},{33,1},{2,34},{34,2},{3,35},{35,3},{4,36},{36... | collective-permute-start | bytes 3145736 | tf_op jit(solution)/shard_map/ppermute | solution.py:343
  83.4 4.1 %collective-permute-start.5 = (bf16[256,2048]{1,0:T(8,128)(2,1)S(1)}, bf16[256,2048]{1,0:T(8,128)(2,1)S(1)}, u32[]{:S(2)}, u32[]{:S(2)}) collective-permute-start(bf16[256,2048]{1,0:T(8,128)(2,1)S(1)} %get-tuple-element.62), channel_id=1, source_target_pairs={{0,32},{32,0},{1,33},{33,1},{2,34},{34,2},{3,35},{35,3},{4,36},{36... | collective-permute-start | bytes 3145736 | tf_op jit(solution)/shard_map/ppermute | solution.py:343
  97.3 8.3 %copy-start = (bf16[1024,1024]{1,0:T(8,128)(2,1)S(1)}, bf16[1024,1024]{1,0:T(8,128)(2,1)}, u32[]{:S(2)}) copy-start(bf16[1024,1024]{1,0:T(8,128)(2,1)} %wk_ref.5) | copy-start | bytes 6291460
  97.3 37.1 %all-to-all-start.1 = ((bf16[64,8,2048]{2,1,0:T(8,128)(2,1)}), bf16[64,8,2048]{2,1,0:T(8,128)(2,1)}, u32[]{:S(2)}, u32[]{:S(2)}) async-start(bf16[64,8,2048]{2,1,0:T(8,128)(2,1)} %bitcast.18), calls=%async_computation.1 | async-start | bytes 4194304 | tf_op jit(solution)/shard_map/all_to_all | solution.py:386
  105.7 4.2 %copy-start.2 = (bf16[1024,1024]{1,0:T(8,128)(2,1)S(1)}, bf16[1024,1024]{1,0:T(8,128)(2,1)}, u32[]{:S(2)}) copy-start(bf16[1024,1024]{1,0:T(8,128)(2,1)} %wq_ref.3) | copy-start | bytes 6291460
  105.7 4.2 %copy-start.5 = (bf16[1024,1024]{1,0:T(8,128)(2,1)S(1)}, bf16[1024,1024]{1,0:T(8,128)(2,1)}, u32[]{:S(2)}) copy-start(bf16[1024,1024]{1,0:T(8,128)(2,1)} %get-tuple-element.63) | copy-start | bytes 6291460
  109.8 2.4 %copy-start.1 = (bf16[1024,1024]{1,0:T(8,128)(2,1)S(1)}, bf16[1024,1024]{1,0:T(8,128)(2,1)}, u32[]{:S(2)}) copy-start(bf16[1024,1024]{1,0:T(8,128)(2,1)} %wv_ref.5) | copy-start | bytes 6291460
  109.8 2.4 %copy-start.6 = (bf16[1024,1024]{1,0:T(8,128)(2,1)S(1)}, bf16[1024,1024]{1,0:T(8,128)(2,1)}, u32[]{:S(2)}) copy-start(bf16[1024,1024]{1,0:T(8,128)(2,1)} %get-tuple-element.65) | copy-start | bytes 6291460
  116.0 20.4 %copy-start.4 = (f32[8,4096]{1,0:T(8,128)S(1)}, f32[8,4096]{1,0:T(8,128)}, u32[]{:S(2)}) copy-start(f32[8,4096]{1,0:T(8,128)} %param.13) | copy-start | bytes 393220
